TPU v7x, 32 devices: a whole 2x2x4 slice. The times are simulated.
32 devices in a mesh: dp: 16 (over z, x, core), shard: 2 (over y).
Axes of the slice: x: 2, y: 2, z: 4, core: 2. Of those that a mesh axis runs over, the one named last changes fastest.
Arguments:
- inputs: bfloat16 [32, 8, 8, 8, 256], P(('dp', 'shard')), may hold values from -6 to 6
- cotangent: bfloat16 [32, 4, 4, 4, 256], P(('dp', 'shard')), may hold values from -6 to 6
- weights: bfloat16 [28, 256, 256], P(None, 'shard'), may hold values from -0.078125 to 0.078125
Outputs:
- outputs: bfloat16 [32, 4, 4, 4, 256], P(('dp', 'shard'))
- input_grad: bfloat16 [32, 8, 8, 8, 256], P(('dp', 'shard'))
- weight_grad: float32 [28, 256, 256], P(None, 'shard')
All inputs are finite; a program needn't handle non-finite values.
Results may differ from a plain program's by a relative error of at most 0.012.
Values may be sent and summed in bfloat16 or wider, within the bound.
No kernel may reach another device: no remote copies, remote signals or barrier semaphores. Data moves between devices by JAX's collectives and lax.ppermute only.
A program may use at most 64 MiB of HBM per device.

v0:
```python
import functools

import jax
import jax.numpy as jnp
from jax import lax
from jax.experimental import pallas as pl
from jax.experimental.pallas import tpu as pltpu
from jax.sharding import PartitionSpec as P

LANES = 128
PARTS = 8
VMEM_BYTES = 48 * 1024 * 1024
BF16 = jnp.bfloat16
F32 = jnp.float32

TAP_CLASS = (1, 0, 1)
TAP_SHIFT = (1, 0, 0)


def tap_table():
    table = []
    for first in range(3):
        for second in range(3):
            for third in range(3):
                taps = (first, second, third)
                table.append(
                    (tuple(TAP_CLASS[t] for t in taps), tuple(TAP_SHIFT[t] for t in taps))
                )
    return table


def class_index(parity):
    return 4 * parity[0] + 2 * parity[1] + parity[2]


def dot(left, right, contract=(1, 0)):
    return lax.dot_general(
        left, right, (((contract[0],), (contract[1],)), ((), ())), preferred_element_type=F32
    )


def row_digits(rows, half):
    row = lax.broadcasted_iota(jnp.int32, (rows, 1), 0)
    return (row // (half * half)) % half, (row // half) % half, row % half


def shift_rows(value, shift, half, forward):
    if not any(shift):
        return value
    rows = value.shape[0]
    offset = (shift[0] * half + shift[1]) * half + shift[2]
    keep = None
    for digit, step in zip(row_digits(rows, half), shift):
        if step:
            inside = digit >= step if forward else digit < half - step
            keep = inside if keep is None else keep & inside
    moved = pltpu.roll(value, offset if forward else rows - offset, 0)
    return jnp.where(keep, moved, 0.0)


def plane_order(edge, blocks):
    half = edge // 2
    plane = edge * edge
    size = blocks * plane
    row = lax.broadcasted_iota(jnp.int32, (size, size), 0)
    col = lax.broadcasted_iota(jnp.int32, (size, size), 1)
    inner = row % plane
    parity, cell = inner // (half * half), inner % (half * half)
    second = 2 * (cell // half) + parity // 2
    third = 2 * (cell % half) + parity % 2
    return (col == (row // plane) * plane + second * edge + third).astype(BF16)


def pack_kernel(edge, shards_of, parts, x_ref, cot_ref, pieces_ref, send_ref, own_ref):
    half = edge // 2
    hh, cells, plane = half * half, half**3, edge * edge
    groups = parts // 2
    width = LANES // groups
    here = lax.axis_index("shard")
    blocks = 256 // plane
    order = plane_order(edge, blocks)
    planes = []
    for start in range(0, edge, blocks):
        part = x_ref[start * plane : (start + blocks) * plane, :]
        moved = dot(order, part).astype(BF16)
        planes += [moved[b * plane : (b + 1) * plane] for b in range(blocks)]
    classes = []
    for first in range(2):
        for inner in range(4):
            classes.append(
                jnp.concatenate(
                    [planes[2 * i + first][inner * hh : (inner + 1) * hh] for i in range(half)], axis=0
                )
            )
    size = 4 * LANES
    row = lax.broadcasted_iota(jnp.int32, (size, size), 0)
    col = lax.broadcasted_iota(jnp.int32, (size, size), 1)
    source = ((col // width) % 4) * LANES + (col // LANES) * width + col % width
    lane_order = (row == source).astype(BF16)
    for owner in range(shards_of):
        lanes = slice(owner * LANES, (owner + 1) * LANES)
        wide = jnp.concatenate(
            [
                jnp.concatenate([classes[4 * first + inner][:, lanes] for inner in range(4)], axis=1)
                for first in range(2)
            ],
            axis=0,
        )
        packed = dot(wide, lane_order).astype(BF16)
        for part in range(parts):
            group, side = part // 2, part % 2
            piece = part * shards_of + owner
            pieces_ref[piece, 0 : 2 * cells, :] = packed[:, group * LANES : (group + 1) * LANES]
            pieces_ref[piece, 2 * cells : 3 * cells, :] = cot_ref[:, side * LANES : (side + 1) * LANES]
    for index, value in enumerate(classes):
        low, high = value[:, :LANES], value[:, LANES:]
        own_ref[index * cells : (index + 1) * cells, :] = jnp.where(here == 0, low, high)
        send_ref[index * cells : (index + 1) * cells, :] = jnp.where(here == 0, high, low)
    for side in range(2):
        rows = slice((8 + side) * cells, (9 + side) * cells)
        own_ref[rows, :] = cot_ref[:, side * LANES : (side + 1) * LANES]
        send_ref[rows, :] = cot_ref[:, side * LANES : (side + 1) * LANES]


def weight_kernel(half, samples, width, splits, got_ref, *out_refs):
    cells = half**3
    rows = samples * cells
    acts, raw = [], None
    for first in range(2):
        value = got_ref[:, first * cells : (first + 1) * cells, :].reshape(rows, LANES)
        if first == 0:
            raw = value
        wide = value.astype(F32)
        acts.append((wide / (1.0 + jnp.exp(-wide))).astype(BF16))
    cots = got_ref[:, 2 * cells : 3 * cells, :].reshape(rows, LANES).astype(F32)
    moved = {}
    for si in range(2):
        for sj in range(2):
            for sk in range(2):
                moved[si, sj, sk] = shift_rows(cots, (si, sj, sk), half, False).astype(BF16)
    sums = {}
    for si in range(2):
        right = jnp.concatenate([moved[si, sj, sk] for sj in range(2) for sk in range(2)], axis=1)
        for first in range(si, 2):
            sums[first, si] = dot(acts[first], right, (0, 0))
    taps = []
    for parity, shift in tap_table():
        block = sums[parity[0], shift[0]]
        row = (2 * parity[1] + parity[2]) * width
        col = (2 * shift[1] + shift[2]) * LANES
        taps.append(block[row : row + width, col : col + LANES])
    taps.append(dot(raw, moved[0, 0, 0], (0, 0))[:width])
    start = 0
    for ref, count in zip(out_refs, splits):
        for index in range(count):
            ref[index] = taps[start + index].astype(BF16)
        start += count


def sample_kernel(half, own_ref, other_ref, w_ref, part_ref, grad_ref, send_ref):
    cells = half**3
    both = 2 * cells
    count = len(tap_table())

    def rows_of(index):
        rows = slice(index * cells, (index + 1) * cells)
        return jnp.concatenate([own_ref[rows, :], other_ref[rows, :]], axis=0)

    cots = jnp.concatenate([rows_of(8), rows_of(9)], axis=1).astype(F32)
    moved, gathered = {}, {}
    shifts = [(si, sj, sk) for si in range(2) for sj in range(2) for sk in range(2)]
    for shift in shifts:
        moved[shift] = shift_rows(cots, shift, half, False).astype(BF16)
    for index in range(8):
        value = rows_of(index)
        wide = value.astype(F32)
        sigma = 1.0 / (1.0 + jnp.exp(-wide))
        act = (wide * sigma).astype(BF16)
        back = None
        for tap, (parity, shift) in enumerate(tap_table()):
            if class_index(parity) != index:
                continue
            weight = w_ref[tap]
            term = dot(act, weight)
            gathered[shift] = term if shift not in gathered else gathered[shift] + term
            term = dot(moved[shift], weight, (1, 1))
            back = term if back is None else back + term
        grad = back * sigma * (1.0 + wide * (1.0 - sigma))
        if index == 0:
            weight = w_ref[count]
            gathered[0, 0, 0] = gathered[0, 0, 0] + dot(value, weight)
            grad = grad + dot(moved[0, 0, 0], weight, (1, 1))
        grad = grad.astype(BF16)
        rows = slice(index * cells, (index + 1) * cells)
        grad_ref[rows, :] = grad[:cells]
        send_ref[rows, :] = grad[cells:]
    total = gathered[0, 0, 0]
    for shift in shifts[1:]:
        total = total + shift_rows(gathered[shift], shift, half, True)
    part_ref[...] = total[:cells]
    for side in range(2):
        send_ref[(8 + side) * cells : (9 + side) * cells, :] = total[
            cells:both, side * LANES : (side + 1) * LANES
        ].astype(BF16)


def finish_kernel(edge, part_ref, grad_ref, got_ref, out_ref, back_ref):
    half = edge // 2
    hh, cells, plane = half * half, half**3, edge * edge
    here = lax.axis_index("shard")
    got = jnp.concatenate(
        [got_ref[8 * cells : 9 * cells, :], got_ref[9 * cells : 10 * cells, :]], axis=1
    )
    out_ref[...] = (part_ref[...] + got.astype(F32)).astype(BF16)
    mine, theirs = grad_ref[...], got_ref[0 : 8 * cells, :]
    wide = jnp.concatenate(
        [jnp.where(here == 0, mine, theirs), jnp.where(here == 0, theirs, mine)], axis=1
    )
    blocks = 256 // plane
    order = plane_order(edge, blocks)
    for start in range(0, edge, blocks):
        pieces = []
        for b in range(blocks):
            first, i = (start + b) % 2, (start + b) // 2
            for inner in range(4):
                row = (4 * first + inner) * cells + i * hh
                pieces.append(wide[row : row + hh])
        back_ref[start * plane : (start + blocks) * plane, :] = dot(
            order, jnp.concatenate(pieces, axis=0), (0, 0)
        ).astype(BF16)


def place_kernel(parts, width, block, has_base, *refs):
    piece_refs, out_ref = refs[has_base : has_base + parts], refs[-1]
    part = lax.rem(lax.axis_index("dp"), parts)
    step = pl.program_id(0)
    for distance, ref in enumerate(piece_refs):
        owner = part ^ distance
        group, side = owner // 2, lax.rem(owner, 2)
        rows = pl.ds(pl.multiple_of(group * width, width), width)
        cols = pl.ds(pl.multiple_of(side * LANES, LANES), LANES)
        out_ref[:, rows, cols] = ref[pl.ds(step * block, block)].astype(F32)


def vmem_call(body, outs, flops=0, **kwargs):
    space = pl.BlockSpec(memory_space=pltpu.VMEM)
    return pl.pallas_call(
        body,
        out_shape=outs,
        out_specs=jax.tree.map(lambda _: space, outs),
        compiler_params=pltpu.CompilerParams(vmem_limit_bytes=VMEM_BYTES),
        cost_estimate=pl.CostEstimate(flops=flops, bytes_accessed=1 << 20, transcendentals=0),
        **kwargs,
    )


def shape(dims, dtype=BF16):
    return jax.ShapeDtypeStruct(dims, dtype)


def shards(groups_of, shards_of, inputs, cotangent, weights):
    edge, chans = inputs.shape[1], inputs.shape[4]
    half = edge // 2
    cells = half**3
    count, own_chans = weights.shape[0], weights.shape[1]
    parts = PARTS
    samples = parts * shards_of
    width = LANES // (parts // 2)
    values = inputs.reshape(edge**3, chans)
    rows = cotangent.reshape(cells, chans)

    pieces, send, own = vmem_call(
        functools.partial(pack_kernel, edge, shards_of, parts),
        (shape((samples, 3 * cells, LANES)), shape((10 * cells, LANES)), shape((10 * cells, LANES))),
    )(values, rows)
    got = lax.all_to_all(
        pieces,
        ("dp", "shard"),
        split_axis=0,
        concat_axis=0,
        tiled=True,
        axis_index_groups=[
            [start + i for i in range(samples)] for start in range(0, groups_of * shards_of, samples)
        ],
    )
    other = lax.ppermute(send, "shard", [(0, 1), (1, 0)])

    def across(value, distance):
        return lax.ppermute(value, "dp", [(i, i ^ distance) for i in range(groups_of)])

    splits = (count // 2, count - count // 2)
    sums = vmem_call(
        functools.partial(weight_kernel, half, samples, width, splits),
        tuple(shape((n, width, LANES)) for n in splits),
    )(got)
    if not isinstance(sums, (tuple, list)):
        sums = (sums,)

    part, grad, back = vmem_call(
        functools.partial(sample_kernel, half),
        (shape((cells, chans), F32), shape((8 * cells, LANES)), shape((10 * cells, LANES))),
    )(own, other, weights)
    returned = lax.ppermute(back, "shard", [(0, 1), (1, 0)])
    outputs, input_grad = vmem_call(
        functools.partial(finish_kernel, edge),
        (shape((cells, chans)), shape((edge**3, chans))),
    )(part, grad, returned)

    block = count // 4
    base = None
    start = 0
    for total, n in zip(sums, splits):
        distance = parts
        while distance < groups_of:
            total = (total.astype(F32) + across(total, distance).astype(F32)).astype(BF16)
            distance *= 2
        held = {0: total}
        for distance in range(2, parts, 2):
            held[distance] = across(total, distance)
        for distance in range(0, parts, 2):
            held[distance + 1] = across(held[distance], 1)
        args = [held[i] for i in range(parts)]
        whole = pl.BlockSpec(memory_space=pltpu.VMEM)
        first = start // block
        base = pl.pallas_call(
            functools.partial(place_kernel, parts, width, block, int(base is not None)),
            grid=(n // block,),
            in_specs=([pl.BlockSpec(memory_space=pl.ANY)] if base is not None else []) + [whole] * parts,
            out_specs=pl.BlockSpec(
                (block, own_chans, chans), functools.partial(lambda first, i: (first + i, 0, 0), first)
            ),
            out_shape=shape((count, own_chans, chans), F32),
            input_output_aliases={0: 0} if base is not None else {},
            compiler_params=pltpu.CompilerParams(vmem_limit_bytes=VMEM_BYTES),
        )(*([base] if base is not None else []), *args)
        start += n
    return outputs.reshape(cotangent.shape), input_grad.reshape(inputs.shape), base


def build_cols(values):
    edge = values.shape[0]
    half = edge // 2
    width = values.shape[3]
    act = jax.nn.silu(values.astype(jnp.float32)).astype(jnp.bfloat16)
    padded = jnp.pad(act, ((1, 1), (1, 1), (1, 1), (0, 0)))
    pieces = []
    for first in range(3):
        for second in range(3):
            for third in range(3):
                pieces.append(
                    padded[
                        first : first + edge : 2,
                        second : second + edge : 2,
                        third : third + edge : 2,
                    ]
                )
    pieces.append(values[0::2, 0::2, 0::2])
    return jnp.stack(pieces, axis=3).reshape(half * half * half, 28, width)


def spread_back(values, grad_rows, piece, half):
    width = piece.shape[1]
    edge = 2 * half
    grid = jnp.zeros((edge + 2, edge + 2, edge + 2, width), jnp.float32)
    for first in range(3):
        block = jnp.einsum(
            "qo,tco->qtc",
            grad_rows,
            piece[9 * first : 9 * first + 9],
            preferred_element_type=jnp.float32,
        )
        block = block.reshape(half, half, half, 9, width)
        for second in range(3):
            for third in range(3):
                grid = grid.at[
                    first : first + edge : 2, second : second + edge : 2, third : third + edge : 2
                ].add(block[:, :, :, 3 * second + third])
    direct = jnp.einsum(
        "qo,co->qc", grad_rows, piece[27], preferred_element_type=jnp.float32
    ).reshape(half, half, half, width)
    own = values.astype(jnp.float32)
    sigma = jax.nn.sigmoid(own)
    grad_in = grid[1:-1, 1:-1, 1:-1] * sigma * (1.0 + own * (1.0 - sigma))
    grad_in = grad_in.at[0::2, 0::2, 0::2].add(direct)
    return grad_in.astype(jnp.bfloat16)


def general(inputs, cotangent, weights):
    values = inputs[0]
    edge = values.shape[0]
    half = edge // 2
    chans = values.shape[3]
    cols = build_cols(values)
    grad_rows = cotangent[0].reshape(half * half * half, chans)
    result = jnp.einsum(
        "qtc,tco->qo",
        cols,
        lax.all_gather(weights, "shard", axis=1, tiled=True),
        preferred_element_type=jnp.float32,
    )
    grad_in = spread_back(
        values, grad_rows, lax.all_gather(weights, "shard", axis=1, tiled=True), half
    )
    group_values = lax.all_to_all(inputs, "shard", split_axis=4, concat_axis=0, tiled=True)
    group_grads = lax.all_gather(cotangent, "shard", axis=0, tiled=True)
    count = group_values.shape[0]
    group_cols = jax.vmap(build_cols)(group_values)
    group_rows = group_grads.reshape(count, half * half * half, chans)
    per_sample = jnp.einsum(
        "sqtc,sqo->stco", group_cols, group_rows, preferred_element_type=jnp.float32
    )
    owned = jnp.sum(per_sample.astype(jnp.bfloat16).astype(jnp.float32), axis=0)
    weight_grad = lax.psum(owned, "dp")
    outputs = result.astype(jnp.bfloat16).reshape(1, half, half, half, chans)
    return (outputs, grad_in.reshape(1, edge, edge, edge, chans), weight_grad)


def fits(mesh, inputs, cotangent, weights):
    groups_of, shards_of = mesh.shape["dp"], mesh.shape["shard"]
    edge, chans = inputs.shape[1], inputs.shape[4]
    ratio = groups_of // PARTS
    return (
        shards_of == 2
        and chans == shards_of * LANES
        and inputs.shape[0] == groups_of * shards_of
        and inputs.shape[1:4] == (8, 8, 8)
        and groups_of % PARTS == 0
        and ratio & (ratio - 1) == 0
    )


def solution(mesh):
    rows = P(("dp", "shard"), None, None, None, None)
    kernel = P(None, "shard", None)

    def whole(inputs, cotangent, weights):
        body = general
        if fits(mesh, inputs, cotangent, weights):
            body = functools.partial(shards, mesh.shape["dp"], mesh.shape["shard"])
        return jax.shard_map(
            body,
            mesh=mesh,
            in_specs=(rows, rows, kernel),
            out_specs=(rows, rows, kernel),
            check_vma=False,
        )(inputs, cotangent, weights)

    return whole
```

profile of v0, /device:TPU:0, one launch (start us, length us, event | category | flops | bytes accessed | tf_op | source)
XLA Modules:
  0.0 54.8 jit_solution(17591131842062873301)
XLA Ops:
  0.6 0.0 copy-start
  0.6 0.9 %reshape.19.cot_ref = bf16[64,256]{1,0:T(8,128)(2,1)S(1)} reshape(bf16[1,4,4,4,256]{4,3,2,1,0:T(4,128)(2,1)} %param.4) | data formatting | bytes 65536 | tf_op jit(solution)/shard_map/reshape | solution.py:270
  1.5 0.0 copy-start.1
  1.6 0.9 %copy-done.1 = bf16[1,8,8,8,256]{4,3,2,1,0:T(8,128)(2,1)S(1)} copy-done((bf16[1,8,8,8,256]{4,3,2,1,0:T(8,128)(2,1)S(1)}, bf16[1,8,8,8,256]{4,3,2,1,0:T(8,128)(2,1)}, u32[]{:S(2)}) %copy-start.1) | copy-done | bytes 262168
  2.5 1.5 %shard_map.58 = (bf16[16,192,128]{2,1,0:T(8,128)(2,1)}, bf16[640,128]{1,0:T(8,128)(2,1)S(1)}, bf16[640,128]{1,0:T(8,128)(2,1)S(1)}) custom-call(bf16[512,256]{1,0:T(8,128)(2,1)S(1)} %bitcast.2, bf16[64,256]{1,0:T(8,128)(2,1)S(1)} %reshape.19.cot_ref), custom_call_target="tpu_custom_call" | custom-call | bytes 1048576 | tf_op jit(solution)/shard_map/pallas_call | solution.py:272
  4.0 6.3 %all-to-all-start = ((bf16[16,192,128]{2,1,0:T(8,128)(2,1)}), bf16[16,192,128]{2,1,0:T(8,128)(2,1)S(1)}, u32[]{:S(2)}, u32[]{:S(2)}) async-start(bf16[16,192,128]{2,1,0:T(8,128)(2,1)} %get-tuple-element.20), calls=%async_computation | async-start | bytes 1572864 | tf_op jit(solution)/shard_map/all_to_all | solution.py:276
  10.3 1.9 %collective-permute-start = (bf16[640,128]{1,0:T(8,128)(2,1)S(1)}, bf16[640,128]{1,0:T(8,128)(2,1)S(1)}, u32[]{:S(2)}, u32[]{:S(2)}) collective-permute-start(bf16[640,128]{1,0:T(8,128)(2,1)S(1)} %get-tuple-element.14), channel_id=1, source_target_pairs={{0,1},{1,0},{2,3},{3,2},{4,5},{5,4},{6,7},{7,6},{8,9},{9,8},{10,11... | collective-permute-start | bytes 491528 | tf_op jit(solution)/shard_map/ppermute | solution.py:286
  12.2 11.3 %all-to-all-done.got_ref = bf16[16,192,128]{2,1,0:T(8,128)(2,1)S(1)} async-done(((bf16[16,192,128]{2,1,0:T(8,128)(2,1)}), bf16[16,192,128]{2,1,0:T(8,128)(2,1)S(1)}, u32[]{:S(2)}, u32[]{:S(2)}) %all-to-all-start) | async-done | bytes 786464 | tf_op jit(solution)/shard_map/all_to_all | solution.py:276
  23.5 1.2 %shard_map.61 = (bf16[14,32,128]{2,1,0:T(8,128)(2,1)S(1)}, bf16[14,32,128]{2,1,0:T(8,128)(2,1)S(1)}) custom-call(bf16[16,192,128]{2,1,0:T(8,128)(2,1)S(1)} %all-to-all-done.got_ref), custom_call_target="tpu_custom_call" | custom-call | bytes 1048576 | tf_op jit(solution)/shard_map/pallas_call | solution.py:292
  24.7 2.6 %collective-permute-start.2 = (bf16[14,32,128]{2,1,0:T(8,128)(2,1)S(1)}, bf16[14,32,128]{2,1,0:T(8,128)(2,1)S(1)}, u32[]{:S(2)}, u32[]{:S(2)}) collective-permute-start(bf16[14,32,128]{2,1,0:T(8,128)(2,1)S(1)} %get-tuple-element.21), channel_id=1, source_target_pairs={{0,16},{2,18},{4,20},{6,22},{8,24},{10,26},{12,28},{14,30},{16,0},... | collective-permute-start | bytes 344072 | tf_op jit(solution)/shard_map/ppermute | solution.py:289
  27.4 0.0 collective-permute-done.other_ref
  27.4 0.0 copy-done
  27.4 1.1 %shard_map.59 = (f32[64,256]{1,0:T(8,128)S(1)}, bf16[512,128]{1,0:T(8,128)(2,1)S(1)}, bf16[640,128]{1,0:T(8,128)(2,1)S(1)}) custom-call(bf16[640,128]{1,0:T(8,128)(2,1)S(1)} %get-tuple-element.13.own_ref, bf16[640,128]{1,0:T(8,128)(2,1)S(1)} %collective-permute-done.other_ref, bf16[28,128,256]{2,1,0:T(8,128)(2,1)S(1)} %copy-done), custom_call_target="tpu_custom_call" | custom-call | bytes 1048576 | tf_op jit(solution)/shard_map/pallas_call | solution.py:299
  28.5 0.6 %collective-permute-start.1 = (bf16[640,128]{1,0:T(8,128)(2,1)S(1)}, bf16[640,128]{1,0:T(8,128)(2,1)S(1)}, u32[]{:S(2)}, u32[]{:S(2)}) collective-permute-start(bf16[640,128]{1,0:T(8,128)(2,1)S(1)} %get-tuple-element.17), channel_id=1, source_target_pairs={{0,1},{1,0},{2,3},{3,2},{4,5},{5,4},{6,7},{7,6},{8,9},{9,8},{10,11... | collective-permute-start | bytes 491528 | tf_op jit(solution)/shard_map/ppermute | solution.py:303
  29.2 0.4 collective-permute-start.10
  29.5 6.9 %collective-permute-done.2 = bf16[14,32,128]{2,1,0:T(8,128)(2,1)S(1)} collective-permute-done((bf16[14,32,128]{2,1,0:T(8,128)(2,1)S(1)}, bf16[14,32,128]{2,1,0:T(8,128)(2,1)S(1)}, u32[]{:S(2)}, u32[]{:S(2)}) %collective-permute-start.2) | collective-permute-done | bytes 114720 | tf_op jit(solution)/shard_map/ppermute | solution.py:289
  36.5 1.0 %collective-permute-start.8 = (bf16[14,32,128]{2,1,0:T(8,128)(2,1)S(1)}, bf16[14,32,128]{2,1,0:T(8,128)(2,1)S(1)}, u32[]{:S(2)}, u32[]{:S(2)}) collective-permute-start(bf16[14,32,128]{2,1,0:T(8,128)(2,1)S(1)} %add_convert_fusion.1.refs_0_), channel_id=1, source_target_pairs={{0,12},{2,14},{4,8},{6,10},{8,4},{10,6},{12,0},{14,2},{16,28},{18,... | collective-permute-start | bytes 344072 | tf_op jit(solution)/shard_map/ppermute | solution.py:289
  37.5 1.9 %collective-permute-start.6 = (bf16[14,32,128]{2,1,0:T(8,128)(2,1)S(1)}, bf16[14,32,128]{2,1,0:T(8,128)(2,1)S(1)}, u32[]{:S(2)}, u32[]{:S(2)}) collective-permute-start(bf16[14,32,128]{2,1,0:T(8,128)(2,1)S(1)} %add_convert_fusion.1.refs_0_), channel_id=1, source_target_pairs={{0,8},{2,10},{4,12},{6,14},{8,0},{10,2},{12,4},{14,6},{16,24},{18,... | collective-permute-start | bytes 344072 | tf_op jit(solution)/shard_map/ppermute | solution.py:289
  39.4 0.6 %collective-permute-start.4 = (bf16[14,32,128]{2,1,0:T(8,128)(2,1)S(1)}, bf16[14,32,128]{2,1,0:T(8,128)(2,1)S(1)}, u32[]{:S(2)}, u32[]{:S(2)}) collective-permute-start(bf16[14,32,128]{2,1,0:T(8,128)(2,1)S(1)} %add_convert_fusion.1.refs_0_), channel_id=1, source_target_pairs={{0,4},{2,6},{4,0},{6,2},{8,12},{10,14},{12,8},{14,10},{16,20},{18,... | collective-permute-start | bytes 344072 | tf_op jit(solution)/shard_map/ppermute | solution.py:289
  40.0 0.0 collective-permute-done.10
  40.0 0.0 collective-permute-start.3
  40.1 0.0 collective-permute-done.1.got_ref
  40.1 1.0 %collective-permute-start.16 = (bf16[14,32,128]{2,1,0:T(8,128)(2,1)S(1)}, bf16[14,32,128]{2,1,0:T(8,128)(2,1)S(1)}, u32[]{:S(2)}, u32[]{:S(2)}) collective-permute-start(bf16[14,32,128]{2,1,0:T(8,128)(2,1)S(1)} %add_convert_fusion.refs_1_), channel_id=1, source_target_pairs={{0,12},{2,14},{4,8},{6,10},{8,4},{10,6},{12,0},{14,2},{16,28},{18,... | collective-permute-start | bytes 344072 | tf_op jit(solution)/shard_map/ppermute | solution.py:289
  41.1 2.2 %collective-permute-done.8.refs_6_ = bf16[14,32,128]{2,1,0:T(8,128)(2,1)S(1)} collective-permute-done((bf16[14,32,128]{2,1,0:T(8,128)(2,1)S(1)}, bf16[14,32,128]{2,1,0:T(8,128)(2,1)S(1)}, u32[]{:S(2)}, u32[]{:S(2)}) %collective-permute-start.8) | collective-permute-done | bytes 114720 | tf_op jit(solution)/shard_map/ppermute | solution.py:289
  43.2 0.0 collective-permute-start.14
  43.3 1.3 %collective-permute-done.6.refs_4_ = bf16[14,32,128]{2,1,0:T(8,128)(2,1)S(1)} collective-permute-done((bf16[14,32,128]{2,1,0:T(8,128)(2,1)S(1)}, bf16[14,32,128]{2,1,0:T(8,128)(2,1)S(1)}, u32[]{:S(2)}, u32[]{:S(2)}) %collective-permute-start.6) | collective-permute-done | bytes 114720 | tf_op jit(solution)/shard_map/ppermute | solution.py:289
  44.6 0.5 collective-permute-start.12
  45.1 2.1 %collective-permute-done.4.refs_2_ = bf16[14,32,128]{2,1,0:T(8,128)(2,1)S(1)} collective-permute-done((bf16[14,32,128]{2,1,0:T(8,128)(2,1)S(1)}, bf16[14,32,128]{2,1,0:T(8,128)(2,1)S(1)}, u32[]{:S(2)}, u32[]{:S(2)}) %collective-permute-start.4) | collective-permute-done | bytes 114720 | tf_op jit(solution)/shard_map/ppermute | solution.py:289
  47.1 0.0 collective-permute-start.9
  47.1 0.0 collective-permute-done.3.refs_1_
  47.1 0.5 collective-permute-start.7
  47.6 0.0 collective-permute-done.16.refs_7_
  47.6 0.1 collective-permute-start.11
  47.7 1.6 %collective-permute-done.14.refs_5_ = bf16[14,32,128]{2,1,0:T(8,128)(2,1)S(1)} collective-permute-done((bf16[14,32,128]{2,1,0:T(8,128)(2,1)S(1)}, bf16[14,32,128]{2,1,0:T(8,128)(2,1)S(1)}, u32[]{:S(2)}, u32[]{:S(2)}) %collective-permute-start.14) | collective-permute-done | bytes 114720 | tf_op jit(solution)/shard_map/ppermute | solution.py:289
  49.3 0.0 collective-permute-start.5
  49.3 0.2 collective-permute-done.12.refs_3_
  49.5 0.3 collective-permute-start.17
  49.8 0.0 collective-permute-done.9.refs_7_
  49.8 0.2 collective-permute-start.15
  50.0 0.0 collective-permute-done.7.refs_5_
  50.0 0.3 collective-permute-start.13
  50.3 1.1 %shard_map.60 = (bf16[64,256]{1,0:T(8,128)(2,1)S(1)}, bf16[512,256]{1,0:T(8,128)(2,1)}) custom-call(f32[64,256]{1,0:T(8,128)S(1)} %get-tuple-element.15.part_ref, bf16[512,128]{1,0:T(8,128)(2,1)S(1)} %get-tuple-element.16.grad_ref, bf16[640,128]{1,0:T(8,128)(2,1)S(1)} %collective-permute-done.1.got_ref), custom_call_target="tpu_custom_call" | custom-call | bytes 1048576 | tf_op jit(solution)/shard_map/pallas_call | solution.py:304
  51.4 0.6 %reshape.20 = bf16[1,4,4,4,256]{4,3,2,1,0:T(4,128)(2,1)} reshape(bf16[64,256]{1,0:T(8,128)(2,1)S(1)} %get-tuple-element.18) | data formatting | bytes 65536 | tf_op jit(solution)/shard_map/reshape | solution.py:337
  52.1 0.0 collective-permute-done.5.refs_3_
  52.1 1.3 %shard_map.62.refs_0_ = f32[28,128,256]{2,1,0:T(8,128)} custom-call(bf16[14,32,128]{2,1,0:T(8,128)(2,1)S(1)} %add_convert_fusion.1.refs_0_, bf16[14,32,128]{2,1,0:T(8,128)(2,1)S(1)} %collective-permute-done.3.refs_1_, bf16[14,32,128]{2,1,0:T(8,128)(2,1)S(1)} %collective-permute-done.4.refs_2_, bf16[14,32,128]{2,1,0:T(8,128)(2,1)S(1)} %collective-permute-done.5.refs_3_, ...), custom_call_target="tpu_custom_call" | custom-call | tf_op jit(solution)/shard_map/pallas_call | solution.py:325
  53.4 0.0 collective-permute-done.11.refs_2_
  53.4 0.0 collective-permute-done.17.refs_8_
  53.4 0.0 collective-permute-done.15.refs_6_
  53.4 0.0 collective-permute-done.13.refs_4_
  53.4 1.4 %shard_map.63 = f32[28,128,256]{2,1,0:T(8,128)} custom-call(f32[28,128,256]{2,1,0:T(8,128)} %shard_map.62.refs_0_, bf16[14,32,128]{2,1,0:T(8,128)(2,1)S(1)} %add_convert_fusion.refs_1_, bf16[14,32,128]{2,1,0:T(8,128)(2,1)S(1)} %collective-permute-done.11.refs_2_, ...), custom_call_target="tpu_custom_call", output_to_operand_aliasing={{}: (0, {})} | custom-call | tf_op jit(solution)/shard_map/pallas_call | solution.py:325
  (2 shorter events, 0.1 us)
Async XLA Ops:
  0.6 26.7 %copy-start = (bf16[28,128,256]{2,1,0:T(8,128)(2,1)S(1)}, bf16[28,128,256]{2,1,0:T(8,128)(2,1)}, u32[]{:S(2)}) copy-start(bf16[28,128,256]{2,1,0:T(8,128)(2,1)} %w_ref.1) | copy-start | bytes 5505028
  1.5 1.0 %copy-start.1 = (bf16[1,8,8,8,256]{4,3,2,1,0:T(8,128)(2,1)S(1)}, bf16[1,8,8,8,256]{4,3,2,1,0:T(8,128)(2,1)}, u32[]{:S(2)}) copy-start(bf16[1,8,8,8,256]{4,3,2,1,0:T(8,128)(2,1)} %param.3) | copy-start | bytes 786436
  4.0 19.6 %all-to-all-start = ((bf16[16,192,128]{2,1,0:T(8,128)(2,1)}), bf16[16,192,128]{2,1,0:T(8,128)(2,1)S(1)}, u32[]{:S(2)}, u32[]{:S(2)}) async-start(bf16[16,192,128]{2,1,0:T(8,128)(2,1)} %get-tuple-element.20), calls=%async_computation | async-start | bytes 1572864 | tf_op jit(solution)/shard_map/all_to_all | solution.py:276
  10.3 17.1 %collective-permute-start = (bf16[640,128]{1,0:T(8,128)(2,1)S(1)}, bf16[640,128]{1,0:T(8,128)(2,1)S(1)}, u32[]{:S(2)}, u32[]{:S(2)}) collective-permute-start(bf16[640,128]{1,0:T(8,128)(2,1)S(1)} %get-tuple-element.14), channel_id=1, source_target_pairs={{0,1},{1,0},{2,3},{3,2},{4,5},{5,4},{6,7},{7,6},{8,9},{9,8},{10,11... | collective-permute-start | bytes 491528 | tf_op jit(solution)/shard_map/ppermute | solution.py:286
  24.7 11.7 %collective-permute-start.2 = (bf16[14,32,128]{2,1,0:T(8,128)(2,1)S(1)}, bf16[14,32,128]{2,1,0:T(8,128)(2,1)S(1)}, u32[]{:S(2)}, u32[]{:S(2)}) collective-permute-start(bf16[14,32,128]{2,1,0:T(8,128)(2,1)S(1)} %get-tuple-element.21), channel_id=1, source_target_pairs={{0,16},{2,18},{4,20},{6,22},{8,24},{10,26},{12,28},{14,30},{16,0},... | collective-permute-start | bytes 344072 | tf_op jit(solution)/shard_map/ppermute | solution.py:289
  28.5 11.5 %collective-permute-start.1 = (bf16[640,128]{1,0:T(8,128)(2,1)S(1)}, bf16[640,128]{1,0:T(8,128)(2,1)S(1)}, u32[]{:S(2)}, u32[]{:S(2)}) collective-permute-start(bf16[640,128]{1,0:T(8,128)(2,1)S(1)} %get-tuple-element.17), channel_id=1, source_target_pairs={{0,1},{1,0},{2,3},{3,2},{4,5},{5,4},{6,7},{7,6},{8,9},{9,8},{10,11... | collective-permute-start | bytes 491528 | tf_op jit(solution)/shard_map/ppermute | solution.py:303
  29.2 10.9 %collective-permute-start.10 = (bf16[14,32,128]{2,1,0:T(8,128)(2,1)S(1)}, bf16[14,32,128]{2,1,0:T(8,128)(2,1)S(1)}, u32[]{:S(2)}, u32[]{:S(2)}) collective-permute-start(bf16[14,32,128]{2,1,0:T(8,128)(2,1)S(1)} %get-tuple-element.22), channel_id=1, source_target_pairs={{0,16},{2,18},{4,20},{6,22},{8,24},{10,26},{12,28},{14,30},{16,0},... | collective-permute-start | bytes 344072 | tf_op jit(solution)/shard_map/ppermute | solution.py:289
  36.5 6.8 %collective-permute-start.8 = (bf16[14,32,128]{2,1,0:T(8,128)(2,1)S(1)}, bf16[14,32,128]{2,1,0:T(8,128)(2,1)S(1)}, u32[]{:S(2)}, u32[]{:S(2)}) collective-permute-start(bf16[14,32,128]{2,1,0:T(8,128)(2,1)S(1)} %add_convert_fusion.1.refs_0_), channel_id=1, source_target_pairs={{0,12},{2,14},{4,8},{6,10},{8,4},{10,6},{12,0},{14,2},{16,28},{18,... | collective-permute-start | bytes 344072 | tf_op jit(solution)/shard_map/ppermute | solution.py:289
  37.5 7.1 %collective-permute-start.6 = (bf16[14,32,128]{2,1,0:T(8,128)(2,1)S(1)}, bf16[14,32,128]{2,1,0:T(8,128)(2,1)S(1)}, u32[]{:S(2)}, u32[]{:S(2)}) collective-permute-start(bf16[14,32,128]{2,1,0:T(8,128)(2,1)S(1)} %add_convert_fusion.1.refs_0_), channel_id=1, source_target_pairs={{0,8},{2,10},{4,12},{6,14},{8,0},{10,2},{12,4},{14,6},{16,24},{18,... | collective-permute-start | bytes 344072 | tf_op jit(solution)/shard_map/ppermute | solution.py:289
  39.4 7.7 %collective-permute-start.4 = (bf16[14,32,128]{2,1,0:T(8,128)(2,1)S(1)}, bf16[14,32,128]{2,1,0:T(8,128)(2,1)S(1)}, u32[]{:S(2)}, u32[]{:S(2)}) collective-permute-start(bf16[14,32,128]{2,1,0:T(8,128)(2,1)S(1)} %add_convert_fusion.1.refs_0_), channel_id=1, source_target_pairs={{0,4},{2,6},{4,0},{6,2},{8,12},{10,14},{12,8},{14,10},{16,20},{18,... | collective-permute-start | bytes 344072 | tf_op jit(solution)/shard_map/ppermute | solution.py:289
  40.0 7.1 %collective-permute-start.3 = (bf16[14,32,128]{2,1,0:T(8,128)(2,1)S(1)}, bf16[14,32,128]{2,1,0:T(8,128)(2,1)S(1)}, u32[]{:S(2)}, u32[]{:S(2)}) collective-permute-start(bf16[14,32,128]{2,1,0:T(8,128)(2,1)S(1)} %add_convert_fusion.1.refs_0_), channel_id=1, source_target_pairs={{0,2},{2,0},{4,6},{6,4},{8,10},{10,8},{12,14},{14,12},{16,18},{18,... | collective-permute-start | bytes 344072 | tf_op jit(solution)/shard_map/ppermute | solution.py:289
  40.1 7.6 %collective-permute-start.16 = (bf16[14,32,128]{2,1,0:T(8,128)(2,1)S(1)}, bf16[14,32,128]{2,1,0:T(8,128)(2,1)S(1)}, u32[]{:S(2)}, u32[]{:S(2)}) collective-permute-start(bf16[14,32,128]{2,1,0:T(8,128)(2,1)S(1)} %add_convert_fusion.refs_1_), channel_id=1, source_target_pairs={{0,12},{2,14},{4,8},{6,10},{8,4},{10,6},{12,0},{14,2},{16,28},{18,... | collective-permute-start | bytes 344072 | tf_op jit(solution)/shard_map/ppermute | solution.py:289
  43.2 6.1 %collective-permute-start.14 = (bf16[14,32,128]{2,1,0:T(8,128)(2,1)S(1)}, bf16[14,32,128]{2,1,0:T(8,128)(2,1)S(1)}, u32[]{:S(2)}, u32[]{:S(2)}) collective-permute-start(bf16[14,32,128]{2,1,0:T(8,128)(2,1)S(1)} %add_convert_fusion.refs_1_), channel_id=1, source_target_pairs={{0,8},{2,10},{4,12},{6,14},{8,0},{10,2},{12,4},{14,6},{16,24},{18,... | collective-permute-start | bytes 344072 | tf_op jit(solution)/shard_map/ppermute | solution.py:289
  44.6 4.9 %collective-permute-start.12 = (bf16[14,32,128]{2,1,0:T(8,128)(2,1)S(1)}, bf16[14,32,128]{2,1,0:T(8,128)(2,1)S(1)}, u32[]{:S(2)}, u32[]{:S(2)}) collective-permute-start(bf16[14,32,128]{2,1,0:T(8,128)(2,1)S(1)} %add_convert_fusion.refs_1_), channel_id=1, source_target_pairs={{0,4},{2,6},{4,0},{6,2},{8,12},{10,14},{12,8},{14,10},{16,20},{18,... | collective-permute-start | bytes 344072 | tf_op jit(solution)/shard_map/ppermute | solution.py:289
  47.1 2.7 %collective-permute-start.9 = (bf16[14,32,128]{2,1,0:T(8,128)(2,1)S(1)}, bf16[14,32,128]{2,1,0:T(8,128)(2,1)S(1)}, u32[]{:S(2)}, u32[]{:S(2)}) collective-permute-start(bf16[14,32,128]{2,1,0:T(8,128)(2,1)S(1)} %collective-permute-done.8.refs_6_), channel_id=1, source_target_pairs={{0,2},{2,0},{4,6},{6,4},{8,10},{10,8},{12,14},{14,12},{16,18},{18,... | collective-permute-start | bytes 344072 | tf_op jit(solution)/shard_map/ppermute | solution.py:289
  47.1 2.9 %collective-permute-start.7 = (bf16[14,32,128]{2,1,0:T(8,128)(2,1)S(1)}, bf16[14,32,128]{2,1,0:T(8,128)(2,1)S(1)}, u32[]{:S(2)}, u32[]{:S(2)}) collective-permute-start(bf16[14,32,128]{2,1,0:T(8,128)(2,1)S(1)} %collective-permute-done.6.refs_4_), channel_id=1, source_target_pairs={{0,2},{2,0},{4,6},{6,4},{8,10},{10,8},{12,14},{14,12},{16,18},{18,... | collective-permute-start | bytes 344072 | tf_op jit(solution)/shard_map/ppermute | solution.py:289
  47.6 5.8 %collective-permute-start.11 = (bf16[14,32,128]{2,1,0:T(8,128)(2,1)S(1)}, bf16[14,32,128]{2,1,0:T(8,128)(2,1)S(1)}, u32[]{:S(2)}, u32[]{:S(2)}) collective-permute-start(bf16[14,32,128]{2,1,0:T(8,128)(2,1)S(1)} %add_convert_fusion.refs_1_), channel_id=1, source_target_pairs={{0,2},{2,0},{4,6},{6,4},{8,10},{10,8},{12,14},{14,12},{16,18},{18,... | collective-permute-start | bytes 344072 | tf_op jit(solution)/shard_map/ppermute | solution.py:289
  49.3 2.8 %collective-permute-start.5 = (bf16[14,32,128]{2,1,0:T(8,128)(2,1)S(1)}, bf16[14,32,128]{2,1,0:T(8,128)(2,1)S(1)}, u32[]{:S(2)}, u32[]{:S(2)}) collective-permute-start(bf16[14,32,128]{2,1,0:T(8,128)(2,1)S(1)} %collective-permute-done.4.refs_2_), channel_id=1, source_target_pairs={{0,2},{2,0},{4,6},{6,4},{8,10},{10,8},{12,14},{14,12},{16,18},{18,... | collective-permute-start | bytes 344072 | tf_op jit(solution)/shard_map/ppermute | solution.py:289
  49.5 3.9 %collective-permute-start.17 = (bf16[14,32,128]{2,1,0:T(8,128)(2,1)S(1)}, bf16[14,32,128]{2,1,0:T(8,128)(2,1)S(1)}, u32[]{:S(2)}, u32[]{:S(2)}) collective-permute-start(bf16[14,32,128]{2,1,0:T(8,128)(2,1)S(1)} %collective-permute-done.16.refs_7_), channel_id=1, source_target_pairs={{0,2},{2,0},{4,6},{6,4},{8,10},{10,8},{12,14},{14,12},{16,18},{18,... | collective-permute-start | bytes 344072 | tf_op jit(solution)/shard_map/ppermute | solution.py:289
  49.8 3.6 %collective-permute-start.15 = (bf16[14,32,128]{2,1,0:T(8,128)(2,1)S(1)}, bf16[14,32,128]{2,1,0:T(8,128)(2,1)S(1)}, u32[]{:S(2)}, u32[]{:S(2)}) collective-permute-start(bf16[14,32,128]{2,1,0:T(8,128)(2,1)S(1)} %collective-permute-done.14.refs_5_), channel_id=1, source_target_pairs={{0,2},{2,0},{4,6},{6,4},{8,10},{10,8},{12,14},{14,12},{16,18},{18,... | collective-permute-start | bytes 344072 | tf_op jit(solution)/shard_map/ppermute | solution.py:289
  50.0 3.4 %collective-permute-start.13 = (bf16[14,32,128]{2,1,0:T(8,128)(2,1)S(1)}, bf16[14,32,128]{2,1,0:T(8,128)(2,1)S(1)}, u32[]{:S(2)}, u32[]{:S(2)}) collective-permute-start(bf16[14,32,128]{2,1,0:T(8,128)(2,1)S(1)} %collective-permute-done.12.refs_3_), channel_id=1, source_target_pairs={{0,2},{2,0},{4,6},{6,4},{8,10},{10,8},{12,14},{14,12},{16,18},{18,... | collective-permute-start | bytes 344072 | tf_op jit(solution)/shard_map/ppermute | solution.py:289
where the time goes:
time: 55.1 us; the launch traced here: 54.8 us
  waiting for transfers between devices  25.6 us (46%)
  starting transfers between devices  18.4 us (33%)
  Pallas kernels  7.6 us (14%)
  local copies, waits for them, and re-layouts  2.48 us (5%)
  between operations  0.72 us (1%)
    ppermute x16, waiting for transfers between devices, across(): lax.ppermute(value, 'dp', [(i, i ^ distance) for i in range(groups_of)])  14.2 us
    all_to_all x1, waiting for transfers between devices, shards(): lax.all_to_all(pieces, ('dp', 'shard'), split_axis=0, concat_axis=0, tile...  11.3 us
    ppermute x16, starting transfers between devices, across(): lax.ppermute(value, 'dp', [(i, i ^ distance) for i in range(groups_of)])  9.51 us
    all_to_all x1, starting transfers between devices, shards(): lax.all_to_all(pieces, ('dp', 'shard'), split_axis=0, concat_axis=0, tile...  6.29 us
    pallas_call x2, Pallas kernels, shards(): pl.pallas_call(functools.partial(place_kernel, parts, width, block, int(b...  2.72 us
    ppermute x1, starting transfers between devices, shards(): other = lax.ppermute(send, 'shard', [(0, 1), (1, 0)])  1.93 us
    pallas_call x1, Pallas kernels, shards(): vmem_call(functools.partial(pack_kernel, edge, shards_of, parts), (shape(...  1.48 us
    pallas_call x1, Pallas kernels, shards(): vmem_call(functools.partial(weight_kernel, half, samples, width, splits),...  1.16 us
  transfers between devices with their start and end apart: 19, of which 7 were waited for; matrix products, arithmetic and copies ran while one was open for 1% of the time, Pallas kernels for 9%

commit v1 on v0

--- a/solution.py
+++ b/solution.py
@@ -9,6 +9,13 @@
 
 LANES = 128
 PARTS = 8
+DELIVERY = (3, 1, 2, 0)
+GATHER = (6, 4, 2)
+SPLITS = (14, 14)
+BLOCK = 7
+ORDER = (0, 1)
+DEPTH = 2
+FINISH = 2
 VMEM_BYTES = 48 * 1024 * 1024
 BF16 = jnp.bfloat16
 F32 = jnp.float32
@@ -71,68 +78,122 @@
     return (col == (row // plane) * plane + second * edge + third).astype(BF16)
 
 
-def pack_kernel(edge, shards_of, parts, x_ref, cot_ref, pieces_ref, send_ref, own_ref):
-    half = edge // 2
-    hh, cells, plane = half * half, half**3, edge * edge
-    groups = parts // 2
-    width = LANES // groups
-    here = lax.axis_index("shard")
+def rows_in(rows_ref, cot_ref, half):
+    for i in range(half):
+        for j in range(half):
+            start = (i * half + j) * half
+            rows_ref[start : start + half, :] = cot_ref[i, j].astype(F32)
+    return rows_ref[...].astype(BF16)
+
+
+def sorted_cells(edge, ref):
+    half = edge // 2
+    hh, plane = half * half, edge * edge
     blocks = 256 // plane
     order = plane_order(edge, blocks)
     planes = []
     for start in range(0, edge, blocks):
-        part = x_ref[start * plane : (start + blocks) * plane, :]
-        moved = dot(order, part).astype(BF16)
+        moved = dot(order, ref[start * plane : (start + blocks) * plane, :]).astype(BF16)
         planes += [moved[b * plane : (b + 1) * plane] for b in range(blocks)]
-    classes = []
-    for first in range(2):
-        for inner in range(4):
-            classes.append(
-                jnp.concatenate(
-                    [planes[2 * i + first][inner * hh : (inner + 1) * hh] for i in range(half)], axis=0
-                )
-            )
+    return [
+        jnp.concatenate([planes[2 * i + first][inner * hh : (inner + 1) * hh] for i in range(half)], axis=0)
+        for first in range(2)
+        for inner in range(4)
+    ]
+
+
+def put_cots(ref, start, cots):
+    cells = cots.shape[0]
+    for side in range(2):
+        ref[start + side * cells : start + (side + 1) * cells, :] = cots[:, side * LANES : (side + 1) * LANES]
+
+
+def sort_kernel(edge, x_hbm, cot_hbm, send_ref, own_ref, rows_ref, x_ref, cot_ref, sems):
+    half = edge // 2
+    cells = half**3
+    here = lax.axis_index("shard")
+    copies = [
+        pltpu.make_async_copy(x_hbm, x_ref, sems.at[0]),
+        pltpu.make_async_copy(cot_hbm, cot_ref, sems.at[1]),
+    ]
+    for copy in copies:
+        copy.start()
+    for copy in copies:
+        copy.wait()
+    for index, value in enumerate(sorted_cells(edge, x_ref)):
+        low, high = value[:, :LANES], value[:, LANES:]
+        own_ref[index * cells : (index + 1) * cells, :] = jnp.where(here == 0, low, high)
+        send_ref[index * cells : (index + 1) * cells, :] = jnp.where(here == 0, high, low)
+    cots = rows_in(rows_ref, cot_ref, half)
+    put_cots(own_ref, 8 * cells, cots)
+    put_cots(send_ref, 8 * cells, cots)
+
+
+def pack_kernel(edge, groups, own_ref, send_ref, x2_ref, cot2_ref, *refs):
+    piece_refs, rows_ref = refs[:groups], refs[groups]
+    half = edge // 2
+    cells = half**3
+    width = LANES // groups
+    place = lax.axis_index("dp")
+    core, group = lax.rem(place, 2), lax.rem(place // 2, groups)
+    target = lax.axis_index("shard") ^ core
+    samples = [
+        [
+            jnp.where(core == 0, own_ref[rows, :], send_ref[rows, :])
+            for rows in (slice(index * cells, (index + 1) * cells) for index in range(8))
+        ],
+        [
+            jnp.where(target == 0, value[:, :LANES], value[:, LANES:])
+            for value in sorted_cells(edge, x2_ref)
+        ],
+    ]
     size = 4 * LANES
     row = lax.broadcasted_iota(jnp.int32, (size, size), 0)
     col = lax.broadcasted_iota(jnp.int32, (size, size), 1)
     source = ((col // width) % 4) * LANES + (col // LANES) * width + col % width
     lane_order = (row == source).astype(BF16)
-    for owner in range(shards_of):
-        lanes = slice(owner * LANES, (owner + 1) * LANES)
-        wide = jnp.concatenate(
-            [
-                jnp.concatenate([classes[4 * first + inner][:, lanes] for inner in range(4)], axis=1)
-                for first in range(2)
-            ],
-            axis=0,
+    wide = jnp.concatenate(
+        [
+            jnp.concatenate(classes[4 * first : 4 * first + 4], axis=1)
+            for classes in samples
+            for first in range(2)
+        ],
+        axis=0,
+    )
+    packed = dot(wide, lane_order).astype(BF16)
+    cots = rows_in(rows_ref, cot2_ref, half)
+    for distance, ref in enumerate(piece_refs):
+        owner = group ^ distance
+        value = packed[:, (groups - 1) * LANES :]
+        for index in range(groups - 1):
+            value = jnp.where(owner == index, packed[:, index * LANES : (index + 1) * LANES], value)
+        ref[0 : 4 * cells, :] = value
+        ref[4 * cells : 6 * cells, :] = own_ref[8 * cells : 10 * cells, :]
+        put_cots(ref, 6 * cells, cots)
+
+
+def weight_kernel(half, groups, splits, *refs):
+    got_refs, out_refs = refs[:groups], refs[groups:]
+    cells = half**3
+    width = LANES // groups
+    core = lax.rem(lax.axis_index("dp"), 2)
+
+    def gather(offset):
+        return jnp.concatenate(
+            [ref[start : start + cells, :] for ref in got_refs for start in offset], axis=0
         )
-        packed = dot(wide, lane_order).astype(BF16)
-        for part in range(parts):
-            group, side = part // 2, part % 2
-            piece = part * shards_of + owner
-            pieces_ref[piece, 0 : 2 * cells, :] = packed[:, group * LANES : (group + 1) * LANES]
-            pieces_ref[piece, 2 * cells : 3 * cells, :] = cot_ref[:, side * LANES : (side + 1) * LANES]
-    for index, value in enumerate(classes):
-        low, high = value[:, :LANES], value[:, LANES:]
-        own_ref[index * cells : (index + 1) * cells, :] = jnp.where(here == 0, low, high)
-        send_ref[index * cells : (index + 1) * cells, :] = jnp.where(here == 0, high, low)
-    for side in range(2):
-        rows = slice((8 + side) * cells, (9 + side) * cells)
-        own_ref[rows, :] = cot_ref[:, side * LANES : (side + 1) * LANES]
-        send_ref[rows, :] = cot_ref[:, side * LANES : (side + 1) * LANES]
-
-
-def weight_kernel(half, samples, width, splits, got_ref, *out_refs):
-    cells = half**3
-    rows = samples * cells
+
     acts, raw = [], None
     for first in range(2):
-        value = got_ref[:, first * cells : (first + 1) * cells, :].reshape(rows, LANES)
+        value = gather([first * cells, (2 + first) * cells])
         if first == 0:
             raw = value
         wide = value.astype(F32)
         acts.append((wide / (1.0 + jnp.exp(-wide))).astype(BF16))
-    cots = got_ref[:, 2 * cells : 3 * cells, :].reshape(rows, LANES).astype(F32)
+    cots = jnp.concatenate(
+        [gather([(4 + side) * cells, (6 + side) * cells]) for side in range(2)], axis=1
+    ).astype(F32)
+    chans = 2 * LANES
     moved = {}
     for si in range(2):
         for sj in range(2):
@@ -147,13 +208,16 @@
     for parity, shift in tap_table():
         block = sums[parity[0], shift[0]]
         row = (2 * parity[1] + parity[2]) * width
-        col = (2 * shift[1] + shift[2]) * LANES
-        taps.append(block[row : row + width, col : col + LANES])
+        col = (2 * shift[1] + shift[2]) * chans
+        taps.append(block[row : row + width, col : col + chans])
     taps.append(dot(raw, moved[0, 0, 0], (0, 0))[:width])
     start = 0
-    for ref, count in zip(out_refs, splits):
-        for index in range(count):
-            ref[index] = taps[start + index].astype(BF16)
+    for index, count in enumerate(splits):
+        keep_ref, give_ref = out_refs[2 * index], out_refs[2 * index + 1]
+        for tap in range(count):
+            low, high = taps[start + tap][:, :LANES], taps[start + tap][:, LANES:]
+            keep_ref[tap] = jnp.where(core == 0, low, high)
+            give_ref[tap] = jnp.where(core == 0, high, low).astype(BF16)
         start += count
 
 
@@ -204,14 +268,18 @@
         ].astype(BF16)
 
 
-def finish_kernel(edge, part_ref, grad_ref, got_ref, out_ref, back_ref):
+def finish_kernel(edge, part_ref, grad_ref, got_ref, out_ref, back_ref, rows_ref):
     half = edge // 2
     hh, cells, plane = half * half, half**3, edge * edge
     here = lax.axis_index("shard")
     got = jnp.concatenate(
         [got_ref[8 * cells : 9 * cells, :], got_ref[9 * cells : 10 * cells, :]], axis=1
     )
-    out_ref[...] = (part_ref[...] + got.astype(F32)).astype(BF16)
+    rows_ref[...] = part_ref[...] + got.astype(F32)
+    for i in range(half):
+        for j in range(half):
+            start = (i * half + j) * half
+            out_ref[i, j] = rows_ref[start : start + half, :].astype(BF16)
     mine, theirs = grad_ref[...], got_ref[0 : 8 * cells, :]
     wide = jnp.concatenate(
         [jnp.where(here == 0, mine, theirs), jnp.where(here == 0, theirs, mine)], axis=1
@@ -242,12 +310,13 @@
         out_ref[:, rows, cols] = ref[pl.ds(step * block, block)].astype(F32)
 
 
-def vmem_call(body, outs, flops=0, **kwargs):
+def vmem_call(body, outs, flops=0, scratch=(), **kwargs):
     space = pl.BlockSpec(memory_space=pltpu.VMEM)
     return pl.pallas_call(
         body,
         out_shape=outs,
         out_specs=jax.tree.map(lambda _: space, outs),
+        scratch_shapes=scratch,
         compiler_params=pltpu.CompilerParams(vmem_limit_bytes=VMEM_BYTES),
         cost_estimate=pl.CostEstimate(flops=flops, bytes_accessed=1 << 20, transcendentals=0),
         **kwargs,
@@ -258,82 +327,112 @@
     return jax.ShapeDtypeStruct(dims, dtype)
 
 
+def after(value, *others):
+    return lax.optimization_barrier((value, *others))[0]
+
+
 def shards(groups_of, shards_of, inputs, cotangent, weights):
     edge, chans = inputs.shape[1], inputs.shape[4]
     half = edge // 2
     cells = half**3
     count, own_chans = weights.shape[0], weights.shape[1]
     parts = PARTS
-    samples = parts * shards_of
-    width = LANES // (parts // 2)
+    groups = parts // 2
+    width = LANES // groups
     values = inputs.reshape(edge**3, chans)
-    rows = cotangent.reshape(cells, chans)
-
-    pieces, send, own = vmem_call(
-        functools.partial(pack_kernel, edge, shards_of, parts),
-        (shape((samples, 3 * cells, LANES)), shape((10 * cells, LANES)), shape((10 * cells, LANES))),
-    )(values, rows)
-    got = lax.all_to_all(
-        pieces,
-        ("dp", "shard"),
-        split_axis=0,
-        concat_axis=0,
-        tiled=True,
-        axis_index_groups=[
-            [start + i for i in range(samples)] for start in range(0, groups_of * shards_of, samples)
-        ],
-    )
-    other = lax.ppermute(send, "shard", [(0, 1), (1, 0)])
+    rows = cotangent.reshape(cotangent.shape[1:])
+    row_buffer = [pltpu.VMEM((cells, chans), F32)]
 
     def across(value, distance):
         return lax.ppermute(value, "dp", [(i, i ^ distance) for i in range(groups_of)])
 
-    splits = (count // 2, count - count // 2)
+    def swap(value):
+        return lax.ppermute(value, "shard", [(0, 1), (1, 0)])
+
+    def deliver(value, distance):
+        pairs = []
+        for i in range(groups_of):
+            for j in range(shards_of):
+                pairs.append((i * shards_of + j, (i ^ (2 * distance)) * shards_of + (j ^ (i % 2))))
+        return lax.ppermute(value, ("dp", "shard"), pairs)
+
+    values2, rows2 = across(values, 1), across(rows, 1)
+    send, own = vmem_call(
+        functools.partial(sort_kernel, edge),
+        (shape((10 * cells, LANES)),) * 2,
+        scratch=row_buffer
+        + [
+            pltpu.VMEM(values.shape, BF16),
+            pltpu.VMEM(rows.shape, BF16),
+            pltpu.SemaphoreType.DMA((2,)),
+        ],
+        in_specs=[pl.BlockSpec(memory_space=pl.ANY)] * 2,
+    )(values, rows)
+    pieces = vmem_call(
+        functools.partial(pack_kernel, edge, groups),
+        (shape((8 * cells, LANES)),) * groups,
+        scratch=row_buffer,
+    )(own, send, values2, rows2)
+    got = [deliver(pieces[distance], distance) for distance in DELIVERY]
+    send = after(send, *got)
+    other = swap(send)
+
+    splits = SPLITS
     sums = vmem_call(
-        functools.partial(weight_kernel, half, samples, width, splits),
-        tuple(shape((n, width, LANES)) for n in splits),
-    )(got)
-    if not isinstance(sums, (tuple, list)):
-        sums = (sums,)
+        functools.partial(weight_kernel, half, groups, splits),
+        tuple(shape((n, width, LANES), t) for n in splits for t in (F32, BF16)),
+    )(*got)
+    totals = [
+        (sums[2 * i] + across(sums[2 * i + 1], 1).astype(F32)).astype(BF16) for i in range(len(splits))
+    ]
 
     part, grad, back = vmem_call(
         functools.partial(sample_kernel, half),
         (shape((cells, chans), F32), shape((8 * cells, LANES)), shape((10 * cells, LANES))),
-    )(own, other, weights)
-    returned = lax.ppermute(back, "shard", [(0, 1), (1, 0)])
+    )(own, after(other, *totals), weights)
+    returned = swap(back)
     outputs, input_grad = vmem_call(
         functools.partial(finish_kernel, edge),
-        (shape((cells, chans)), shape((edge**3, chans))),
+        (shape(rows.shape), shape((edge**3, chans))),
+        scratch=row_buffer,
     )(part, grad, returned)
 
-    block = count // 4
-    base = None
-    start = 0
-    for total, n in zip(sums, splits):
+    block = BLOCK
+    arrivals, held = [], []
+    for index in ORDER:
+        total = totals[index]
         distance = parts
         while distance < groups_of:
-            total = (total.astype(F32) + across(total, distance).astype(F32)).astype(BF16)
+            if len(arrivals) >= DEPTH:
+                total = after(total, arrivals[-DEPTH])
+            arrived = across(total, distance)
+            arrivals.append(arrived)
+            if len(arrivals) == FINISH:
+                arrived, outputs, input_grad = lax.optimization_barrier((arrived, outputs, input_grad))
+            total = (total.astype(F32) + arrived.astype(F32)).astype(BF16)
             distance *= 2
-        held = {0: total}
-        for distance in range(2, parts, 2):
-            held[distance] = across(total, distance)
-        for distance in range(0, parts, 2):
-            held[distance + 1] = across(held[distance], 1)
-        args = [held[i] for i in range(parts)]
+        held.append({0: total, **{distance: across(total, distance) for distance in GATHER}})
+    base = None
+    for turn, index in enumerate(ORDER):
+        n, start = splits[index], sum(splits[:index])
+        pieces = held[turn]
+        for distance in (0,) + GATHER:
+            value = pieces[distance]
+            if base is not None and distance == GATHER[-1]:
+                value = after(value, base)
+            pieces[distance + 1] = across(value, 1)
         whole = pl.BlockSpec(memory_space=pltpu.VMEM)
-        first = start // block
         base = pl.pallas_call(
             functools.partial(place_kernel, parts, width, block, int(base is not None)),
             grid=(n // block,),
             in_specs=([pl.BlockSpec(memory_space=pl.ANY)] if base is not None else []) + [whole] * parts,
             out_specs=pl.BlockSpec(
-                (block, own_chans, chans), functools.partial(lambda first, i: (first + i, 0, 0), first)
+                (block, own_chans, chans), functools.partial(lambda first, i: (first + i, 0, 0), start // block)
             ),
             out_shape=shape((count, own_chans, chans), F32),
             input_output_aliases={0: 0} if base is not None else {},
             compiler_params=pltpu.CompilerParams(vmem_limit_bytes=VMEM_BYTES),
-        )(*([base] if base is not None else []), *args)
-        start += n
+        )(*([base] if base is not None else []), *(pieces[i] for i in range(parts)))
     return outputs.reshape(cotangent.shape), input_grad.reshape(inputs.shape), base
 
 

time: 55.1 us -> 50.2 us (0.911)
  waiting for transfers between devices: 25.6 us -> 17.1 us
  starting transfers between devices: 18.4 us -> 22.1 us
  Pallas kernels: 7.6 us -> 6.62 us
  local copies, waits for them, and re-layouts: 2.48 us -> 3.21 us
    all_to_all x1 -> x0, waiting for transfers between devices: 11.3 us -> none  [shards(): lax.all_to_all(pieces, ('dp', 'shard'), split_axis=0, concat_axis=0, tile...]
    ppermute x2 -> x6, waiting for transfers between devices: 0.01 us -> 6.77 us  [the longest x4 6.28 us: deliver(): return lax.ppermute(value, ('dp', 'shard'), pairs)]
    all_to_all x1 -> x0, starting transfers between devices: 6.29 us -> none  [shards(): lax.all_to_all(pieces, ('dp', 'shard'), split_axis=0, concat_axis=0, tile...]
    ppermute x2 -> x6, starting transfers between devices: 2.56 us -> 8.32 us  [the longest x4 5.29 us: deliver(): return lax.ppermute(value, ('dp', 'shard'), pairs)]
    ppermute x16 -> x20, starting transfers between devices: 9.51 us -> 13.8 us  [across(): lax.ppermute(value, 'dp', [(i, i ^ distance) for i in range(groups_of)])]
    ppermute x16 -> x20, waiting for transfers between devices: 14.2 us -> 10.4 us  [across(): lax.ppermute(value, 'dp', [(i, i ^ distance) for i in range(groups_of)])]
    unnamed x4 -> x6, local copies, waits for them, and re-layouts: 0.95 us -> 3.21 us
    reshape x2 -> x0, local copies, waits for them, and re-layouts: 1.53 us -> none  [the longest x1 0.91 us: shards(): rows = cotangent.reshape(cells, chans)]
  transfers between devices with their start and end apart: 19 -> 26, of which waited for: 7 -> 12; matrix products, arithmetic and copies ran while one was open for 1% -> 0% of each run, Pallas kernels for 9% -> 8%
where the time goes in v1:
time: 50.2 us; the launch traced here: 49.9 us
  starting transfers between devices  22.1 us (44%)
  waiting for transfers between devices  17.1 us (34%)
  Pallas kernels  6.62 us (13%)
  local copies, waits for them, and re-layouts  3.21 us (6%)
  between operations  0.74 us (1%)
    ppermute x20, starting transfers between devices, across(): lax.ppermute(value, 'dp', [(i, i ^ distance) for i in range(groups_of)])  13.8 us
    ppermute x20, waiting for transfers between devices, across(): lax.ppermute(value, 'dp', [(i, i ^ distance) for i in range(groups_of)])  10.4 us
    ppermute x4, waiting for transfers between devices, deliver(): return lax.ppermute(value, ('dp', 'shard'), pairs)  6.28 us
    ppermute x4, starting transfers between devices, deliver(): return lax.ppermute(value, ('dp', 'shard'), pairs)  5.29 us
    unnamed x6, local copies, waits for them, and re-layouts  3.21 us
    ppermute x2, starting transfers between devices, swap(): return lax.ppermute(value, 'shard', [(0, 1), (1, 0)])  3.03 us
    pallas_call x2, Pallas kernels, shards(): pl.pallas_call(functools.partial(place_kernel, parts, width, block, int(b...  2.65 us
    pallas_call x1, Pallas kernels, shards(): vmem_call(functools.partial(sample_kernel, half), (shape((cells, chans),...  1.15 us
  transfers between devices with their start and end apart: 26, of which 12 were waited for; matrix products, arithmetic and copies ran while one was open for 0% of the time, Pallas kernels for 8%

profile of v1, /device:TPU:0, one launch (start us, length us, event | category | flops | bytes accessed | tf_op | source)
XLA Modules:
  0.0 49.9 jit_solution(3330527203095799157)
XLA Ops:
  0.6 0.5 %collective-permute-start = (bf16[512,256]{1,0:T(8,128)(2,1)}, bf16[512,256]{1,0:T(8,128)(2,1)S(1)}, u32[]{:S(2)}, u32[]{:S(2)}) collective-permute-start(bf16[512,256]{1,0:T(8,128)(2,1)} %bitcast.4), channel_id=1, source_target_pairs={{0,2},{2,0},{4,6},{6,4},{8,10},{10,8},{12,14},{14,12},{16,18},{18,... | collective-permute-start | bytes 786440 | tf_op jit(solution)/shard_map/ppermute | solution.py:347
  1.1 0.1 collective-permute-start.1
  1.2 0.0 copy-start.1
  1.2 0.9 %copy-done.1 = bf16[1,8,8,8,256]{4,3,2,1,0:T(8,128)(2,1)S(1)} copy-done((bf16[1,8,8,8,256]{4,3,2,1,0:T(8,128)(2,1)S(1)}, bf16[1,8,8,8,256]{4,3,2,1,0:T(8,128)(2,1)}, u32[]{:S(2)}) %copy-start.1) | copy-done | bytes 262168
  2.2 0.0 copy-start.2
  2.2 0.8 %copy-done.2 = bf16[1,4,4,4,256]{4,3,2,1,0:T(4,128)(2,1)S(1)} copy-done((bf16[1,4,4,4,256]{4,3,2,1,0:T(4,128)(2,1)S(1)}, bf16[1,4,4,4,256]{4,3,2,1,0:T(4,128)(2,1)}, u32[]{:S(2)}) %copy-start.2) | copy-done | bytes 32792
  2.9 0.4 shard_map.58
  3.3 0.0 collective-permute-done.1.cot2_ref
  3.3 0.0 collective-permute-done.x2_ref
  3.3 0.5 shard_map.59
  3.8 4.0 %collective-permute-start.2 = (bf16[512,128]{1,0:T(8,128)(2,1)S(1)}, bf16[512,128]{1,0:T(8,128)(2,1)S(1)}, u32[]{:S(2)}, u32[]{:S(2)}) collective-permute-start(bf16[512,128]{1,0:T(8,128)(2,1)S(1)} %get-tuple-element.26), channel_id=1, source_target_pairs={{0,12},{1,13},{2,15},{3,14},{4,8},{5,9},{6,11},{7,10},{8,4},{9,5},... | collective-permute-start | bytes 393224 | tf_op jit(solution)/shard_map/ppermute | solution.py:357
  7.8 0.5 %collective-permute-start.3 = (bf16[512,128]{1,0:T(8,128)(2,1)S(1)}, bf16[512,128]{1,0:T(8,128)(2,1)S(1)}, u32[]{:S(2)}, u32[]{:S(2)}) collective-permute-start(bf16[512,128]{1,0:T(8,128)(2,1)S(1)} %get-tuple-element.27), channel_id=1, source_target_pairs={{0,4},{1,5},{2,7},{3,6},{4,0},{5,1},{6,3},{7,2},{8,12},{9,13},{10,... | collective-permute-start | bytes 393224 | tf_op jit(solution)/shard_map/ppermute | solution.py:357
  8.4 0.1 collective-permute-start.4
  8.5 0.7 %collective-permute-start.5 = (bf16[512,128]{1,0:T(8,128)(2,1)S(1)}, bf16[512,128]{1,0:T(8,128)(2,1)S(1)}, u32[]{:S(2)}, u32[]{:S(2)}) collective-permute-start(bf16[512,128]{1,0:T(8,128)(2,1)S(1)} %get-tuple-element.29), channel_id=1, source_target_pairs={{0,0},{1,1},{2,3},{3,2},{4,4},{5,5},{6,7},{7,6},{8,8},{9,9},{10,11... | collective-permute-start | bytes 393224 | tf_op jit(solution)/shard_map/ppermute | solution.py:357
  9.1 2.7 %collective-permute-done.2.refs_0_ = bf16[512,128]{1,0:T(8,128)(2,1)S(1)} collective-permute-done((bf16[512,128]{1,0:T(8,128)(2,1)S(1)}, bf16[512,128]{1,0:T(8,128)(2,1)S(1)}, u32[]{:S(2)}, u32[]{:S(2)}) %collective-permute-start.2) | collective-permute-done | bytes 131104 | tf_op jit(solution)/shard_map/ppermute | solution.py:357
  11.8 3.1 %collective-permute-done.3.refs_1_ = bf16[512,128]{1,0:T(8,128)(2,1)S(1)} collective-permute-done((bf16[512,128]{1,0:T(8,128)(2,1)S(1)}, bf16[512,128]{1,0:T(8,128)(2,1)S(1)}, u32[]{:S(2)}, u32[]{:S(2)}) %collective-permute-start.3) | collective-permute-done | bytes 131104 | tf_op jit(solution)/shard_map/ppermute | solution.py:357
  15.0 0.4 collective-permute-done.4.refs_2_
  15.4 0.0 collective-permute-done.5.refs_3_
  15.4 0.9 %shard_map.60 = (f32[14,32,128]{2,1,0:T(8,128)S(1)}, bf16[14,32,128]{2,1,0:T(8,128)(2,1)S(1)}, f32[14,32,128]{2,1,0:T(8,128)S(1)}, bf16[14,32,128]{2,1,0:T(8,128)(2,1)S(1)}) custom-call(bf16[512,128]{1,0:T(8,128)(2,1)S(1)} %collective-permute-done.2.refs_0_, bf16[512,128]{1,0:T(8,128)(2,1)S(1)} %collective-permute-done.3.refs_1_, ...), custom_call_target="tpu_custom_call" | custom-call | bytes 1048576 | tf_op jit(solution)/shard_map/pallas_call | solution.py:381
  16.3 1.1 %collective-permute-start.9 = (bf16[14,32,128]{2,1,0:T(8,128)(2,1)S(1)}, bf16[14,32,128]{2,1,0:T(8,128)(2,1)S(1)}, u32[]{:S(2)}, u32[]{:S(2)}) collective-permute-start(bf16[14,32,128]{2,1,0:T(8,128)(2,1)S(1)} %get-tuple-element.34), channel_id=1, source_target_pairs={{0,2},{2,0},{4,6},{6,4},{8,10},{10,8},{12,14},{14,12},{16,18},{18,... | collective-permute-start | bytes 344072 | tf_op jit(solution)/shard_map/ppermute | solution.py:347
  17.4 1.5 %collective-permute-start.8 = (bf16[640,128]{1,0:T(8,128)(2,1)S(1)}, bf16[640,128]{1,0:T(8,128)(2,1)S(1)}, u32[]{:S(2)}, u32[]{:S(2)}) collective-permute-start(bf16[640,128]{1,0:T(8,128)(2,1)S(1)} %get-tuple-element.32.send_ref), channel_id=1, source_target_pairs={{0,1},{1,0},{2,3},{3,2},{4,5},{5,4},{6,7},{7,6},{8,9},{9,8},{10,11... | collective-permute-start | bytes 491528 | tf_op jit(solution)/shard_map/ppermute | solution.py:350
  18.9 0.0 collective-permute-start.6
  18.9 0.0 collective-permute-done.9
  18.9 2.9 %collective-permute-start.11 = (bf16[14,32,128]{2,1,0:T(8,128)(2,1)S(1)}, bf16[14,32,128]{2,1,0:T(8,128)(2,1)S(1)}, u32[]{:S(2)}, u32[]{:S(2)}) collective-permute-start(bf16[14,32,128]{2,1,0:T(8,128)(2,1)S(1)} %add_convert_fusion.2), channel_id=1, source_target_pairs={{0,16},{2,18},{4,20},{6,22},{8,24},{10,26},{12,28},{14,30},{16,0},... | collective-permute-start | bytes 344072 | tf_op jit(solution)/shard_map/ppermute | solution.py:347
  21.8 0.0 collective-permute-done.6
  21.8 1.3 %collective-permute-start.7 = (bf16[14,32,128]{2,1,0:T(8,128)(2,1)S(1)}, bf16[14,32,128]{2,1,0:T(8,128)(2,1)S(1)}, u32[]{:S(2)}, u32[]{:S(2)}) collective-permute-start(bf16[14,32,128]{2,1,0:T(8,128)(2,1)S(1)} %add_convert_fusion.3), channel_id=1, source_target_pairs={{0,16},{2,18},{4,20},{6,22},{8,24},{10,26},{12,28},{14,30},{16,0},... | collective-permute-start | bytes 344072 | tf_op jit(solution)/shard_map/ppermute | solution.py:347
  23.1 0.5 collective-permute-done.8.other_ref
  23.6 1.5 %copy-done = bf16[28,128,256]{2,1,0:T(8,128)(2,1)S(1)} copy-done((bf16[28,128,256]{2,1,0:T(8,128)(2,1)S(1)}, bf16[28,128,256]{2,1,0:T(8,128)(2,1)}, u32[]{:S(2)}) %copy-start) | copy-done | bytes 1835032
  25.1 1.1 %shard_map.61 = (f32[64,256]{1,0:T(8,128)S(1)}, bf16[512,128]{1,0:T(8,128)(2,1)S(1)}, bf16[640,128]{1,0:T(8,128)(2,1)S(1)}) custom-call(bf16[640,128]{1,0:T(8,128)(2,1)S(1)} %get-tuple-element.24.own_ref, bf16[640,128]{1,0:T(8,128)(2,1)S(1)} %collective-permute-done.8.other_ref, bf16[28,128,256]{2,1,0:T(8,128)(2,1)S(1)} %copy-done), custom_call_target="tpu_custom_call" | custom-call | bytes 1048576 | tf_op jit(solution)/shard_map/pallas_call | solution.py:389
  26.2 1.5 %collective-permute-start.10 = (bf16[640,128]{1,0:T(8,128)(2,1)S(1)}, bf16[640,128]{1,0:T(8,128)(2,1)S(1)}, u32[]{:S(2)}, u32[]{:S(2)}) collective-permute-start(bf16[640,128]{1,0:T(8,128)(2,1)S(1)} %get-tuple-element.38), channel_id=1, source_target_pairs={{0,1},{1,0},{2,3},{3,2},{4,5},{5,4},{6,7},{7,6},{8,9},{9,8},{10,11... | collective-permute-start | bytes 491528 | tf_op jit(solution)/shard_map/ppermute | solution.py:350
  27.8 3.0 %collective-permute-done.11 = bf16[14,32,128]{2,1,0:T(8,128)(2,1)S(1)} collective-permute-done((bf16[14,32,128]{2,1,0:T(8,128)(2,1)S(1)}, bf16[14,32,128]{2,1,0:T(8,128)(2,1)S(1)}, u32[]{:S(2)}, u32[]{:S(2)}) %collective-permute-start.11) | collective-permute-done | bytes 114720 | tf_op jit(solution)/shard_map/ppermute | solution.py:347
  30.9 1.0 %collective-permute-start.17 = (bf16[14,32,128]{2,1,0:T(8,128)(2,1)S(1)}, bf16[14,32,128]{2,1,0:T(8,128)(2,1)S(1)}, u32[]{:S(2)}, u32[]{:S(2)}) collective-permute-start(bf16[14,32,128]{2,1,0:T(8,128)(2,1)S(1)} %add_convert_fusion.1.refs_0_), channel_id=1, source_target_pairs={{0,12},{2,14},{4,8},{6,10},{8,4},{10,6},{12,0},{14,2},{16,28},{18,... | collective-permute-start | bytes 344072 | tf_op jit(solution)/shard_map/ppermute | solution.py:347
  31.8 2.0 %collective-permute-start.15 = (bf16[14,32,128]{2,1,0:T(8,128)(2,1)S(1)}, bf16[14,32,128]{2,1,0:T(8,128)(2,1)S(1)}, u32[]{:S(2)}, u32[]{:S(2)}) collective-permute-start(bf16[14,32,128]{2,1,0:T(8,128)(2,1)S(1)} %add_convert_fusion.1.refs_0_), channel_id=1, source_target_pairs={{0,8},{2,10},{4,12},{6,14},{8,0},{10,2},{12,4},{14,6},{16,24},{18,... | collective-permute-start | bytes 344072 | tf_op jit(solution)/shard_map/ppermute | solution.py:347
  33.8 0.6 %collective-permute-start.13 = (bf16[14,32,128]{2,1,0:T(8,128)(2,1)S(1)}, bf16[14,32,128]{2,1,0:T(8,128)(2,1)S(1)}, u32[]{:S(2)}, u32[]{:S(2)}) collective-permute-start(bf16[14,32,128]{2,1,0:T(8,128)(2,1)S(1)} %add_convert_fusion.1.refs_0_), channel_id=1, source_target_pairs={{0,4},{2,6},{4,0},{6,2},{8,12},{10,14},{12,8},{14,10},{16,20},{18,... | collective-permute-start | bytes 344072 | tf_op jit(solution)/shard_map/ppermute | solution.py:347
  34.4 0.0 collective-permute-done.10.got_ref
  34.4 0.0 collective-permute-start.12
  34.4 1.1 %shard_map.62 = (bf16[4,4,4,256]{3,2,1,0:T(4,128)(2,1)}, bf16[512,256]{1,0:T(8,128)(2,1)}) custom-call(f32[64,256]{1,0:T(8,128)S(1)} %get-tuple-element.36.part_ref, bf16[512,128]{1,0:T(8,128)(2,1)S(1)} %get-tuple-element.37.grad_ref, bf16[640,128]{1,0:T(8,128)(2,1)S(1)} %collective-permute-done.10.got_ref), custom_call_target="tpu_custom_call" | custom-call | bytes 1048576 | tf_op jit(solution)/shard_map/pallas_call | solution.py:394
  35.5 0.0 collective-permute-done.7
  35.6 1.0 %collective-permute-start.24 = (bf16[14,32,128]{2,1,0:T(8,128)(2,1)S(1)}, bf16[14,32,128]{2,1,0:T(8,128)(2,1)S(1)}, u32[]{:S(2)}, u32[]{:S(2)}) collective-permute-start(bf16[14,32,128]{2,1,0:T(8,128)(2,1)S(1)} %add_convert_fusion.refs_1_), channel_id=1, source_target_pairs={{0,12},{2,14},{4,8},{6,10},{8,4},{10,6},{12,0},{14,2},{16,28},{18,... | collective-permute-start | bytes 344072 | tf_op jit(solution)/shard_map/ppermute | solution.py:347
  36.5 1.2 %collective-permute-done.17.refs_6_ = bf16[14,32,128]{2,1,0:T(8,128)(2,1)S(1)} collective-permute-done((bf16[14,32,128]{2,1,0:T(8,128)(2,1)S(1)}, bf16[14,32,128]{2,1,0:T(8,128)(2,1)S(1)}, u32[]{:S(2)}, u32[]{:S(2)}) %collective-permute-start.17) | collective-permute-done | bytes 114720 | tf_op jit(solution)/shard_map/ppermute | solution.py:347
  37.7 0.8 %collective-permute-start.22 = (bf16[14,32,128]{2,1,0:T(8,128)(2,1)S(1)}, bf16[14,32,128]{2,1,0:T(8,128)(2,1)S(1)}, u32[]{:S(2)}, u32[]{:S(2)}) collective-permute-start(bf16[14,32,128]{2,1,0:T(8,128)(2,1)S(1)} %add_convert_fusion.refs_1_), channel_id=1, source_target_pairs={{0,8},{2,10},{4,12},{6,14},{8,0},{10,2},{12,4},{14,6},{16,24},{18,... | collective-permute-start | bytes 344072 | tf_op jit(solution)/shard_map/ppermute | solution.py:347
  38.5 0.1 collective-permute-done.15.refs_4_
  38.7 0.0 collective-permute-start.18
  38.7 0.2 collective-permute-done.13.refs_2_
  38.9 0.3 collective-permute-start.16
  39.2 0.0 collective-permute-done.12.refs_1_
  39.2 0.2 collective-permute-start.14
  39.4 3.0 %collective-permute-done.24.refs_7_ = bf16[14,32,128]{2,1,0:T(8,128)(2,1)S(1)} collective-permute-done((bf16[14,32,128]{2,1,0:T(8,128)(2,1)S(1)}, bf16[14,32,128]{2,1,0:T(8,128)(2,1)S(1)}, u32[]{:S(2)}, u32[]{:S(2)}) %collective-permute-start.24) | collective-permute-done | bytes 114720 | tf_op jit(solution)/shard_map/ppermute | solution.py:347
  42.5 1.5 %collective-permute-start.20 = (bf16[14,32,128]{2,1,0:T(8,128)(2,1)S(1)}, bf16[14,32,128]{2,1,0:T(8,128)(2,1)S(1)}, u32[]{:S(2)}, u32[]{:S(2)}) collective-permute-start(bf16[14,32,128]{2,1,0:T(8,128)(2,1)S(1)} %add_convert_fusion.refs_1_), channel_id=1, source_target_pairs={{0,4},{2,6},{4,0},{6,2},{8,12},{10,14},{12,8},{14,10},{16,20},{18,... | collective-permute-start | bytes 344072 | tf_op jit(solution)/shard_map/ppermute | solution.py:347
  43.9 0.6 %collective-permute-done.22.refs_5_ = bf16[14,32,128]{2,1,0:T(8,128)(2,1)S(1)} collective-permute-done((bf16[14,32,128]{2,1,0:T(8,128)(2,1)S(1)}, bf16[14,32,128]{2,1,0:T(8,128)(2,1)S(1)}, u32[]{:S(2)}, u32[]{:S(2)}) %collective-permute-start.22) | collective-permute-done | bytes 114720 | tf_op jit(solution)/shard_map/ppermute | solution.py:347
  44.5 0.0 collective-permute-start.19
  44.5 0.0 collective-permute-done.18.refs_7_
  44.5 0.5 %collective-permute-start.25 = (bf16[14,32,128]{2,1,0:T(8,128)(2,1)S(1)}, bf16[14,32,128]{2,1,0:T(8,128)(2,1)S(1)}, u32[]{:S(2)}, u32[]{:S(2)}) collective-permute-start(bf16[14,32,128]{2,1,0:T(8,128)(2,1)S(1)} %collective-permute-done.24.refs_7_), channel_id=1, source_target_pairs={{0,2},{2,0},{4,6},{6,4},{8,10},{10,8},{12,14},{14,12},{16,18},{18,... | collective-permute-start | bytes 344072 | tf_op jit(solution)/shard_map/ppermute | solution.py:347
  45.0 0.0 collective-permute-done.16.refs_5_
  45.0 0.1 collective-permute-start.23
  45.1 0.0 collective-permute-done.14.refs_3_
  45.1 1.3 %shard_map.63.refs_0_ = f32[28,128,256]{2,1,0:T(8,128)} custom-call(bf16[14,32,128]{2,1,0:T(8,128)(2,1)S(1)} %add_convert_fusion.1.refs_0_, bf16[14,32,128]{2,1,0:T(8,128)(2,1)S(1)} %collective-permute-done.12.refs_1_, bf16[14,32,128]{2,1,0:T(8,128)(2,1)S(1)} %collective-permute-done.13.refs_2_, bf16[14,32,128]{2,1,0:T(8,128)(2,1)S(1)} %collective-permute-done.14.refs_3_, ...), custom_call_target="tpu_custom_call" | custom-call | tf_op jit(solution)/shard_map/pallas_call | solution.py:425
  46.4 0.8 %collective-permute-done.20.refs_3_ = bf16[14,32,128]{2,1,0:T(8,128)(2,1)S(1)} collective-permute-done((bf16[14,32,128]{2,1,0:T(8,128)(2,1)S(1)}, bf16[14,32,128]{2,1,0:T(8,128)(2,1)S(1)}, u32[]{:S(2)}, u32[]{:S(2)}) %collective-permute-start.20) | collective-permute-done | bytes 114720 | tf_op jit(solution)/shard_map/ppermute | solution.py:347
  47.3 0.0 collective-permute-start.21
  47.3 0.0 collective-permute-done.19.refs_2_
  47.3 0.0 collective-permute-done.25.refs_8_
  47.3 0.0 collective-permute-done.23.refs_6_
  47.3 1.3 %collective-permute-done.21.refs_4_ = bf16[14,32,128]{2,1,0:T(8,128)(2,1)S(1)} collective-permute-done((bf16[14,32,128]{2,1,0:T(8,128)(2,1)S(1)}, bf16[14,32,128]{2,1,0:T(8,128)(2,1)S(1)}, u32[]{:S(2)}, u32[]{:S(2)}) %collective-permute-start.21) | collective-permute-done | bytes 114720 | tf_op jit(solution)/shard_map/ppermute | solution.py:347
  48.6 1.3 %shard_map.64 = f32[28,128,256]{2,1,0:T(8,128)} custom-call(f32[28,128,256]{2,1,0:T(8,128)} %shard_map.63.refs_0_, bf16[14,32,128]{2,1,0:T(8,128)(2,1)S(1)} %add_convert_fusion.refs_1_, bf16[14,32,128]{2,1,0:T(8,128)(2,1)S(1)} %collective-permute-done.19.refs_2_, ...), custom_call_target="tpu_custom_call", output_to_operand_aliasing={{}: (0, {})} | custom-call | tf_op jit(solution)/shard_map/pallas_call | solution.py:425
  (5 shorter events, 0.1 us)
Async XLA Ops:
  0.6 2.7 %collective-permute-start = (bf16[512,256]{1,0:T(8,128)(2,1)}, bf16[512,256]{1,0:T(8,128)(2,1)S(1)}, u32[]{:S(2)}, u32[]{:S(2)}) collective-permute-start(bf16[512,256]{1,0:T(8,128)(2,1)} %bitcast.4), channel_id=1, source_target_pairs={{0,2},{2,0},{4,6},{6,4},{8,10},{10,8},{12,14},{14,12},{16,18},{18,... | collective-permute-start | bytes 786440 | tf_op jit(solution)/shard_map/ppermute | solution.py:347
  1.1 2.2 %collective-permute-start.1 = (bf16[4,4,4,256]{3,2,1,0:T(4,128)(2,1)}, bf16[4,4,4,256]{3,2,1,0:T(4,128)(2,1)S(1)}, u32[]{:S(2)}, u32[]{:S(2)}) collective-permute-start(bf16[4,4,4,256]{3,2,1,0:T(4,128)(2,1)} %bitcast.6), channel_id=1, source_target_pairs={{0,2},{2,0},{4,6},{6,4},{8,10},{10,8},{12,14},{14,12},{16,18},{18,... | collective-permute-start | bytes 98312 | tf_op jit(solution)/shard_map/ppermute | solution.py:347
  1.2 0.9 %copy-start.1 = (bf16[1,8,8,8,256]{4,3,2,1,0:T(8,128)(2,1)S(1)}, bf16[1,8,8,8,256]{4,3,2,1,0:T(8,128)(2,1)}, u32[]{:S(2)}) copy-start(bf16[1,8,8,8,256]{4,3,2,1,0:T(8,128)(2,1)} %param.3) | copy-start | bytes 786436
  2.2 0.8 %copy-start.2 = (bf16[1,4,4,4,256]{4,3,2,1,0:T(4,128)(2,1)S(1)}, bf16[1,4,4,4,256]{4,3,2,1,0:T(4,128)(2,1)}, u32[]{:S(2)}) copy-start(bf16[1,4,4,4,256]{4,3,2,1,0:T(4,128)(2,1)} %param.4) | copy-start | bytes 98308
  3.8 8.0 %collective-permute-start.2 = (bf16[512,128]{1,0:T(8,128)(2,1)S(1)}, bf16[512,128]{1,0:T(8,128)(2,1)S(1)}, u32[]{:S(2)}, u32[]{:S(2)}) collective-permute-start(bf16[512,128]{1,0:T(8,128)(2,1)S(1)} %get-tuple-element.26), channel_id=1, source_target_pairs={{0,12},{1,13},{2,15},{3,14},{4,8},{5,9},{6,11},{7,10},{8,4},{9,5},... | collective-permute-start | bytes 393224 | tf_op jit(solution)/shard_map/ppermute | solution.py:357
  7.8 7.2 %collective-permute-start.3 = (bf16[512,128]{1,0:T(8,128)(2,1)S(1)}, bf16[512,128]{1,0:T(8,128)(2,1)S(1)}, u32[]{:S(2)}, u32[]{:S(2)}) collective-permute-start(bf16[512,128]{1,0:T(8,128)(2,1)S(1)} %get-tuple-element.27), channel_id=1, source_target_pairs={{0,4},{1,5},{2,7},{3,6},{4,0},{5,1},{6,3},{7,2},{8,12},{9,13},{10,... | collective-permute-start | bytes 393224 | tf_op jit(solution)/shard_map/ppermute | solution.py:357
  8.4 7.1 %collective-permute-start.4 = (bf16[512,128]{1,0:T(8,128)(2,1)S(1)}, bf16[512,128]{1,0:T(8,128)(2,1)S(1)}, u32[]{:S(2)}, u32[]{:S(2)}) collective-permute-start(bf16[512,128]{1,0:T(8,128)(2,1)S(1)} %get-tuple-element.28), channel_id=1, source_target_pairs={{0,8},{1,9},{2,11},{3,10},{4,12},{5,13},{6,15},{7,14},{8,0},{9,1},... | collective-permute-start | bytes 393224 | tf_op jit(solution)/shard_map/ppermute | solution.py:357
  8.5 7.0 %collective-permute-start.5 = (bf16[512,128]{1,0:T(8,128)(2,1)S(1)}, bf16[512,128]{1,0:T(8,128)(2,1)S(1)}, u32[]{:S(2)}, u32[]{:S(2)}) collective-permute-start(bf16[512,128]{1,0:T(8,128)(2,1)S(1)} %get-tuple-element.29), channel_id=1, source_target_pairs={{0,0},{1,1},{2,3},{3,2},{4,4},{5,5},{6,7},{7,6},{8,8},{9,9},{10,11... | collective-permute-start | bytes 393224 | tf_op jit(solution)/shard_map/ppermute | solution.py:357
  16.3 2.6 %collective-permute-start.9 = (bf16[14,32,128]{2,1,0:T(8,128)(2,1)S(1)}, bf16[14,32,128]{2,1,0:T(8,128)(2,1)S(1)}, u32[]{:S(2)}, u32[]{:S(2)}) collective-permute-start(bf16[14,32,128]{2,1,0:T(8,128)(2,1)S(1)} %get-tuple-element.34), channel_id=1, source_target_pairs={{0,2},{2,0},{4,6},{6,4},{8,10},{10,8},{12,14},{14,12},{16,18},{18,... | collective-permute-start | bytes 344072 | tf_op jit(solution)/shard_map/ppermute | solution.py:347
  17.4 6.2 %collective-permute-start.8 = (bf16[640,128]{1,0:T(8,128)(2,1)S(1)}, bf16[640,128]{1,0:T(8,128)(2,1)S(1)}, u32[]{:S(2)}, u32[]{:S(2)}) collective-permute-start(bf16[640,128]{1,0:T(8,128)(2,1)S(1)} %get-tuple-element.32.send_ref), channel_id=1, source_target_pairs={{0,1},{1,0},{2,3},{3,2},{4,5},{5,4},{6,7},{7,6},{8,9},{9,8},{10,11... | collective-permute-start | bytes 491528 | tf_op jit(solution)/shard_map/ppermute | solution.py:350
  18.9 2.9 %collective-permute-start.6 = (bf16[14,32,128]{2,1,0:T(8,128)(2,1)S(1)}, bf16[14,32,128]{2,1,0:T(8,128)(2,1)S(1)}, u32[]{:S(2)}, u32[]{:S(2)}) collective-permute-start(bf16[14,32,128]{2,1,0:T(8,128)(2,1)S(1)} %get-tuple-element.31), channel_id=1, source_target_pairs={{0,2},{2,0},{4,6},{6,4},{8,10},{10,8},{12,14},{14,12},{16,18},{18,... | collective-permute-start | bytes 344072 | tf_op jit(solution)/shard_map/ppermute | solution.py:347
  18.9 11.9 %collective-permute-start.11 = (bf16[14,32,128]{2,1,0:T(8,128)(2,1)S(1)}, bf16[14,32,128]{2,1,0:T(8,128)(2,1)S(1)}, u32[]{:S(2)}, u32[]{:S(2)}) collective-permute-start(bf16[14,32,128]{2,1,0:T(8,128)(2,1)S(1)} %add_convert_fusion.2), channel_id=1, source_target_pairs={{0,16},{2,18},{4,20},{6,22},{8,24},{10,26},{12,28},{14,30},{16,0},... | collective-permute-start | bytes 344072 | tf_op jit(solution)/shard_map/ppermute | solution.py:347
  21.8 13.7 %collective-permute-start.7 = (bf16[14,32,128]{2,1,0:T(8,128)(2,1)S(1)}, bf16[14,32,128]{2,1,0:T(8,128)(2,1)S(1)}, u32[]{:S(2)}, u32[]{:S(2)}) collective-permute-start(bf16[14,32,128]{2,1,0:T(8,128)(2,1)S(1)} %add_convert_fusion.3), channel_id=1, source_target_pairs={{0,16},{2,18},{4,20},{6,22},{8,24},{10,26},{12,28},{14,30},{16,0},... | collective-permute-start | bytes 344072 | tf_op jit(solution)/shard_map/ppermute | solution.py:347
  23.6 1.5 %copy-start = (bf16[28,128,256]{2,1,0:T(8,128)(2,1)S(1)}, bf16[28,128,256]{2,1,0:T(8,128)(2,1)}, u32[]{:S(2)}) copy-start(bf16[28,128,256]{2,1,0:T(8,128)(2,1)} %w_ref.1) | copy-start | bytes 5505028
  26.2 8.2 %collective-permute-start.10 = (bf16[640,128]{1,0:T(8,128)(2,1)S(1)}, bf16[640,128]{1,0:T(8,128)(2,1)S(1)}, u32[]{:S(2)}, u32[]{:S(2)}) collective-permute-start(bf16[640,128]{1,0:T(8,128)(2,1)S(1)} %get-tuple-element.38), channel_id=1, source_target_pairs={{0,1},{1,0},{2,3},{3,2},{4,5},{5,4},{6,7},{7,6},{8,9},{9,8},{10,11... | collective-permute-start | bytes 491528 | tf_op jit(solution)/shard_map/ppermute | solution.py:350
  30.9 6.9 %collective-permute-start.17 = (bf16[14,32,128]{2,1,0:T(8,128)(2,1)S(1)}, bf16[14,32,128]{2,1,0:T(8,128)(2,1)S(1)}, u32[]{:S(2)}, u32[]{:S(2)}) collective-permute-start(bf16[14,32,128]{2,1,0:T(8,128)(2,1)S(1)} %add_convert_fusion.1.refs_0_), channel_id=1, source_target_pairs={{0,12},{2,14},{4,8},{6,10},{8,4},{10,6},{12,0},{14,2},{16,28},{18,... | collective-permute-start | bytes 344072 | tf_op jit(solution)/shard_map/ppermute | solution.py:347
  31.8 6.9 %collective-permute-start.15 = (bf16[14,32,128]{2,1,0:T(8,128)(2,1)S(1)}, bf16[14,32,128]{2,1,0:T(8,128)(2,1)S(1)}, u32[]{:S(2)}, u32[]{:S(2)}) collective-permute-start(bf16[14,32,128]{2,1,0:T(8,128)(2,1)S(1)} %add_convert_fusion.1.refs_0_), channel_id=1, source_target_pairs={{0,8},{2,10},{4,12},{6,14},{8,0},{10,2},{12,4},{14,6},{16,24},{18,... | collective-permute-start | bytes 344072 | tf_op jit(solution)/shard_map/ppermute | solution.py:347
  33.8 5.1 %collective-permute-start.13 = (bf16[14,32,128]{2,1,0:T(8,128)(2,1)S(1)}, bf16[14,32,128]{2,1,0:T(8,128)(2,1)S(1)}, u32[]{:S(2)}, u32[]{:S(2)}) collective-permute-start(bf16[14,32,128]{2,1,0:T(8,128)(2,1)S(1)} %add_convert_fusion.1.refs_0_), channel_id=1, source_target_pairs={{0,4},{2,6},{4,0},{6,2},{8,12},{10,14},{12,8},{14,10},{16,20},{18,... | collective-permute-start | bytes 344072 | tf_op jit(solution)/shard_map/ppermute | solution.py:347
  34.4 4.8 %collective-permute-start.12 = (bf16[14,32,128]{2,1,0:T(8,128)(2,1)S(1)}, bf16[14,32,128]{2,1,0:T(8,128)(2,1)S(1)}, u32[]{:S(2)}, u32[]{:S(2)}) collective-permute-start(bf16[14,32,128]{2,1,0:T(8,128)(2,1)S(1)} %add_convert_fusion.1.refs_0_), channel_id=1, source_target_pairs={{0,2},{2,0},{4,6},{6,4},{8,10},{10,8},{12,14},{14,12},{16,18},{18,... | collective-permute-start | bytes 344072 | tf_op jit(solution)/shard_map/ppermute | solution.py:347
  35.6 6.9 %collective-permute-start.24 = (bf16[14,32,128]{2,1,0:T(8,128)(2,1)S(1)}, bf16[14,32,128]{2,1,0:T(8,128)(2,1)S(1)}, u32[]{:S(2)}, u32[]{:S(2)}) collective-permute-start(bf16[14,32,128]{2,1,0:T(8,128)(2,1)S(1)} %add_convert_fusion.refs_1_), channel_id=1, source_target_pairs={{0,12},{2,14},{4,8},{6,10},{8,4},{10,6},{12,0},{14,2},{16,28},{18,... | collective-permute-start | bytes 344072 | tf_op jit(solution)/shard_map/ppermute | solution.py:347
  37.7 6.8 %collective-permute-start.22 = (bf16[14,32,128]{2,1,0:T(8,128)(2,1)S(1)}, bf16[14,32,128]{2,1,0:T(8,128)(2,1)S(1)}, u32[]{:S(2)}, u32[]{:S(2)}) collective-permute-start(bf16[14,32,128]{2,1,0:T(8,128)(2,1)S(1)} %add_convert_fusion.refs_1_), channel_id=1, source_target_pairs={{0,8},{2,10},{4,12},{6,14},{8,0},{10,2},{12,4},{14,6},{16,24},{18,... | collective-permute-start | bytes 344072 | tf_op jit(solution)/shard_map/ppermute | solution.py:347
  38.7 5.9 %collective-permute-start.18 = (bf16[14,32,128]{2,1,0:T(8,128)(2,1)S(1)}, bf16[14,32,128]{2,1,0:T(8,128)(2,1)S(1)}, u32[]{:S(2)}, u32[]{:S(2)}) collective-permute-start(bf16[14,32,128]{2,1,0:T(8,128)(2,1)S(1)} %collective-permute-done.17.refs_6_), channel_id=1, source_target_pairs={{0,2},{2,0},{4,6},{6,4},{8,10},{10,8},{12,14},{14,12},{16,18},{18,... | collective-permute-start | bytes 344072 | tf_op jit(solution)/shard_map/ppermute | solution.py:347
  38.9 6.1 %collective-permute-start.16 = (bf16[14,32,128]{2,1,0:T(8,128)(2,1)S(1)}, bf16[14,32,128]{2,1,0:T(8,128)(2,1)S(1)}, u32[]{:S(2)}, u32[]{:S(2)}) collective-permute-start(bf16[14,32,128]{2,1,0:T(8,128)(2,1)S(1)} %collective-permute-done.15.refs_4_), channel_id=1, source_target_pairs={{0,2},{2,0},{4,6},{6,4},{8,10},{10,8},{12,14},{14,12},{16,18},{18,... | collective-permute-start | bytes 344072 | tf_op jit(solution)/shard_map/ppermute | solution.py:347
  39.2 5.9 %collective-permute-start.14 = (bf16[14,32,128]{2,1,0:T(8,128)(2,1)S(1)}, bf16[14,32,128]{2,1,0:T(8,128)(2,1)S(1)}, u32[]{:S(2)}, u32[]{:S(2)}) collective-permute-start(bf16[14,32,128]{2,1,0:T(8,128)(2,1)S(1)} %collective-permute-done.13.refs_2_), channel_id=1, source_target_pairs={{0,2},{2,0},{4,6},{6,4},{8,10},{10,8},{12,14},{14,12},{16,18},{18,... | collective-permute-start | bytes 344072 | tf_op jit(solution)/shard_map/ppermute | solution.py:347
  42.5 4.8 %collective-permute-start.20 = (bf16[14,32,128]{2,1,0:T(8,128)(2,1)S(1)}, bf16[14,32,128]{2,1,0:T(8,128)(2,1)S(1)}, u32[]{:S(2)}, u32[]{:S(2)}) collective-permute-start(bf16[14,32,128]{2,1,0:T(8,128)(2,1)S(1)} %add_convert_fusion.refs_1_), channel_id=1, source_target_pairs={{0,4},{2,6},{4,0},{6,2},{8,12},{10,14},{12,8},{14,10},{16,20},{18,... | collective-permute-start | bytes 344072 | tf_op jit(solution)/shard_map/ppermute | solution.py:347
  44.5 2.7 %collective-permute-start.19 = (bf16[14,32,128]{2,1,0:T(8,128)(2,1)S(1)}, bf16[14,32,128]{2,1,0:T(8,128)(2,1)S(1)}, u32[]{:S(2)}, u32[]{:S(2)}) collective-permute-start(bf16[14,32,128]{2,1,0:T(8,128)(2,1)S(1)} %add_convert_fusion.refs_1_), channel_id=1, source_target_pairs={{0,2},{2,0},{4,6},{6,4},{8,10},{10,8},{12,14},{14,12},{16,18},{18,... | collective-permute-start | bytes 344072 | tf_op jit(solution)/shard_map/ppermute | solution.py:347
  44.5 2.7 %collective-permute-start.25 = (bf16[14,32,128]{2,1,0:T(8,128)(2,1)S(1)}, bf16[14,32,128]{2,1,0:T(8,128)(2,1)S(1)}, u32[]{:S(2)}, u32[]{:S(2)}) collective-permute-start(bf16[14,32,128]{2,1,0:T(8,128)(2,1)S(1)} %collective-permute-done.24.refs_7_), channel_id=1, source_target_pairs={{0,2},{2,0},{4,6},{6,4},{8,10},{10,8},{12,14},{14,12},{16,18},{18,... | collective-permute-start | bytes 344072 | tf_op jit(solution)/shard_map/ppermute | solution.py:347
  45.0 2.2 %collective-permute-start.23 = (bf16[14,32,128]{2,1,0:T(8,128)(2,1)S(1)}, bf16[14,32,128]{2,1,0:T(8,128)(2,1)S(1)}, u32[]{:S(2)}, u32[]{:S(2)}) collective-permute-start(bf16[14,32,128]{2,1,0:T(8,128)(2,1)S(1)} %collective-permute-done.22.refs_5_), channel_id=1, source_target_pairs={{0,2},{2,0},{4,6},{6,4},{8,10},{10,8},{12,14},{14,12},{16,18},{18,... | collective-permute-start | bytes 344072 | tf_op jit(solution)/shard_map/ppermute | solution.py:347
  47.3 1.3 %collective-permute-start.21 = (bf16[14,32,128]{2,1,0:T(8,128)(2,1)S(1)}, bf16[14,32,128]{2,1,0:T(8,128)(2,1)S(1)}, u32[]{:S(2)}, u32[]{:S(2)}) collective-permute-start(bf16[14,32,128]{2,1,0:T(8,128)(2,1)S(1)} %collective-permute-done.20.refs_3_), channel_id=1, source_target_pairs={{0,2},{2,0},{4,6},{6,4},{8,10},{10,8},{12,14},{14,12},{16,18},{18,... | collective-permute-start | bytes 344072 | tf_op jit(solution)/shard_map/ppermute | solution.py:347

commit v2 on v1

--- a/solution.py
+++ b/solution.py
@@ -14,8 +14,13 @@
 SPLITS = (14, 14)
 BLOCK = 7
 ORDER = (0, 1)
-DEPTH = 2
-FINISH = 2
+SWAP = 2
+SAMPLE = 1
+STAGGER = True
+BACK = 4
+FINISH = 1
+DELAY = 0
+PLACE = 0
 VMEM_BYTES = 48 * 1024 * 1024
 BF16 = jnp.bfloat16
 F32 = jnp.float32
@@ -172,71 +177,68 @@
         put_cots(ref, 6 * cells, cots)
 
 
-def weight_kernel(half, groups, splits, *refs):
-    got_refs, out_refs = refs[:groups], refs[groups:]
+def weight_kernel(half, groups, start, count, *refs):
+    got_refs, (keep_ref, give_ref) = refs[:groups], refs[groups:]
     cells = half**3
     width = LANES // groups
+    chans = 2 * LANES
     core = lax.rem(lax.axis_index("dp"), 2)
+    table = tap_table()
+    wanted = range(start, start + count)
+    needs = {(table[tap][0][0], table[tap][1][0]) for tap in wanted if tap < len(table)}
 
     def gather(offset):
         return jnp.concatenate(
             [ref[start : start + cells, :] for ref in got_refs for start in offset], axis=0
         )
 
-    acts, raw = [], None
+    raw, acts = {}, {}
     for first in range(2):
-        value = gather([first * cells, (2 + first) * cells])
-        if first == 0:
-            raw = value
-        wide = value.astype(F32)
-        acts.append((wide / (1.0 + jnp.exp(-wide))).astype(BF16))
+        raw[first] = gather([first * cells, (2 + first) * cells])
+        wide = raw[first].astype(F32)
+        acts[first] = (wide / (1.0 + jnp.exp(-wide))).astype(BF16)
     cots = jnp.concatenate(
         [gather([(4 + side) * cells, (6 + side) * cells]) for side in range(2)], axis=1
-    ).astype(F32)
-    chans = 2 * LANES
-    moved = {}
-    for si in range(2):
-        for sj in range(2):
-            for sk in range(2):
-                moved[si, sj, sk] = shift_rows(cots, (si, sj, sk), half, False).astype(BF16)
+    )
     sums = {}
     for si in range(2):
-        right = jnp.concatenate([moved[si, sj, sk] for sj in range(2) for sk in range(2)], axis=1)
-        for first in range(si, 2):
-            sums[first, si] = dot(acts[first], right, (0, 0))
-    taps = []
-    for parity, shift in tap_table():
-        block = sums[parity[0], shift[0]]
-        row = (2 * parity[1] + parity[2]) * width
-        col = (2 * shift[1] + shift[2]) * chans
-        taps.append(block[row : row + width, col : col + chans])
-    taps.append(dot(raw, moved[0, 0, 0], (0, 0))[:width])
-    start = 0
-    for index, count in enumerate(splits):
-        keep_ref, give_ref = out_refs[2 * index], out_refs[2 * index + 1]
-        for tap in range(count):
-            low, high = taps[start + tap][:, :LANES], taps[start + tap][:, LANES:]
-            keep_ref[tap] = jnp.where(core == 0, low, high)
-            give_ref[tap] = jnp.where(core == 0, high, low).astype(BF16)
-        start += count
-
-
-def sample_kernel(half, own_ref, other_ref, w_ref, part_ref, grad_ref, send_ref):
+        firsts = [first for first in range(2) if (first, si) in needs]
+        if firsts:
+            right = jnp.concatenate(
+                [
+                    shift_rows(cots.astype(F32), (si, sj, sk), half, False).astype(BF16)
+                    for sj in range(2)
+                    for sk in range(2)
+                ],
+                axis=1,
+            )
+            for first in firsts:
+                sums[first, si] = dot(acts[first], right, (0, 0))
+    for tap in wanted:
+        if tap < len(table):
+            parity, shift = table[tap]
+            row = (2 * parity[1] + parity[2]) * width
+            col = (2 * shift[1] + shift[2]) * chans
+            value = sums[parity[0], shift[0]][row : row + width, col : col + chans]
+        else:
+            value = dot(raw[0], cots, (0, 0))[:width]
+        low, high = value[:, :LANES], value[:, LANES:]
+        keep_ref[tap - start] = jnp.where(core == 0, low, high)
+        give_ref[tap - start] = jnp.where(core == 0, high, low).astype(BF16)
+
+
+def sample_kernel(half, give, own_ref, w_ref, *refs):
+    grad_ref = refs[-1]
     cells = half**3
-    both = 2 * cells
     count = len(tap_table())
-
-    def rows_of(index):
-        rows = slice(index * cells, (index + 1) * cells)
-        return jnp.concatenate([own_ref[rows, :], other_ref[rows, :]], axis=0)
-
-    cots = jnp.concatenate([rows_of(8), rows_of(9)], axis=1).astype(F32)
+    cots = jnp.concatenate([own_ref[(8 + side) * cells : (9 + side) * cells, :] for side in range(2)], axis=1).astype(F32)
     moved, gathered = {}, {}
     shifts = [(si, sj, sk) for si in range(2) for sj in range(2) for sk in range(2)]
     for shift in shifts:
         moved[shift] = shift_rows(cots, shift, half, False).astype(BF16)
     for index in range(8):
-        value = rows_of(index)
+        rows = slice(index * cells, (index + 1) * cells)
+        value = own_ref[rows, :]
         wide = value.astype(F32)
         sigma = 1.0 / (1.0 + jnp.exp(-wide))
         act = (wide * sigma).astype(BF16)
@@ -254,18 +256,14 @@
             weight = w_ref[count]
             gathered[0, 0, 0] = gathered[0, 0, 0] + dot(value, weight)
             grad = grad + dot(moved[0, 0, 0], weight, (1, 1))
-        grad = grad.astype(BF16)
-        rows = slice(index * cells, (index + 1) * cells)
-        grad_ref[rows, :] = grad[:cells]
-        send_ref[rows, :] = grad[cells:]
+        grad_ref[rows, :] = grad.astype(BF16)
     total = gathered[0, 0, 0]
     for shift in shifts[1:]:
         total = total + shift_rows(gathered[shift], shift, half, True)
-    part_ref[...] = total[:cells]
-    for side in range(2):
-        send_ref[(8 + side) * cells : (9 + side) * cells, :] = total[
-            cells:both, side * LANES : (side + 1) * LANES
-        ].astype(BF16)
+    if give:
+        put_cots(grad_ref, 8 * cells, total.astype(BF16))
+    else:
+        refs[0][...] = total
 
 
 def finish_kernel(edge, part_ref, grad_ref, got_ref, out_ref, back_ref, rows_ref):
@@ -298,16 +296,31 @@
         ).astype(BF16)
 
 
-def place_kernel(parts, width, block, has_base, *refs):
-    piece_refs, out_ref = refs[has_base : has_base + parts], refs[-1]
-    part = lax.rem(lax.axis_index("dp"), parts)
-    step = pl.program_id(0)
-    for distance, ref in enumerate(piece_refs):
-        owner = part ^ distance
-        group, side = owner // 2, lax.rem(owner, 2)
-        rows = pl.ds(pl.multiple_of(group * width, width), width)
+def place_kernel(parts, width, step, runs, has_base, *refs):
+    out_ref, buffer, sem = refs[-3:]
+    refs = refs[has_base:-3]
+    place = lax.axis_index("dp")
+    part = lax.rem(place, parts)
+    copies = []
+    for slot, (start, flip, pieces) in enumerate(runs):
+        count = pieces[0][3]
+        for index, offset, distance, _ in pieces:
+            group = (part ^ distance) // 2
+            rows = pl.ds(pl.multiple_of(group * width, width), width)
+            buffer[start : start + count, rows, flip * LANES : (flip + 1) * LANES] = refs[index][
+                offset : offset + count
+            ].astype(F32)
+        side = lax.rem(place, 2) ^ flip
         cols = pl.ds(pl.multiple_of(side * LANES, LANES), LANES)
-        out_ref[:, rows, cols] = ref[pl.ds(step * block, block)].astype(F32)
+        copy = pltpu.make_async_copy(
+            buffer.at[start : start + count, :, flip * LANES : (flip + 1) * LANES],
+            out_ref.at[start : start + count, :, cols],
+            sem.at[slot],
+        )
+        copy.start()
+        copies.append(copy)
+    for copy in copies:
+        copy.wait()
 
 
 def vmem_call(body, outs, flops=0, scratch=(), **kwargs):
@@ -373,23 +386,47 @@
         (shape((8 * cells, LANES)),) * groups,
         scratch=row_buffer,
     )(own, send, values2, rows2)
+    splits = SPLITS
     got = [deliver(pieces[distance], distance) for distance in DELIVERY]
-    send = after(send, *got)
+    if SWAP == 1:
+        send = after(send, *pieces)
+    elif SWAP == 2:
+        send = after(send, *got)
     other = swap(send)
 
-    splits = SPLITS
-    sums = vmem_call(
-        functools.partial(weight_kernel, half, groups, splits),
-        tuple(shape((n, width, LANES), t) for n in splits for t in (F32, BF16)),
-    )(*got)
-    totals = [
-        (sums[2 * i] + across(sums[2 * i + 1], 1).astype(F32)).astype(BF16) for i in range(len(splits))
-    ]
-
-    part, grad, back = vmem_call(
-        functools.partial(sample_kernel, half),
-        (shape((cells, chans), F32), shape((8 * cells, LANES)), shape((10 * cells, LANES))),
-    )(own, after(other, *totals), weights)
+    part, grad = vmem_call(
+        functools.partial(sample_kernel, half, False),
+        (shape((cells, chans), F32), shape((8 * cells, LANES))),
+    )(own, weights)
+    if SAMPLE == 0:
+        other, part, grad = lax.optimization_barrier((other, part, grad))
+    (back,) = vmem_call(
+        functools.partial(sample_kernel, half, True), (shape((10 * cells, LANES)),)
+    )(other, weights)
+    if SAMPLE == 0:
+        *got, back = lax.optimization_barrier((*got, back))
+    elif SAMPLE == 1:
+        *got, part, grad = lax.optimization_barrier((*got, part, grad))
+    totals, sums = {}, []
+    for turn, index in enumerate(ORDER):
+        n, start = splits[index], sum(splits[:index])
+        operands = got
+        if turn == 1 and STAGGER:
+            operands = lax.optimization_barrier((*got, totals[ORDER[0]]))[:-1]
+        keep, give = vmem_call(
+            functools.partial(weight_kernel, half, groups, start, n),
+            (shape((n, width, LANES), F32), shape((n, width, LANES))),
+        )(*operands)
+        sums.append(give)
+        if turn == 0 and BACK == 3:
+            back = after(back, give)
+        totals[index] = (keep + across(give, 1).astype(F32)).astype(BF16)
+        if turn == 0 and BACK == 4:
+            back = after(back, totals[index])
+    if BACK == 1:
+        back = after(back, *totals.values())
+    elif BACK == 2:
+        back = after(back, *sums)
     returned = swap(back)
     outputs, input_grad = vmem_call(
         functools.partial(finish_kernel, edge),
@@ -397,42 +434,73 @@
         scratch=row_buffer,
     )(part, grad, returned)
 
-    block = BLOCK
-    arrivals, held = [], []
-    for index in ORDER:
+    held = []
+    for turn, index in enumerate(ORDER):
         total = totals[index]
+        if turn == 1 and DELAY == 1:
+            total = after(total, other)
+        if turn == 1 and DELAY == 2:
+            total = after(total, back)
         distance = parts
         while distance < groups_of:
-            if len(arrivals) >= DEPTH:
-                total = after(total, arrivals[-DEPTH])
             arrived = across(total, distance)
-            arrivals.append(arrived)
-            if len(arrivals) == FINISH:
+            if turn == FINISH:
                 arrived, outputs, input_grad = lax.optimization_barrier((arrived, outputs, input_grad))
             total = (total.astype(F32) + arrived.astype(F32)).astype(BF16)
             distance *= 2
-        held.append({0: total, **{distance: across(total, distance) for distance in GATHER}})
+        held.append(total)
+    direct, crossed = [None] * len(splits), [None] * len(splits)
+    for index, total in zip(ORDER, held):
+        direct[index] = [total] + [across(total, distance) for distance in GATHER]
+    for index in ORDER:
+        crossed[index] = across(jnp.concatenate(direct[index], axis=0), 1)
     base = None
-    for turn, index in enumerate(ORDER):
-        n, start = splits[index], sum(splits[:index])
-        pieces = held[turn]
-        for distance in (0,) + GATHER:
-            value = pieces[distance]
-            if base is not None and distance == GATHER[-1]:
-                value = after(value, base)
-            pieces[distance + 1] = across(value, 1)
-        whole = pl.BlockSpec(memory_space=pltpu.VMEM)
-        base = pl.pallas_call(
-            functools.partial(place_kernel, parts, width, block, int(base is not None)),
-            grid=(n // block,),
-            in_specs=([pl.BlockSpec(memory_space=pl.ANY)] if base is not None else []) + [whole] * parts,
-            out_specs=pl.BlockSpec(
-                (block, own_chans, chans), functools.partial(lambda first, i: (first + i, 0, 0), start // block)
-            ),
+
+    def put(base, operands, runs):
+        have = [] if base is None else [base]
+        return pl.pallas_call(
+            functools.partial(place_kernel, parts, width, BLOCK, runs, len(have)),
+            in_specs=[pl.BlockSpec(memory_space=pl.ANY)] * len(have)
+            + [pl.BlockSpec(memory_space=pltpu.VMEM)] * len(operands),
+            out_specs=pl.BlockSpec(memory_space=pl.ANY),
             out_shape=shape((count, own_chans, chans), F32),
-            input_output_aliases={0: 0} if base is not None else {},
+            scratch_shapes=[
+                pltpu.VMEM((count, own_chans, chans), F32),
+                pltpu.SemaphoreType.DMA((len(runs),)),
+            ],
+            input_output_aliases={0: 0} if have else {},
             compiler_params=pltpu.CompilerParams(vmem_limit_bytes=VMEM_BYTES),
-        )(*([base] if base is not None else []), *(pieces[i] for i in range(parts)))
+        )(*have, *operands)
+
+    def runs_of(indices, sets):
+        runs, at = [], 0
+        for index, kinds in zip(indices, sets):
+            n, first = splits[index], sum(splits[:index])
+            for kind in kinds:
+                for low in range(0, n, BLOCK):
+                    size = min(BLOCK, n - low)
+                    pieces = []
+                    for order, distance in enumerate((0,) + GATHER):
+                        if kind == 0:
+                            pieces.append((at + order, low, distance, size))
+                        else:
+                            pieces.append((at, order * n + low, distance, size))
+                    runs.append((first + low, kind, pieces))
+                at += 1 if kind else 1 + len(GATHER)
+        return runs
+
+    if PLACE == 0:
+        base = put(None, sum(direct, []), runs_of(range(len(splits)), [(0,)] * len(splits)))
+        base = put(base, crossed, runs_of(range(len(splits)), [(1,)] * len(splits)))
+    else:
+        early, late = ORDER[0], ORDER[1]
+        base = put(None, direct[early] + [crossed[early]], runs_of([early], [(0, 1)]))
+        if PLACE == 2:
+            *there, base = lax.optimization_barrier((*direct[late], base))
+            direct[late] = list(there)
+            crossed[late] = across(jnp.concatenate(there, axis=0), 1)
+        base = put(base, direct[late], runs_of([late], [(0,)]))
+        base = put(base, [crossed[late]], runs_of([late], [(1,)]))
     return outputs.reshape(cotangent.shape), input_grad.reshape(inputs.shape), base
 
 

time: 50.2 us -> 46.8 us (0.932)
  waiting for transfers between devices: 17.1 us -> 11.4 us
  Pallas kernels: 6.62 us -> 7.82 us
  starting transfers between devices: 22.1 us -> 23.1 us
    ppermute x20 -> x14, waiting for transfers between devices: 10.4 us -> 6.43 us  [across(): lax.ppermute(value, 'dp', [(i, i ^ distance) for i in range(groups_of)])]
    ppermute x4, waiting for transfers between devices: 6.28 us -> 3.82 us  [deliver(): return lax.ppermute(value, ('dp', 'shard'), pairs)]
    pallas_call x4 -> x6, Pallas kernels: 4.66 us -> 5.85 us  [the longest x2 2.63 us: put(): pl.pallas_call(functools.partial(place_kernel, parts, width, BLOCK, runs,...]
    ppermute x20 -> x14, starting transfers between devices: 13.8 us -> 14.7 us  [across(): lax.ppermute(value, 'dp', [(i, i ^ distance) for i in range(groups_of)])]
    ppermute x2, waiting for transfers between devices: 0.48 us -> 1.12 us  [swap(): return lax.ppermute(value, 'shard', [(0, 1), (1, 0)])]
    unnamed x6 -> x8, local copies, waits for them, and re-layouts: 3.21 us -> 3.21 us
  transfers between devices with their start and end apart: 26 -> 20, of which waited for: 12 -> 10; matrix products, arithmetic and copies ran while one was open for 0% -> 1% of each run, Pallas kernels for 8% -> 11%
where the time goes in v2:
time: 46.8 us; the launch traced here: 46.5 us
  starting transfers between devices  23.1 us (49%)
  waiting for transfers between devices  11.4 us (24%)
  Pallas kernels  7.82 us (17%)
  local copies, waits for them, and re-layouts  3.21 us (7%)
  between operations  0.79 us (2%)
    ppermute x14, starting transfers between devices, across(): lax.ppermute(value, 'dp', [(i, i ^ distance) for i in range(groups_of)])  14.7 us
    ppermute x14, waiting for transfers between devices, across(): lax.ppermute(value, 'dp', [(i, i ^ distance) for i in range(groups_of)])  6.43 us
    ppermute x4, starting transfers between devices, deliver(): return lax.ppermute(value, ('dp', 'shard'), pairs)  5.29 us
    ppermute x4, waiting for transfers between devices, deliver(): return lax.ppermute(value, ('dp', 'shard'), pairs)  3.82 us
    unnamed x8, local copies, waits for them, and re-layouts  3.21 us
    ppermute x2, starting transfers between devices, swap(): return lax.ppermute(value, 'shard', [(0, 1), (1, 0)])  3.03 us
    pallas_call x2, Pallas kernels, put(): pl.pallas_call(functools.partial(place_kernel, parts, width, BLOCK, runs,...  2.63 us
    pallas_call x2, Pallas kernels, shards(): vmem_call(functools.partial(weight_kernel, half, groups, start, n), (shap...  1.31 us
  transfers between devices with their start and end apart: 20, of which 10 were waited for; matrix products, arithmetic and copies ran while one was open for 1% of the time, Pallas kernels for 11%

profile of v2, /device:TPU:0, one launch (start us, length us, event | category | flops | bytes accessed | tf_op | source)
XLA Modules:
  0.0 46.5 jit_solution(6581230769651731874)
XLA Ops:
  0.6 0.5 %collective-permute-start = (bf16[512,256]{1,0:T(8,128)(2,1)}, bf16[512,256]{1,0:T(8,128)(2,1)S(1)}, u32[]{:S(2)}, u32[]{:S(2)}) collective-permute-start(bf16[512,256]{1,0:T(8,128)(2,1)} %bitcast.4), channel_id=1, source_target_pairs={{0,2},{2,0},{4,6},{6,4},{8,10},{10,8},{12,14},{14,12},{16,18},{18,... | collective-permute-start | bytes 786440 | tf_op jit(solution)/shard_map/ppermute | solution.py:360
  1.1 0.1 collective-permute-start.1
  1.2 0.0 copy-start.2
  1.2 0.9 %copy-done.2 = bf16[1,8,8,8,256]{4,3,2,1,0:T(8,128)(2,1)S(1)} copy-done((bf16[1,8,8,8,256]{4,3,2,1,0:T(8,128)(2,1)S(1)}, bf16[1,8,8,8,256]{4,3,2,1,0:T(8,128)(2,1)}, u32[]{:S(2)}) %copy-start.2) | copy-done | bytes 262168
  2.2 0.0 copy-start.3
  2.2 0.8 %copy-done.3 = bf16[1,4,4,4,256]{4,3,2,1,0:T(4,128)(2,1)S(1)} copy-done((bf16[1,4,4,4,256]{4,3,2,1,0:T(4,128)(2,1)S(1)}, bf16[1,4,4,4,256]{4,3,2,1,0:T(4,128)(2,1)}, u32[]{:S(2)}) %copy-start.3) | copy-done | bytes 32792
  2.9 0.4 shard_map.58
  3.3 0.0 collective-permute-done.1.cot2_ref
  3.3 0.0 collective-permute-done.x2_ref
  3.3 0.5 %shard_map.59 = (bf16[512,128]{1,0:T(8,128)(2,1)S(1)}, bf16[512,128]{1,0:T(8,128)(2,1)S(1)}, bf16[512,128]{1,0:T(8,128)(2,1)S(1)}, bf16[512,128]{1,0:T(8,128)(2,1)S(1)}) custom-call(bf16[640,128]{1,0:T(8,128)(2,1)S(1)} %get-tuple-element.32.own_ref, bf16[640,128]{1,0:T(8,128)(2,1)S(1)} %get-tuple-element.54.send_ref, ...), custom_call_target="tpu_custom_call" | custom-call | bytes 1048576 | tf_op jit(solution)/shard_map/pallas_call | solution.py:384
  3.8 4.0 %collective-permute-start.2 = (bf16[512,128]{1,0:T(8,128)(2,1)S(1)}, bf16[512,128]{1,0:T(8,128)(2,1)S(1)}, u32[]{:S(2)}, u32[]{:S(2)}) collective-permute-start(bf16[512,128]{1,0:T(8,128)(2,1)S(1)} %get-tuple-element.34), channel_id=1, source_target_pairs={{0,12},{1,13},{2,15},{3,14},{4,8},{5,9},{6,11},{7,10},{8,4},{9,5},... | collective-permute-start | bytes 393224 | tf_op jit(solution)/shard_map/ppermute | solution.py:370
  7.8 0.5 %collective-permute-start.3 = (bf16[512,128]{1,0:T(8,128)(2,1)S(1)}, bf16[512,128]{1,0:T(8,128)(2,1)S(1)}, u32[]{:S(2)}, u32[]{:S(2)}) collective-permute-start(bf16[512,128]{1,0:T(8,128)(2,1)S(1)} %get-tuple-element.35), channel_id=1, source_target_pairs={{0,4},{1,5},{2,7},{3,6},{4,0},{5,1},{6,3},{7,2},{8,12},{9,13},{10,... | collective-permute-start | bytes 393224 | tf_op jit(solution)/shard_map/ppermute | solution.py:370
  8.4 0.1 collective-permute-start.4
  8.5 0.7 %collective-permute-start.5 = (bf16[512,128]{1,0:T(8,128)(2,1)S(1)}, bf16[512,128]{1,0:T(8,128)(2,1)S(1)}, u32[]{:S(2)}, u32[]{:S(2)}) collective-permute-start(bf16[512,128]{1,0:T(8,128)(2,1)S(1)} %get-tuple-element.37), channel_id=1, source_target_pairs={{0,0},{1,1},{2,3},{3,2},{4,4},{5,5},{6,7},{7,6},{8,8},{9,9},{10,11... | collective-permute-start | bytes 393224 | tf_op jit(solution)/shard_map/ppermute | solution.py:370
  9.1 0.0 copy-start
  9.2 1.5 %copy-done = bf16[28,128,256]{2,1,0:T(8,128)(2,1)S(1)} copy-done((bf16[28,128,256]{2,1,0:T(8,128)(2,1)S(1)}, bf16[28,128,256]{2,1,0:T(8,128)(2,1)}, u32[]{:S(2)}) %copy-start) | copy-done | bytes 1835032
  10.6 0.0 copy-start.1
  10.6 1.0 %shard_map.60 = (f32[64,256]{1,0:T(8,128)S(1)}, bf16[512,128]{1,0:T(8,128)(2,1)S(1)}) custom-call(bf16[640,128]{1,0:T(8,128)(2,1)S(1)} %get-tuple-element.32.own_ref, bf16[28,128,256]{2,1,0:T(8,128)(2,1)S(1)} %copy-done), custom_call_target="tpu_custom_call" | custom-call | bytes 1048576 | tf_op jit(solution)/shard_map/pallas_call | solution.py:397
  11.6 0.2 collective-permute-done.2.refs_0_
  11.8 3.1 %collective-permute-done.3.refs_1_ = bf16[512,128]{1,0:T(8,128)(2,1)S(1)} collective-permute-done((bf16[512,128]{1,0:T(8,128)(2,1)S(1)}, bf16[512,128]{1,0:T(8,128)(2,1)S(1)}, u32[]{:S(2)}, u32[]{:S(2)}) %collective-permute-start.3) | collective-permute-done | bytes 131104 | tf_op jit(solution)/shard_map/ppermute | solution.py:370
  15.0 0.4 collective-permute-done.4.refs_2_
  15.4 0.0 collective-permute-done.5.refs_3_
  15.4 0.7 %shard_map.61 = (f32[14,32,128]{2,1,0:T(8,128)S(1)}, bf16[14,32,128]{2,1,0:T(8,128)(2,1)S(1)}) custom-call(bf16[512,128]{1,0:T(8,128)(2,1)S(1)} %collective-permute-done.2.refs_0_, bf16[512,128]{1,0:T(8,128)(2,1)S(1)} %collective-permute-done.3.refs_1_, bf16[512,128]{1,0:T(8,128)(2,1)S(1)} %collective-permute-done.4.refs_2_, ...), custom_call_target="tpu_custom_call" | custom-call | bytes 1048576 | tf_op jit(solution)/shard_map/pallas_call | solution.py:416
  16.2 1.1 %collective-permute-start.6 = (bf16[14,32,128]{2,1,0:T(8,128)(2,1)S(1)}, bf16[14,32,128]{2,1,0:T(8,128)(2,1)S(1)}, u32[]{:S(2)}, u32[]{:S(2)}) collective-permute-start(bf16[14,32,128]{2,1,0:T(8,128)(2,1)S(1)} %get-tuple-element.45), channel_id=1, source_target_pairs={{0,2},{2,0},{4,6},{6,4},{8,10},{10,8},{12,14},{14,12},{16,18},{18,... | collective-permute-start | bytes 344072 | tf_op jit(solution)/shard_map/ppermute | solution.py:360
  17.2 1.5 %collective-permute-start.9 = (bf16[640,128]{1,0:T(8,128)(2,1)S(1)}, bf16[640,128]{1,0:T(8,128)(2,1)S(1)}, u32[]{:S(2)}, u32[]{:S(2)}) collective-permute-start(bf16[640,128]{1,0:T(8,128)(2,1)S(1)} %get-tuple-element.54.send_ref), channel_id=1, source_target_pairs={{0,1},{1,0},{2,3},{3,2},{4,5},{5,4},{6,7},{7,6},{8,9},{9,8},{10,11... | collective-permute-start | bytes 491528 | tf_op jit(solution)/shard_map/ppermute | solution.py:363
  18.7 0.0 collective-permute-done.6
  18.8 0.6 %shard_map.62 = (f32[14,32,128]{2,1,0:T(8,128)S(1)}, bf16[14,32,128]{2,1,0:T(8,128)(2,1)S(1)}) custom-call(bf16[512,128]{1,0:T(8,128)(2,1)S(1)} %collective-permute-done.2.refs_0_, bf16[512,128]{1,0:T(8,128)(2,1)S(1)} %collective-permute-done.3.refs_1_, bf16[512,128]{1,0:T(8,128)(2,1)S(1)} %collective-permute-done.4.refs_2_, ...), custom_call_target="tpu_custom_call" | custom-call | bytes 1048576 | tf_op jit(solution)/shard_map/pallas_call | solution.py:416
  19.4 0.1 collective-permute-start.7
  19.4 2.9 %collective-permute-start.11 = (bf16[14,32,128]{2,1,0:T(8,128)(2,1)S(1)}, bf16[14,32,128]{2,1,0:T(8,128)(2,1)S(1)}, u32[]{:S(2)}, u32[]{:S(2)}) collective-permute-start(bf16[14,32,128]{2,1,0:T(8,128)(2,1)S(1)} %add_convert_fusion.3), channel_id=1, source_target_pairs={{0,16},{2,18},{4,20},{6,22},{8,24},{10,26},{12,28},{14,30},{16,0},... | collective-permute-start | bytes 344072 | tf_op jit(solution)/shard_map/ppermute | solution.py:360
  22.3 1.1 %collective-permute-done.9.own_ref = bf16[640,128]{1,0:T(8,128)(2,1)S(1)} collective-permute-done((bf16[640,128]{1,0:T(8,128)(2,1)S(1)}, bf16[640,128]{1,0:T(8,128)(2,1)S(1)}, u32[]{:S(2)}, u32[]{:S(2)}) %collective-permute-start.9) | collective-permute-done | bytes 163872 | tf_op jit(solution)/shard_map/ppermute | solution.py:363
  23.4 0.0 copy-done.1
  23.4 1.0 %shard_map.63 = bf16[640,128]{1,0:T(8,128)(2,1)S(1)} custom-call(bf16[640,128]{1,0:T(8,128)(2,1)S(1)} %collective-permute-done.9.own_ref, bf16[28,128,256]{2,1,0:T(8,128)(2,1)S(1)} %copy-done.1), custom_call_target="tpu_custom_call" | custom-call | bytes 1048576 | tf_op jit(solution)/shard_map/pallas_call | solution.py:403
  24.4 1.6 %collective-permute-start.10 = (bf16[640,128]{1,0:T(8,128)(2,1)S(1)}, bf16[640,128]{1,0:T(8,128)(2,1)S(1)}, u32[]{:S(2)}, u32[]{:S(2)}) collective-permute-start(bf16[640,128]{1,0:T(8,128)(2,1)S(1)} %shard_map.63), channel_id=1, source_target_pairs={{0,1},{1,0},{2,3},{3,2},{4,5},{5,4},{6,7},{7,6},{8,9},{9,8},{10,11... | collective-permute-start | bytes 491528 | tf_op jit(solution)/shard_map/ppermute | solution.py:363
  25.9 0.0 collective-permute-done.7
  26.0 2.9 %collective-permute-start.8 = (bf16[14,32,128]{2,1,0:T(8,128)(2,1)S(1)}, bf16[14,32,128]{2,1,0:T(8,128)(2,1)S(1)}, u32[]{:S(2)}, u32[]{:S(2)}) collective-permute-start(bf16[14,32,128]{2,1,0:T(8,128)(2,1)S(1)} %add_convert_fusion.2), channel_id=1, source_target_pairs={{0,16},{2,18},{4,20},{6,22},{8,24},{10,26},{12,28},{14,30},{16,0},... | collective-permute-start | bytes 344072 | tf_op jit(solution)/shard_map/ppermute | solution.py:360
  28.9 0.0 collective-permute-done.11
  28.9 1.4 %collective-permute-start.14 = (bf16[14,32,128]{2,1,0:T(8,128)(2,1)S(1)}, bf16[14,32,128]{2,1,0:T(8,128)(2,1)S(1)}, u32[]{:S(2)}, u32[]{:S(2)}) collective-permute-start(bf16[14,32,128]{2,1,0:T(8,128)(2,1)S(1)} %add_convert_fusion.1.refs_0_), channel_id=1, source_target_pairs={{0,4},{2,6},{4,0},{6,2},{8,12},{10,14},{12,8},{14,10},{16,20},{18,... | collective-permute-start | bytes 344072 | tf_op jit(solution)/shard_map/ppermute | solution.py:360
  30.3 0.8 %collective-permute-start.13 = (bf16[14,32,128]{2,1,0:T(8,128)(2,1)S(1)}, bf16[14,32,128]{2,1,0:T(8,128)(2,1)S(1)}, u32[]{:S(2)}, u32[]{:S(2)}) collective-permute-start(bf16[14,32,128]{2,1,0:T(8,128)(2,1)S(1)} %add_convert_fusion.1.refs_0_), channel_id=1, source_target_pairs={{0,8},{2,10},{4,12},{6,14},{8,0},{10,2},{12,4},{14,6},{16,24},{18,... | collective-permute-start | bytes 344072 | tf_op jit(solution)/shard_map/ppermute | solution.py:360
  31.1 1.4 %collective-permute-start.12 = (bf16[14,32,128]{2,1,0:T(8,128)(2,1)S(1)}, bf16[14,32,128]{2,1,0:T(8,128)(2,1)S(1)}, u32[]{:S(2)}, u32[]{:S(2)}) collective-permute-start(bf16[14,32,128]{2,1,0:T(8,128)(2,1)S(1)} %add_convert_fusion.1.refs_0_), channel_id=1, source_target_pairs={{0,12},{2,14},{4,8},{6,10},{8,4},{10,6},{12,0},{14,2},{16,28},{18,... | collective-permute-start | bytes 344072 | tf_op jit(solution)/shard_map/ppermute | solution.py:360
  32.4 0.0 collective-permute-done.10.got_ref
  32.5 1.1 %shard_map.64 = (bf16[4,4,4,256]{3,2,1,0:T(4,128)(2,1)}, bf16[512,256]{1,0:T(8,128)(2,1)}) custom-call(f32[64,256]{1,0:T(8,128)S(1)} %get-tuple-element.52.part_ref, bf16[512,128]{1,0:T(8,128)(2,1)S(1)} %get-tuple-element.53.grad_ref, bf16[640,128]{1,0:T(8,128)(2,1)S(1)} %collective-permute-done.10.got_ref), custom_call_target="tpu_custom_call" | custom-call | bytes 1048576 | tf_op jit(solution)/shard_map/pallas_call | solution.py:431
  33.6 0.1 collective-permute-done.8
  33.7 1.4 %collective-permute-start.17 = (bf16[14,32,128]{2,1,0:T(8,128)(2,1)S(1)}, bf16[14,32,128]{2,1,0:T(8,128)(2,1)S(1)}, u32[]{:S(2)}, u32[]{:S(2)}) collective-permute-start(bf16[14,32,128]{2,1,0:T(8,128)(2,1)S(1)} %add_convert_fusion.refs_4_), channel_id=1, source_target_pairs={{0,4},{2,6},{4,0},{6,2},{8,12},{10,14},{12,8},{14,10},{16,20},{18,... | collective-permute-start | bytes 344072 | tf_op jit(solution)/shard_map/ppermute | solution.py:360
  35.2 0.6 %collective-permute-start.16 = (bf16[14,32,128]{2,1,0:T(8,128)(2,1)S(1)}, bf16[14,32,128]{2,1,0:T(8,128)(2,1)S(1)}, u32[]{:S(2)}, u32[]{:S(2)}) collective-permute-start(bf16[14,32,128]{2,1,0:T(8,128)(2,1)S(1)} %add_convert_fusion.refs_4_), channel_id=1, source_target_pairs={{0,8},{2,10},{4,12},{6,14},{8,0},{10,2},{12,4},{14,6},{16,24},{18,... | collective-permute-start | bytes 344072 | tf_op jit(solution)/shard_map/ppermute | solution.py:360
  35.8 0.0 collective-permute-done.14.refs_3_
  35.8 1.5 %collective-permute-start.15 = (bf16[14,32,128]{2,1,0:T(8,128)(2,1)S(1)}, bf16[14,32,128]{2,1,0:T(8,128)(2,1)S(1)}, u32[]{:S(2)}, u32[]{:S(2)}) collective-permute-start(bf16[14,32,128]{2,1,0:T(8,128)(2,1)S(1)} %add_convert_fusion.refs_4_), channel_id=1, source_target_pairs={{0,12},{2,14},{4,8},{6,10},{8,4},{10,6},{12,0},{14,2},{16,28},{18,... | collective-permute-start | bytes 344072 | tf_op jit(solution)/shard_map/ppermute | solution.py:360
  37.3 0.0 collective-permute-done.13.refs_2_
  37.3 2.2 %collective-permute-done.12.refs_1_ = bf16[14,32,128]{2,1,0:T(8,128)(2,1)S(1)} collective-permute-done((bf16[14,32,128]{2,1,0:T(8,128)(2,1)S(1)}, bf16[14,32,128]{2,1,0:T(8,128)(2,1)S(1)}, u32[]{:S(2)}, u32[]{:S(2)}) %collective-permute-start.12) | collective-permute-done | bytes 114720 | tf_op jit(solution)/shard_map/ppermute | solution.py:360
  39.5 0.1 pad_maximum_fusion
  39.5 0.1 collective-permute-start.18
  39.6 0.5 %collective-permute-done.17.refs_7_ = bf16[14,32,128]{2,1,0:T(8,128)(2,1)S(1)} collective-permute-done((bf16[14,32,128]{2,1,0:T(8,128)(2,1)S(1)}, bf16[14,32,128]{2,1,0:T(8,128)(2,1)S(1)}, u32[]{:S(2)}, u32[]{:S(2)}) %collective-permute-start.17) | collective-permute-done | bytes 114720 | tf_op jit(solution)/shard_map/ppermute | solution.py:360
  40.1 1.1 %collective-permute-done.16.refs_6_ = bf16[14,32,128]{2,1,0:T(8,128)(2,1)S(1)} collective-permute-done((bf16[14,32,128]{2,1,0:T(8,128)(2,1)S(1)}, bf16[14,32,128]{2,1,0:T(8,128)(2,1)S(1)}, u32[]{:S(2)}, u32[]{:S(2)}) %collective-permute-start.16) | collective-permute-done | bytes 114720 | tf_op jit(solution)/shard_map/ppermute | solution.py:360
  41.1 2.1 %collective-permute-done.15.refs_5_ = bf16[14,32,128]{2,1,0:T(8,128)(2,1)S(1)} collective-permute-done((bf16[14,32,128]{2,1,0:T(8,128)(2,1)S(1)}, bf16[14,32,128]{2,1,0:T(8,128)(2,1)S(1)}, u32[]{:S(2)}, u32[]{:S(2)}) %collective-permute-start.15) | collective-permute-done | bytes 114720 | tf_op jit(solution)/shard_map/ppermute | solution.py:360
  43.2 0.1 pad_maximum_fusion.1
  43.3 0.1 collective-permute-start.19
  43.4 1.3 %shard_map.65.refs_0_ = f32[28,128,256]{2,1,0:T(8,128)} custom-call(bf16[14,32,128]{2,1,0:T(8,128)(2,1)S(1)} %add_convert_fusion.1.refs_0_, bf16[14,32,128]{2,1,0:T(8,128)(2,1)S(1)} %collective-permute-done.12.refs_1_, bf16[14,32,128]{2,1,0:T(8,128)(2,1)S(1)} %collective-permute-done.13.refs_2_, bf16[14,32,128]{2,1,0:T(8,128)(2,1)S(1)} %collective-permute-done.14.refs_3_, ...), custom_call_target="tpu_custom_call" | custom-call | tf_op jit(solution)/shard_map/pallas_call | solution.py:461
  44.7 0.0 collective-permute-done.18.refs_1_
  44.7 0.5 %collective-permute-done.19.refs_2_ = bf16[56,32,128]{2,1,0:T(8,128)(2,1)S(1)} collective-permute-done((bf16[56,32,128]{2,1,0:T(8,128)(2,1)S(1)}, bf16[56,32,128]{2,1,0:T(8,128)(2,1)S(1)}, u32[]{:S(2)}, u32[]{:S(2)}) %collective-permute-start.19) | collective-permute-done | bytes 458784 | tf_op jit(solution)/shard_map/ppermute | solution.py:360
  45.2 1.3 %shard_map.66 = f32[28,128,256]{2,1,0:T(8,128)} custom-call(f32[28,128,256]{2,1,0:T(8,128)} %shard_map.65.refs_0_, bf16[56,32,128]{2,1,0:T(8,128)(2,1)S(1)} %collective-permute-done.18.refs_1_, bf16[56,32,128]{2,1,0:T(8,128)(2,1)S(1)} %collective-permute-done.19.refs_2_), custom_call_target="tpu_custom_call", output_to_operand_aliasing={{}: (0, {})} | custom-call | tf_op jit(solution)/shard_map/pallas_call | solution.py:461
  (4 shorter events, 0.1 us)
Async XLA Ops:
  0.6 2.7 %collective-permute-start = (bf16[512,256]{1,0:T(8,128)(2,1)}, bf16[512,256]{1,0:T(8,128)(2,1)S(1)}, u32[]{:S(2)}, u32[]{:S(2)}) collective-permute-start(bf16[512,256]{1,0:T(8,128)(2,1)} %bitcast.4), channel_id=1, source_target_pairs={{0,2},{2,0},{4,6},{6,4},{8,10},{10,8},{12,14},{14,12},{16,18},{18,... | collective-permute-start | bytes 786440 | tf_op jit(solution)/shard_map/ppermute | solution.py:360
  1.1 2.2 %collective-permute-start.1 = (bf16[4,4,4,256]{3,2,1,0:T(4,128)(2,1)}, bf16[4,4,4,256]{3,2,1,0:T(4,128)(2,1)S(1)}, u32[]{:S(2)}, u32[]{:S(2)}) collective-permute-start(bf16[4,4,4,256]{3,2,1,0:T(4,128)(2,1)} %bitcast.6), channel_id=1, source_target_pairs={{0,2},{2,0},{4,6},{6,4},{8,10},{10,8},{12,14},{14,12},{16,18},{18,... | collective-permute-start | bytes 98312 | tf_op jit(solution)/shard_map/ppermute | solution.py:360
  1.2 0.9 %copy-start.2 = (bf16[1,8,8,8,256]{4,3,2,1,0:T(8,128)(2,1)S(1)}, bf16[1,8,8,8,256]{4,3,2,1,0:T(8,128)(2,1)}, u32[]{:S(2)}) copy-start(bf16[1,8,8,8,256]{4,3,2,1,0:T(8,128)(2,1)} %param.3) | copy-start | bytes 786436
  2.2 0.8 %copy-start.3 = (bf16[1,4,4,4,256]{4,3,2,1,0:T(4,128)(2,1)S(1)}, bf16[1,4,4,4,256]{4,3,2,1,0:T(4,128)(2,1)}, u32[]{:S(2)}) copy-start(bf16[1,4,4,4,256]{4,3,2,1,0:T(4,128)(2,1)} %param.4) | copy-start | bytes 98308
  3.8 8.0 %collective-permute-start.2 = (bf16[512,128]{1,0:T(8,128)(2,1)S(1)}, bf16[512,128]{1,0:T(8,128)(2,1)S(1)}, u32[]{:S(2)}, u32[]{:S(2)}) collective-permute-start(bf16[512,128]{1,0:T(8,128)(2,1)S(1)} %get-tuple-element.34), channel_id=1, source_target_pairs={{0,12},{1,13},{2,15},{3,14},{4,8},{5,9},{6,11},{7,10},{8,4},{9,5},... | collective-permute-start | bytes 393224 | tf_op jit(solution)/shard_map/ppermute | solution.py:370
  7.8 7.2 %collective-permute-start.3 = (bf16[512,128]{1,0:T(8,128)(2,1)S(1)}, bf16[512,128]{1,0:T(8,128)(2,1)S(1)}, u32[]{:S(2)}, u32[]{:S(2)}) collective-permute-start(bf16[512,128]{1,0:T(8,128)(2,1)S(1)} %get-tuple-element.35), channel_id=1, source_target_pairs={{0,4},{1,5},{2,7},{3,6},{4,0},{5,1},{6,3},{7,2},{8,12},{9,13},{10,... | collective-permute-start | bytes 393224 | tf_op jit(solution)/shard_map/ppermute | solution.py:370
  8.4 7.1 %collective-permute-start.4 = (bf16[512,128]{1,0:T(8,128)(2,1)S(1)}, bf16[512,128]{1,0:T(8,128)(2,1)S(1)}, u32[]{:S(2)}, u32[]{:S(2)}) collective-permute-start(bf16[512,128]{1,0:T(8,128)(2,1)S(1)} %get-tuple-element.36), channel_id=1, source_target_pairs={{0,8},{1,9},{2,11},{3,10},{4,12},{5,13},{6,15},{7,14},{8,0},{9,1},... | collective-permute-start | bytes 393224 | tf_op jit(solution)/shard_map/ppermute | solution.py:370
  8.5 7.0 %collective-permute-start.5 = (bf16[512,128]{1,0:T(8,128)(2,1)S(1)}, bf16[512,128]{1,0:T(8,128)(2,1)S(1)}, u32[]{:S(2)}, u32[]{:S(2)}) collective-permute-start(bf16[512,128]{1,0:T(8,128)(2,1)S(1)} %get-tuple-element.37), channel_id=1, source_target_pairs={{0,0},{1,1},{2,3},{3,2},{4,4},{5,5},{6,7},{7,6},{8,8},{9,9},{10,11... | collective-permute-start | bytes 393224 | tf_op jit(solution)/shard_map/ppermute | solution.py:370
  9.1 1.5 %copy-start = (bf16[28,128,256]{2,1,0:T(8,128)(2,1)S(1)}, bf16[28,128,256]{2,1,0:T(8,128)(2,1)}, u32[]{:S(2)}) copy-start(bf16[28,128,256]{2,1,0:T(8,128)(2,1)} %w_ref.3) | copy-start | bytes 5505028
  10.6 12.8 %copy-start.1 = (bf16[28,128,256]{2,1,0:T(8,128)(2,1)S(1)}, bf16[28,128,256]{2,1,0:T(8,128)(2,1)}, u32[]{:S(2)}) copy-start(bf16[28,128,256]{2,1,0:T(8,128)(2,1)} %w_ref.3) | copy-start | bytes 5505028
  16.2 2.6 %collective-permute-start.6 = (bf16[14,32,128]{2,1,0:T(8,128)(2,1)S(1)}, bf16[14,32,128]{2,1,0:T(8,128)(2,1)S(1)}, u32[]{:S(2)}, u32[]{:S(2)}) collective-permute-start(bf16[14,32,128]{2,1,0:T(8,128)(2,1)S(1)} %get-tuple-element.45), channel_id=1, source_target_pairs={{0,2},{2,0},{4,6},{6,4},{8,10},{10,8},{12,14},{14,12},{16,18},{18,... | collective-permute-start | bytes 344072 | tf_op jit(solution)/shard_map/ppermute | solution.py:360
  17.2 6.2 %collective-permute-start.9 = (bf16[640,128]{1,0:T(8,128)(2,1)S(1)}, bf16[640,128]{1,0:T(8,128)(2,1)S(1)}, u32[]{:S(2)}, u32[]{:S(2)}) collective-permute-start(bf16[640,128]{1,0:T(8,128)(2,1)S(1)} %get-tuple-element.54.send_ref), channel_id=1, source_target_pairs={{0,1},{1,0},{2,3},{3,2},{4,5},{5,4},{6,7},{7,6},{8,9},{9,8},{10,11... | collective-permute-start | bytes 491528 | tf_op jit(solution)/shard_map/ppermute | solution.py:363
  19.4 6.6 %collective-permute-start.7 = (bf16[14,32,128]{2,1,0:T(8,128)(2,1)S(1)}, bf16[14,32,128]{2,1,0:T(8,128)(2,1)S(1)}, u32[]{:S(2)}, u32[]{:S(2)}) collective-permute-start(bf16[14,32,128]{2,1,0:T(8,128)(2,1)S(1)} %get-tuple-element.51), channel_id=1, source_target_pairs={{0,2},{2,0},{4,6},{6,4},{8,10},{10,8},{12,14},{14,12},{16,18},{18,... | collective-permute-start | bytes 344072 | tf_op jit(solution)/shard_map/ppermute | solution.py:360
  19.4 9.4 %collective-permute-start.11 = (bf16[14,32,128]{2,1,0:T(8,128)(2,1)S(1)}, bf16[14,32,128]{2,1,0:T(8,128)(2,1)S(1)}, u32[]{:S(2)}, u32[]{:S(2)}) collective-permute-start(bf16[14,32,128]{2,1,0:T(8,128)(2,1)S(1)} %add_convert_fusion.3), channel_id=1, source_target_pairs={{0,16},{2,18},{4,20},{6,22},{8,24},{10,26},{12,28},{14,30},{16,0},... | collective-permute-start | bytes 344072 | tf_op jit(solution)/shard_map/ppermute | solution.py:360
  24.4 8.1 %collective-permute-start.10 = (bf16[640,128]{1,0:T(8,128)(2,1)S(1)}, bf16[640,128]{1,0:T(8,128)(2,1)S(1)}, u32[]{:S(2)}, u32[]{:S(2)}) collective-permute-start(bf16[640,128]{1,0:T(8,128)(2,1)S(1)} %shard_map.63), channel_id=1, source_target_pairs={{0,1},{1,0},{2,3},{3,2},{4,5},{5,4},{6,7},{7,6},{8,9},{9,8},{10,11... | collective-permute-start | bytes 491528 | tf_op jit(solution)/shard_map/ppermute | solution.py:363
  26.0 7.7 %collective-permute-start.8 = (bf16[14,32,128]{2,1,0:T(8,128)(2,1)S(1)}, bf16[14,32,128]{2,1,0:T(8,128)(2,1)S(1)}, u32[]{:S(2)}, u32[]{:S(2)}) collective-permute-start(bf16[14,32,128]{2,1,0:T(8,128)(2,1)S(1)} %add_convert_fusion.2), channel_id=1, source_target_pairs={{0,16},{2,18},{4,20},{6,22},{8,24},{10,26},{12,28},{14,30},{16,0},... | collective-permute-start | bytes 344072 | tf_op jit(solution)/shard_map/ppermute | solution.py:360
  28.9 6.9 %collective-permute-start.14 = (bf16[14,32,128]{2,1,0:T(8,128)(2,1)S(1)}, bf16[14,32,128]{2,1,0:T(8,128)(2,1)S(1)}, u32[]{:S(2)}, u32[]{:S(2)}) collective-permute-start(bf16[14,32,128]{2,1,0:T(8,128)(2,1)S(1)} %add_convert_fusion.1.refs_0_), channel_id=1, source_target_pairs={{0,4},{2,6},{4,0},{6,2},{8,12},{10,14},{12,8},{14,10},{16,20},{18,... | collective-permute-start | bytes 344072 | tf_op jit(solution)/shard_map/ppermute | solution.py:360
  30.3 7.0 %collective-permute-start.13 = (bf16[14,32,128]{2,1,0:T(8,128)(2,1)S(1)}, bf16[14,32,128]{2,1,0:T(8,128)(2,1)S(1)}, u32[]{:S(2)}, u32[]{:S(2)}) collective-permute-start(bf16[14,32,128]{2,1,0:T(8,128)(2,1)S(1)} %add_convert_fusion.1.refs_0_), channel_id=1, source_target_pairs={{0,8},{2,10},{4,12},{6,14},{8,0},{10,2},{12,4},{14,6},{16,24},{18,... | collective-permute-start | bytes 344072 | tf_op jit(solution)/shard_map/ppermute | solution.py:360
  31.1 8.4 %collective-permute-start.12 = (bf16[14,32,128]{2,1,0:T(8,128)(2,1)S(1)}, bf16[14,32,128]{2,1,0:T(8,128)(2,1)S(1)}, u32[]{:S(2)}, u32[]{:S(2)}) collective-permute-start(bf16[14,32,128]{2,1,0:T(8,128)(2,1)S(1)} %add_convert_fusion.1.refs_0_), channel_id=1, source_target_pairs={{0,12},{2,14},{4,8},{6,10},{8,4},{10,6},{12,0},{14,2},{16,28},{18,... | collective-permute-start | bytes 344072 | tf_op jit(solution)/shard_map/ppermute | solution.py:360
  33.7 6.4 %collective-permute-start.17 = (bf16[14,32,128]{2,1,0:T(8,128)(2,1)S(1)}, bf16[14,32,128]{2,1,0:T(8,128)(2,1)S(1)}, u32[]{:S(2)}, u32[]{:S(2)}) collective-permute-start(bf16[14,32,128]{2,1,0:T(8,128)(2,1)S(1)} %add_convert_fusion.refs_4_), channel_id=1, source_target_pairs={{0,4},{2,6},{4,0},{6,2},{8,12},{10,14},{12,8},{14,10},{16,20},{18,... | collective-permute-start | bytes 344072 | tf_op jit(solution)/shard_map/ppermute | solution.py:360
  35.2 6.0 %collective-permute-start.16 = (bf16[14,32,128]{2,1,0:T(8,128)(2,1)S(1)}, bf16[14,32,128]{2,1,0:T(8,128)(2,1)S(1)}, u32[]{:S(2)}, u32[]{:S(2)}) collective-permute-start(bf16[14,32,128]{2,1,0:T(8,128)(2,1)S(1)} %add_convert_fusion.refs_4_), channel_id=1, source_target_pairs={{0,8},{2,10},{4,12},{6,14},{8,0},{10,2},{12,4},{14,6},{16,24},{18,... | collective-permute-start | bytes 344072 | tf_op jit(solution)/shard_map/ppermute | solution.py:360
  35.8 7.5 %collective-permute-start.15 = (bf16[14,32,128]{2,1,0:T(8,128)(2,1)S(1)}, bf16[14,32,128]{2,1,0:T(8,128)(2,1)S(1)}, u32[]{:S(2)}, u32[]{:S(2)}) collective-permute-start(bf16[14,32,128]{2,1,0:T(8,128)(2,1)S(1)} %add_convert_fusion.refs_4_), channel_id=1, source_target_pairs={{0,12},{2,14},{4,8},{6,10},{8,4},{10,6},{12,0},{14,2},{16,28},{18,... | collective-permute-start | bytes 344072 | tf_op jit(solution)/shard_map/ppermute | solution.py:360
  39.5 5.2 %collective-permute-start.18 = (bf16[56,32,128]{2,1,0:T(8,128)(2,1)S(1)}, bf16[56,32,128]{2,1,0:T(8,128)(2,1)S(1)}, u32[]{:S(2)}, u32[]{:S(2)}) collective-permute-start(bf16[56,32,128]{2,1,0:T(8,128)(2,1)S(1)} %pad_maximum_fusion), channel_id=1, source_target_pairs={{0,2},{2,0},{4,6},{6,4},{8,10},{10,8},{12,14},{14,12},{16,18},{18,... | collective-permute-start | bytes 1376264 | tf_op jit(solution)/shard_map/ppermute | solution.py:360
  43.3 1.9 %collective-permute-start.19 = (bf16[56,32,128]{2,1,0:T(8,128)(2,1)S(1)}, bf16[56,32,128]{2,1,0:T(8,128)(2,1)S(1)}, u32[]{:S(2)}, u32[]{:S(2)}) collective-permute-start(bf16[56,32,128]{2,1,0:T(8,128)(2,1)S(1)} %pad_maximum_fusion.1), channel_id=1, source_target_pairs={{0,2},{2,0},{4,6},{6,4},{8,10},{10,8},{12,14},{14,12},{16,18},{18,... | collective-permute-start | bytes 1376264 | tf_op jit(solution)/shard_map/ppermute | solution.py:360

commit v3 on v2

--- a/solution.py
+++ b/solution.py
@@ -10,7 +10,7 @@
 LANES = 128
 PARTS = 8
 DELIVERY = (3, 1, 2, 0)
-GATHER = (6, 4, 2)
+GATHER = (2, 4, 6)
 SPLITS = (14, 14)
 BLOCK = 7
 ORDER = (0, 1)
@@ -20,7 +20,9 @@
 BACK = 4
 FINISH = 1
 DELAY = 0
-PLACE = 0
+PLACE = 3
+RELAY = False
+LATE_OTHER = 9
 VMEM_BYTES = 48 * 1024 * 1024
 BF16 = jnp.bfloat16
 F32 = jnp.float32
@@ -394,6 +396,8 @@
         send = after(send, *got)
     other = swap(send)
 
+    if LATE_OTHER == 0:
+        other, got[0] = lax.optimization_barrier((other, got[0]))
     part, grad = vmem_call(
         functools.partial(sample_kernel, half, False),
         (shape((cells, chans), F32), shape((8 * cells, LANES))),
@@ -451,7 +455,12 @@
         held.append(total)
     direct, crossed = [None] * len(splits), [None] * len(splits)
     for index, total in zip(ORDER, held):
-        direct[index] = [total] + [across(total, distance) for distance in GATHER]
+        if RELAY and index == ORDER[0]:
+            behind, beside = across(total, 4), across(total, 2)
+            found = {4: behind, 2: beside, 6: across(behind, 2)}
+            direct[index] = [total] + [found[distance] for distance in GATHER]
+        else:
+            direct[index] = [total] + [across(total, distance) for distance in GATHER]
     for index in ORDER:
         crossed[index] = across(jnp.concatenate(direct[index], axis=0), 1)
     base = None
@@ -489,7 +498,11 @@
                 at += 1 if kind else 1 + len(GATHER)
         return runs
 
-    if PLACE == 0:
+    if PLACE == 3:
+        early, late = ORDER[0], ORDER[1]
+        base = put(None, direct[early] + [crossed[early]] + direct[late], runs_of([early, late], [(0, 1), (0,)]))
+        base = put(base, [crossed[late]], runs_of([late], [(1,)]))
+    elif PLACE == 0:
         base = put(None, sum(direct, []), runs_of(range(len(splits)), [(0,)] * len(splits)))
         base = put(base, crossed, runs_of(range(len(splits)), [(1,)] * len(splits)))
     else:

time: 46.8 us -> 45.5 us (0.972)
  waiting for transfers between devices: 11.4 us -> 9.92 us
    ppermute x14, waiting for transfers between devices: 6.43 us -> 4.98 us  [across(): lax.ppermute(value, 'dp', [(i, i ^ distance) for i in range(groups_of)])]
  transfers between devices with their start and end apart: 20 -> 20, of which waited for: 10 -> 11; matrix products, arithmetic and copies ran while one was open for 1% -> 1% of each run, Pallas kernels for 11% -> 12%
where the time goes in v3:
time: 45.5 us; the launch traced here: 45.2 us
  starting transfers between devices  23.2 us (51%)
  waiting for transfers between devices  9.92 us (22%)
  Pallas kernels  7.81 us (17%)
  local copies, waits for them, and re-layouts  3.21 us (7%)
  between operations  0.79 us (2%)
    ppermute x14, starting transfers between devices, across(): lax.ppermute(value, 'dp', [(i, i ^ distance) for i in range(groups_of)])  14.9 us
    ppermute x4, starting transfers between devices, deliver(): return lax.ppermute(value, ('dp', 'shard'), pairs)  5.29 us
    ppermute x14, waiting for transfers between devices, across(): lax.ppermute(value, 'dp', [(i, i ^ distance) for i in range(groups_of)])  4.98 us
    ppermute x4, waiting for transfers between devices, deliver(): return lax.ppermute(value, ('dp', 'shard'), pairs)  3.82 us
    unnamed x8, local copies, waits for them, and re-layouts  3.21 us
    ppermute x2, starting transfers between devices, swap(): return lax.ppermute(value, 'shard', [(0, 1), (1, 0)])  3.03 us
    pallas_call x2, Pallas kernels, put(): pl.pallas_call(functools.partial(place_kernel, parts, width, BLOCK, runs,...  2.62 us
    pallas_call x2, Pallas kernels, shards(): vmem_call(functools.partial(weight_kernel, half, groups, start, n), (shap...  1.31 us
  transfers between devices with their start and end apart: 20, of which 11 were waited for; matrix products, arithmetic and copies ran while one was open for 1% of the time, Pallas kernels for 12%

profile of v3, /device:TPU:0, one launch (start us, length us, event | category | flops | bytes accessed | tf_op | source)
XLA Modules:
  0.0 45.2 jit_solution(2903407063946339454)
XLA Ops:
  0.6 0.5 %collective-permute-start = (bf16[512,256]{1,0:T(8,128)(2,1)}, bf16[512,256]{1,0:T(8,128)(2,1)S(1)}, u32[]{:S(2)}, u32[]{:S(2)}) collective-permute-start(bf16[512,256]{1,0:T(8,128)(2,1)} %bitcast.4), channel_id=1, source_target_pairs={{0,2},{2,0},{4,6},{6,4},{8,10},{10,8},{12,14},{14,12},{16,18},{18,... | collective-permute-start | bytes 786440 | tf_op jit(solution)/shard_map/ppermute | solution.py:362
  1.1 0.1 collective-permute-start.1
  1.2 0.0 copy-start.2
  1.2 0.9 %copy-done.2 = bf16[1,8,8,8,256]{4,3,2,1,0:T(8,128)(2,1)S(1)} copy-done((bf16[1,8,8,8,256]{4,3,2,1,0:T(8,128)(2,1)S(1)}, bf16[1,8,8,8,256]{4,3,2,1,0:T(8,128)(2,1)}, u32[]{:S(2)}) %copy-start.2) | copy-done | bytes 262168
  2.2 0.0 copy-start.3
  2.2 0.8 %copy-done.3 = bf16[1,4,4,4,256]{4,3,2,1,0:T(4,128)(2,1)S(1)} copy-done((bf16[1,4,4,4,256]{4,3,2,1,0:T(4,128)(2,1)S(1)}, bf16[1,4,4,4,256]{4,3,2,1,0:T(4,128)(2,1)}, u32[]{:S(2)}) %copy-start.3) | copy-done | bytes 32792
  2.9 0.4 shard_map.58
  3.3 0.0 collective-permute-done.1.cot2_ref
  3.3 0.0 collective-permute-done.x2_ref
  3.3 0.5 %shard_map.59 = (bf16[512,128]{1,0:T(8,128)(2,1)S(1)}, bf16[512,128]{1,0:T(8,128)(2,1)S(1)}, bf16[512,128]{1,0:T(8,128)(2,1)S(1)}, bf16[512,128]{1,0:T(8,128)(2,1)S(1)}) custom-call(bf16[640,128]{1,0:T(8,128)(2,1)S(1)} %get-tuple-element.32.own_ref, bf16[640,128]{1,0:T(8,128)(2,1)S(1)} %get-tuple-element.54.send_ref, ...), custom_call_target="tpu_custom_call" | custom-call | bytes 1048576 | tf_op jit(solution)/shard_map/pallas_call | solution.py:386
  3.8 4.0 %collective-permute-start.2 = (bf16[512,128]{1,0:T(8,128)(2,1)S(1)}, bf16[512,128]{1,0:T(8,128)(2,1)S(1)}, u32[]{:S(2)}, u32[]{:S(2)}) collective-permute-start(bf16[512,128]{1,0:T(8,128)(2,1)S(1)} %get-tuple-element.34), channel_id=1, source_target_pairs={{0,12},{1,13},{2,15},{3,14},{4,8},{5,9},{6,11},{7,10},{8,4},{9,5},... | collective-permute-start | bytes 393224 | tf_op jit(solution)/shard_map/ppermute | solution.py:372
  7.8 0.5 %collective-permute-start.3 = (bf16[512,128]{1,0:T(8,128)(2,1)S(1)}, bf16[512,128]{1,0:T(8,128)(2,1)S(1)}, u32[]{:S(2)}, u32[]{:S(2)}) collective-permute-start(bf16[512,128]{1,0:T(8,128)(2,1)S(1)} %get-tuple-element.35), channel_id=1, source_target_pairs={{0,4},{1,5},{2,7},{3,6},{4,0},{5,1},{6,3},{7,2},{8,12},{9,13},{10,... | collective-permute-start | bytes 393224 | tf_op jit(solution)/shard_map/ppermute | solution.py:372
  8.4 0.1 collective-permute-start.4
  8.5 0.7 %collective-permute-start.5 = (bf16[512,128]{1,0:T(8,128)(2,1)S(1)}, bf16[512,128]{1,0:T(8,128)(2,1)S(1)}, u32[]{:S(2)}, u32[]{:S(2)}) collective-permute-start(bf16[512,128]{1,0:T(8,128)(2,1)S(1)} %get-tuple-element.37), channel_id=1, source_target_pairs={{0,0},{1,1},{2,3},{3,2},{4,4},{5,5},{6,7},{7,6},{8,8},{9,9},{10,11... | collective-permute-start | bytes 393224 | tf_op jit(solution)/shard_map/ppermute | solution.py:372
  9.1 0.0 copy-start
  9.2 1.5 %copy-done = bf16[28,128,256]{2,1,0:T(8,128)(2,1)S(1)} copy-done((bf16[28,128,256]{2,1,0:T(8,128)(2,1)S(1)}, bf16[28,128,256]{2,1,0:T(8,128)(2,1)}, u32[]{:S(2)}) %copy-start) | copy-done | bytes 1835032
  10.6 0.0 copy-start.1
  10.6 1.0 %shard_map.60 = (f32[64,256]{1,0:T(8,128)S(1)}, bf16[512,128]{1,0:T(8,128)(2,1)S(1)}) custom-call(bf16[640,128]{1,0:T(8,128)(2,1)S(1)} %get-tuple-element.32.own_ref, bf16[28,128,256]{2,1,0:T(8,128)(2,1)S(1)} %copy-done), custom_call_target="tpu_custom_call" | custom-call | bytes 1048576 | tf_op jit(solution)/shard_map/pallas_call | solution.py:401
  11.6 0.2 collective-permute-done.2.refs_0_
  11.8 3.1 %collective-permute-done.3.refs_1_ = bf16[512,128]{1,0:T(8,128)(2,1)S(1)} collective-permute-done((bf16[512,128]{1,0:T(8,128)(2,1)S(1)}, bf16[512,128]{1,0:T(8,128)(2,1)S(1)}, u32[]{:S(2)}, u32[]{:S(2)}) %collective-permute-start.3) | collective-permute-done | bytes 131104 | tf_op jit(solution)/shard_map/ppermute | solution.py:372
  15.0 0.4 collective-permute-done.4.refs_2_
  15.4 0.0 collective-permute-done.5.refs_3_
  15.4 0.7 %shard_map.61 = (f32[14,32,128]{2,1,0:T(8,128)S(1)}, bf16[14,32,128]{2,1,0:T(8,128)(2,1)S(1)}) custom-call(bf16[512,128]{1,0:T(8,128)(2,1)S(1)} %collective-permute-done.2.refs_0_, bf16[512,128]{1,0:T(8,128)(2,1)S(1)} %collective-permute-done.3.refs_1_, bf16[512,128]{1,0:T(8,128)(2,1)S(1)} %collective-permute-done.4.refs_2_, ...), custom_call_target="tpu_custom_call" | custom-call | bytes 1048576 | tf_op jit(solution)/shard_map/pallas_call | solution.py:420
  16.2 1.1 %collective-permute-start.6 = (bf16[14,32,128]{2,1,0:T(8,128)(2,1)S(1)}, bf16[14,32,128]{2,1,0:T(8,128)(2,1)S(1)}, u32[]{:S(2)}, u32[]{:S(2)}) collective-permute-start(bf16[14,32,128]{2,1,0:T(8,128)(2,1)S(1)} %get-tuple-element.45), channel_id=1, source_target_pairs={{0,2},{2,0},{4,6},{6,4},{8,10},{10,8},{12,14},{14,12},{16,18},{18,... | collective-permute-start | bytes 344072 | tf_op jit(solution)/shard_map/ppermute | solution.py:362
  17.2 1.5 %collective-permute-start.9 = (bf16[640,128]{1,0:T(8,128)(2,1)S(1)}, bf16[640,128]{1,0:T(8,128)(2,1)S(1)}, u32[]{:S(2)}, u32[]{:S(2)}) collective-permute-start(bf16[640,128]{1,0:T(8,128)(2,1)S(1)} %get-tuple-element.54.send_ref), channel_id=1, source_target_pairs={{0,1},{1,0},{2,3},{3,2},{4,5},{5,4},{6,7},{7,6},{8,9},{9,8},{10,11... | collective-permute-start | bytes 491528 | tf_op jit(solution)/shard_map/ppermute | solution.py:365
  18.7 0.0 collective-permute-done.6
  18.8 0.6 %shard_map.62 = (f32[14,32,128]{2,1,0:T(8,128)S(1)}, bf16[14,32,128]{2,1,0:T(8,128)(2,1)S(1)}) custom-call(bf16[512,128]{1,0:T(8,128)(2,1)S(1)} %collective-permute-done.2.refs_0_, bf16[512,128]{1,0:T(8,128)(2,1)S(1)} %collective-permute-done.3.refs_1_, bf16[512,128]{1,0:T(8,128)(2,1)S(1)} %collective-permute-done.4.refs_2_, ...), custom_call_target="tpu_custom_call" | custom-call | bytes 1048576 | tf_op jit(solution)/shard_map/pallas_call | solution.py:420
  19.4 0.1 collective-permute-start.7
  19.4 2.9 %collective-permute-start.11 = (bf16[14,32,128]{2,1,0:T(8,128)(2,1)S(1)}, bf16[14,32,128]{2,1,0:T(8,128)(2,1)S(1)}, u32[]{:S(2)}, u32[]{:S(2)}) collective-permute-start(bf16[14,32,128]{2,1,0:T(8,128)(2,1)S(1)} %add_convert_fusion.3), channel_id=1, source_target_pairs={{0,16},{2,18},{4,20},{6,22},{8,24},{10,26},{12,28},{14,30},{16,0},... | collective-permute-start | bytes 344072 | tf_op jit(solution)/shard_map/ppermute | solution.py:362
  22.3 1.1 %collective-permute-done.9.own_ref = bf16[640,128]{1,0:T(8,128)(2,1)S(1)} collective-permute-done((bf16[640,128]{1,0:T(8,128)(2,1)S(1)}, bf16[640,128]{1,0:T(8,128)(2,1)S(1)}, u32[]{:S(2)}, u32[]{:S(2)}) %collective-permute-start.9) | collective-permute-done | bytes 163872 | tf_op jit(solution)/shard_map/ppermute | solution.py:365
  23.4 0.0 copy-done.1
  23.4 1.0 %shard_map.63 = bf16[640,128]{1,0:T(8,128)(2,1)S(1)} custom-call(bf16[640,128]{1,0:T(8,128)(2,1)S(1)} %collective-permute-done.9.own_ref, bf16[28,128,256]{2,1,0:T(8,128)(2,1)S(1)} %copy-done.1), custom_call_target="tpu_custom_call" | custom-call | bytes 1048576 | tf_op jit(solution)/shard_map/pallas_call | solution.py:407
  24.4 1.6 %collective-permute-start.10 = (bf16[640,128]{1,0:T(8,128)(2,1)S(1)}, bf16[640,128]{1,0:T(8,128)(2,1)S(1)}, u32[]{:S(2)}, u32[]{:S(2)}) collective-permute-start(bf16[640,128]{1,0:T(8,128)(2,1)S(1)} %shard_map.63), channel_id=1, source_target_pairs={{0,1},{1,0},{2,3},{3,2},{4,5},{5,4},{6,7},{7,6},{8,9},{9,8},{10,11... | collective-permute-start | bytes 491528 | tf_op jit(solution)/shard_map/ppermute | solution.py:365
  25.9 0.0 collective-permute-done.7
  26.0 2.9 %collective-permute-start.8 = (bf16[14,32,128]{2,1,0:T(8,128)(2,1)S(1)}, bf16[14,32,128]{2,1,0:T(8,128)(2,1)S(1)}, u32[]{:S(2)}, u32[]{:S(2)}) collective-permute-start(bf16[14,32,128]{2,1,0:T(8,128)(2,1)S(1)} %add_convert_fusion.2), channel_id=1, source_target_pairs={{0,16},{2,18},{4,20},{6,22},{8,24},{10,26},{12,28},{14,30},{16,0},... | collective-permute-start | bytes 344072 | tf_op jit(solution)/shard_map/ppermute | solution.py:362
  28.9 0.0 collective-permute-done.11
  28.9 1.6 %collective-permute-start.14 = (bf16[14,32,128]{2,1,0:T(8,128)(2,1)S(1)}, bf16[14,32,128]{2,1,0:T(8,128)(2,1)S(1)}, u32[]{:S(2)}, u32[]{:S(2)}) collective-permute-start(bf16[14,32,128]{2,1,0:T(8,128)(2,1)S(1)} %add_convert_fusion.1.refs_0_), channel_id=1, source_target_pairs={{0,12},{2,14},{4,8},{6,10},{8,4},{10,6},{12,0},{14,2},{16,28},{18,... | collective-permute-start | bytes 344072 | tf_op jit(solution)/shard_map/ppermute | solution.py:362
  30.5 1.2 %collective-permute-start.13 = (bf16[14,32,128]{2,1,0:T(8,128)(2,1)S(1)}, bf16[14,32,128]{2,1,0:T(8,128)(2,1)S(1)}, u32[]{:S(2)}, u32[]{:S(2)}) collective-permute-start(bf16[14,32,128]{2,1,0:T(8,128)(2,1)S(1)} %add_convert_fusion.1.refs_0_), channel_id=1, source_target_pairs={{0,8},{2,10},{4,12},{6,14},{8,0},{10,2},{12,4},{14,6},{16,24},{18,... | collective-permute-start | bytes 344072 | tf_op jit(solution)/shard_map/ppermute | solution.py:362
  31.7 0.7 %collective-permute-start.12 = (bf16[14,32,128]{2,1,0:T(8,128)(2,1)S(1)}, bf16[14,32,128]{2,1,0:T(8,128)(2,1)S(1)}, u32[]{:S(2)}, u32[]{:S(2)}) collective-permute-start(bf16[14,32,128]{2,1,0:T(8,128)(2,1)S(1)} %add_convert_fusion.1.refs_0_), channel_id=1, source_target_pairs={{0,4},{2,6},{4,0},{6,2},{8,12},{10,14},{12,8},{14,10},{16,20},{18,... | collective-permute-start | bytes 344072 | tf_op jit(solution)/shard_map/ppermute | solution.py:362
  32.4 0.0 collective-permute-done.10.got_ref
  32.5 1.1 %shard_map.64 = (bf16[4,4,4,256]{3,2,1,0:T(4,128)(2,1)}, bf16[512,256]{1,0:T(8,128)(2,1)}) custom-call(f32[64,256]{1,0:T(8,128)S(1)} %get-tuple-element.52.part_ref, bf16[512,128]{1,0:T(8,128)(2,1)S(1)} %get-tuple-element.53.grad_ref, bf16[640,128]{1,0:T(8,128)(2,1)S(1)} %collective-permute-done.10.got_ref), custom_call_target="tpu_custom_call" | custom-call | bytes 1048576 | tf_op jit(solution)/shard_map/pallas_call | solution.py:435
  33.6 0.1 collective-permute-done.8
  33.7 1.5 %collective-permute-start.18 = (bf16[14,32,128]{2,1,0:T(8,128)(2,1)S(1)}, bf16[14,32,128]{2,1,0:T(8,128)(2,1)S(1)}, u32[]{:S(2)}, u32[]{:S(2)}) collective-permute-start(bf16[14,32,128]{2,1,0:T(8,128)(2,1)S(1)} %add_convert_fusion.refs_5_), channel_id=1, source_target_pairs={{0,12},{2,14},{4,8},{6,10},{8,4},{10,6},{12,0},{14,2},{16,28},{18,... | collective-permute-start | bytes 344072 | tf_op jit(solution)/shard_map/ppermute | solution.py:362
  35.2 1.4 %collective-permute-start.17 = (bf16[14,32,128]{2,1,0:T(8,128)(2,1)S(1)}, bf16[14,32,128]{2,1,0:T(8,128)(2,1)S(1)}, u32[]{:S(2)}, u32[]{:S(2)}) collective-permute-start(bf16[14,32,128]{2,1,0:T(8,128)(2,1)S(1)} %add_convert_fusion.refs_5_), channel_id=1, source_target_pairs={{0,8},{2,10},{4,12},{6,14},{8,0},{10,2},{12,4},{14,6},{16,24},{18,... | collective-permute-start | bytes 344072 | tf_op jit(solution)/shard_map/ppermute | solution.py:362
  36.6 0.2 collective-permute-done.14.refs_3_
  36.8 0.8 %collective-permute-start.16 = (bf16[14,32,128]{2,1,0:T(8,128)(2,1)S(1)}, bf16[14,32,128]{2,1,0:T(8,128)(2,1)S(1)}, u32[]{:S(2)}, u32[]{:S(2)}) collective-permute-start(bf16[14,32,128]{2,1,0:T(8,128)(2,1)S(1)} %add_convert_fusion.refs_5_), channel_id=1, source_target_pairs={{0,4},{2,6},{4,0},{6,2},{8,12},{10,14},{12,8},{14,10},{16,20},{18,... | collective-permute-start | bytes 344072 | tf_op jit(solution)/shard_map/ppermute | solution.py:362
  37.6 0.6 %collective-permute-done.13.refs_2_ = bf16[14,32,128]{2,1,0:T(8,128)(2,1)S(1)} collective-permute-done((bf16[14,32,128]{2,1,0:T(8,128)(2,1)S(1)}, bf16[14,32,128]{2,1,0:T(8,128)(2,1)S(1)}, u32[]{:S(2)}, u32[]{:S(2)}) %collective-permute-start.13) | collective-permute-done | bytes 114720 | tf_op jit(solution)/shard_map/ppermute | solution.py:362
  38.2 0.0 collective-permute-done.12.refs_1_
  38.2 0.1 pad_maximum_fusion
  38.3 0.1 collective-permute-start.15
  38.4 3.3 %collective-permute-done.18.refs_8_ = bf16[14,32,128]{2,1,0:T(8,128)(2,1)S(1)} collective-permute-done((bf16[14,32,128]{2,1,0:T(8,128)(2,1)S(1)}, bf16[14,32,128]{2,1,0:T(8,128)(2,1)S(1)}, u32[]{:S(2)}, u32[]{:S(2)}) %collective-permute-start.18) | collective-permute-done | bytes 114720 | tf_op jit(solution)/shard_map/ppermute | solution.py:362
  41.7 0.5 %collective-permute-done.17.refs_7_ = bf16[14,32,128]{2,1,0:T(8,128)(2,1)S(1)} collective-permute-done((bf16[14,32,128]{2,1,0:T(8,128)(2,1)S(1)}, bf16[14,32,128]{2,1,0:T(8,128)(2,1)S(1)}, u32[]{:S(2)}, u32[]{:S(2)}) %collective-permute-start.17) | collective-permute-done | bytes 114720 | tf_op jit(solution)/shard_map/ppermute | solution.py:362
  42.2 0.1 collective-permute-done.16.refs_6_
  42.3 0.1 pad_maximum_fusion.1
  42.3 0.1 collective-permute-start.19
  42.4 0.0 collective-permute-done.15.refs_4_
  42.4 1.6 %shard_map.65.refs_0_ = f32[28,128,256]{2,1,0:T(8,128)} custom-call(bf16[14,32,128]{2,1,0:T(8,128)(2,1)S(1)} %add_convert_fusion.1.refs_0_, bf16[14,32,128]{2,1,0:T(8,128)(2,1)S(1)} %collective-permute-done.12.refs_1_, bf16[14,32,128]{2,1,0:T(8,128)(2,1)S(1)} %collective-permute-done.13.refs_2_, bf16[14,32,128]{2,1,0:T(8,128)(2,1)S(1)} %collective-permute-done.14.refs_3_, ...), custom_call_target="tpu_custom_call" | custom-call | tf_op jit(solution)/shard_map/pallas_call | solution.py:470
  44.1 0.2 collective-permute-done.19.refs_1_
  44.2 1.0 %shard_map.66 = f32[28,128,256]{2,1,0:T(8,128)} custom-call(f32[28,128,256]{2,1,0:T(8,128)} %shard_map.65.refs_0_, bf16[56,32,128]{2,1,0:T(8,128)(2,1)S(1)} %collective-permute-done.19.refs_1_), custom_call_target="tpu_custom_call", output_to_operand_aliasing={{}: (0, {})} | custom-call | tf_op jit(solution)/shard_map/pallas_call | solution.py:470
  (4 shorter events, 0.1 us)
Async XLA Ops:
  0.6 2.7 %collective-permute-start = (bf16[512,256]{1,0:T(8,128)(2,1)}, bf16[512,256]{1,0:T(8,128)(2,1)S(1)}, u32[]{:S(2)}, u32[]{:S(2)}) collective-permute-start(bf16[512,256]{1,0:T(8,128)(2,1)} %bitcast.4), channel_id=1, source_target_pairs={{0,2},{2,0},{4,6},{6,4},{8,10},{10,8},{12,14},{14,12},{16,18},{18,... | collective-permute-start | bytes 786440 | tf_op jit(solution)/shard_map/ppermute | solution.py:362
  1.1 2.2 %collective-permute-start.1 = (bf16[4,4,4,256]{3,2,1,0:T(4,128)(2,1)}, bf16[4,4,4,256]{3,2,1,0:T(4,128)(2,1)S(1)}, u32[]{:S(2)}, u32[]{:S(2)}) collective-permute-start(bf16[4,4,4,256]{3,2,1,0:T(4,128)(2,1)} %bitcast.6), channel_id=1, source_target_pairs={{0,2},{2,0},{4,6},{6,4},{8,10},{10,8},{12,14},{14,12},{16,18},{18,... | collective-permute-start | bytes 98312 | tf_op jit(solution)/shard_map/ppermute | solution.py:362
  1.2 0.9 %copy-start.2 = (bf16[1,8,8,8,256]{4,3,2,1,0:T(8,128)(2,1)S(1)}, bf16[1,8,8,8,256]{4,3,2,1,0:T(8,128)(2,1)}, u32[]{:S(2)}) copy-start(bf16[1,8,8,8,256]{4,3,2,1,0:T(8,128)(2,1)} %param.3) | copy-start | bytes 786436
  2.2 0.8 %copy-start.3 = (bf16[1,4,4,4,256]{4,3,2,1,0:T(4,128)(2,1)S(1)}, bf16[1,4,4,4,256]{4,3,2,1,0:T(4,128)(2,1)}, u32[]{:S(2)}) copy-start(bf16[1,4,4,4,256]{4,3,2,1,0:T(4,128)(2,1)} %param.4) | copy-start | bytes 98308
  3.8 8.0 %collective-permute-start.2 = (bf16[512,128]{1,0:T(8,128)(2,1)S(1)}, bf16[512,128]{1,0:T(8,128)(2,1)S(1)}, u32[]{:S(2)}, u32[]{:S(2)}) collective-permute-start(bf16[512,128]{1,0:T(8,128)(2,1)S(1)} %get-tuple-element.34), channel_id=1, source_target_pairs={{0,12},{1,13},{2,15},{3,14},{4,8},{5,9},{6,11},{7,10},{8,4},{9,5},... | collective-permute-start | bytes 393224 | tf_op jit(solution)/shard_map/ppermute | solution.py:372
  7.8 7.2 %collective-permute-start.3 = (bf16[512,128]{1,0:T(8,128)(2,1)S(1)}, bf16[512,128]{1,0:T(8,128)(2,1)S(1)}, u32[]{:S(2)}, u32[]{:S(2)}) collective-permute-start(bf16[512,128]{1,0:T(8,128)(2,1)S(1)} %get-tuple-element.35), channel_id=1, source_target_pairs={{0,4},{1,5},{2,7},{3,6},{4,0},{5,1},{6,3},{7,2},{8,12},{9,13},{10,... | collective-permute-start | bytes 393224 | tf_op jit(solution)/shard_map/ppermute | solution.py:372
  8.4 7.1 %collective-permute-start.4 = (bf16[512,128]{1,0:T(8,128)(2,1)S(1)}, bf16[512,128]{1,0:T(8,128)(2,1)S(1)}, u32[]{:S(2)}, u32[]{:S(2)}) collective-permute-start(bf16[512,128]{1,0:T(8,128)(2,1)S(1)} %get-tuple-element.36), channel_id=1, source_target_pairs={{0,8},{1,9},{2,11},{3,10},{4,12},{5,13},{6,15},{7,14},{8,0},{9,1},... | collective-permute-start | bytes 393224 | tf_op jit(solution)/shard_map/ppermute | solution.py:372
  8.5 7.0 %collective-permute-start.5 = (bf16[512,128]{1,0:T(8,128)(2,1)S(1)}, bf16[512,128]{1,0:T(8,128)(2,1)S(1)}, u32[]{:S(2)}, u32[]{:S(2)}) collective-permute-start(bf16[512,128]{1,0:T(8,128)(2,1)S(1)} %get-tuple-element.37), channel_id=1, source_target_pairs={{0,0},{1,1},{2,3},{3,2},{4,4},{5,5},{6,7},{7,6},{8,8},{9,9},{10,11... | collective-permute-start | bytes 393224 | tf_op jit(solution)/shard_map/ppermute | solution.py:372
  9.1 1.5 %copy-start = (bf16[28,128,256]{2,1,0:T(8,128)(2,1)S(1)}, bf16[28,128,256]{2,1,0:T(8,128)(2,1)}, u32[]{:S(2)}) copy-start(bf16[28,128,256]{2,1,0:T(8,128)(2,1)} %w_ref.3) | copy-start | bytes 5505028
  10.6 12.8 %copy-start.1 = (bf16[28,128,256]{2,1,0:T(8,128)(2,1)S(1)}, bf16[28,128,256]{2,1,0:T(8,128)(2,1)}, u32[]{:S(2)}) copy-start(bf16[28,128,256]{2,1,0:T(8,128)(2,1)} %w_ref.3) | copy-start | bytes 5505028
  16.2 2.6 %collective-permute-start.6 = (bf16[14,32,128]{2,1,0:T(8,128)(2,1)S(1)}, bf16[14,32,128]{2,1,0:T(8,128)(2,1)S(1)}, u32[]{:S(2)}, u32[]{:S(2)}) collective-permute-start(bf16[14,32,128]{2,1,0:T(8,128)(2,1)S(1)} %get-tuple-element.45), channel_id=1, source_target_pairs={{0,2},{2,0},{4,6},{6,4},{8,10},{10,8},{12,14},{14,12},{16,18},{18,... | collective-permute-start | bytes 344072 | tf_op jit(solution)/shard_map/ppermute | solution.py:362
  17.2 6.2 %collective-permute-start.9 = (bf16[640,128]{1,0:T(8,128)(2,1)S(1)}, bf16[640,128]{1,0:T(8,128)(2,1)S(1)}, u32[]{:S(2)}, u32[]{:S(2)}) collective-permute-start(bf16[640,128]{1,0:T(8,128)(2,1)S(1)} %get-tuple-element.54.send_ref), channel_id=1, source_target_pairs={{0,1},{1,0},{2,3},{3,2},{4,5},{5,4},{6,7},{7,6},{8,9},{9,8},{10,11... | collective-permute-start | bytes 491528 | tf_op jit(solution)/shard_map/ppermute | solution.py:365
  19.4 6.6 %collective-permute-start.7 = (bf16[14,32,128]{2,1,0:T(8,128)(2,1)S(1)}, bf16[14,32,128]{2,1,0:T(8,128)(2,1)S(1)}, u32[]{:S(2)}, u32[]{:S(2)}) collective-permute-start(bf16[14,32,128]{2,1,0:T(8,128)(2,1)S(1)} %get-tuple-element.51), channel_id=1, source_target_pairs={{0,2},{2,0},{4,6},{6,4},{8,10},{10,8},{12,14},{14,12},{16,18},{18,... | collective-permute-start | bytes 344072 | tf_op jit(solution)/shard_map/ppermute | solution.py:362
  19.4 9.4 %collective-permute-start.11 = (bf16[14,32,128]{2,1,0:T(8,128)(2,1)S(1)}, bf16[14,32,128]{2,1,0:T(8,128)(2,1)S(1)}, u32[]{:S(2)}, u32[]{:S(2)}) collective-permute-start(bf16[14,32,128]{2,1,0:T(8,128)(2,1)S(1)} %add_convert_fusion.3), channel_id=1, source_target_pairs={{0,16},{2,18},{4,20},{6,22},{8,24},{10,26},{12,28},{14,30},{16,0},... | collective-permute-start | bytes 344072 | tf_op jit(solution)/shard_map/ppermute | solution.py:362
  24.4 8.1 %collective-permute-start.10 = (bf16[640,128]{1,0:T(8,128)(2,1)S(1)}, bf16[640,128]{1,0:T(8,128)(2,1)S(1)}, u32[]{:S(2)}, u32[]{:S(2)}) collective-permute-start(bf16[640,128]{1,0:T(8,128)(2,1)S(1)} %shard_map.63), channel_id=1, source_target_pairs={{0,1},{1,0},{2,3},{3,2},{4,5},{5,4},{6,7},{7,6},{8,9},{9,8},{10,11... | collective-permute-start | bytes 491528 | tf_op jit(solution)/shard_map/ppermute | solution.py:365
  26.0 7.7 %collective-permute-start.8 = (bf16[14,32,128]{2,1,0:T(8,128)(2,1)S(1)}, bf16[14,32,128]{2,1,0:T(8,128)(2,1)S(1)}, u32[]{:S(2)}, u32[]{:S(2)}) collective-permute-start(bf16[14,32,128]{2,1,0:T(8,128)(2,1)S(1)} %add_convert_fusion.2), channel_id=1, source_target_pairs={{0,16},{2,18},{4,20},{6,22},{8,24},{10,26},{12,28},{14,30},{16,0},... | collective-permute-start | bytes 344072 | tf_op jit(solution)/shard_map/ppermute | solution.py:362
  28.9 7.9 %collective-permute-start.14 = (bf16[14,32,128]{2,1,0:T(8,128)(2,1)S(1)}, bf16[14,32,128]{2,1,0:T(8,128)(2,1)S(1)}, u32[]{:S(2)}, u32[]{:S(2)}) collective-permute-start(bf16[14,32,128]{2,1,0:T(8,128)(2,1)S(1)} %add_convert_fusion.1.refs_0_), channel_id=1, source_target_pairs={{0,12},{2,14},{4,8},{6,10},{8,4},{10,6},{12,0},{14,2},{16,28},{18,... | collective-permute-start | bytes 344072 | tf_op jit(solution)/shard_map/ppermute | solution.py:362
  30.5 7.7 %collective-permute-start.13 = (bf16[14,32,128]{2,1,0:T(8,128)(2,1)S(1)}, bf16[14,32,128]{2,1,0:T(8,128)(2,1)S(1)}, u32[]{:S(2)}, u32[]{:S(2)}) collective-permute-start(bf16[14,32,128]{2,1,0:T(8,128)(2,1)S(1)} %add_convert_fusion.1.refs_0_), channel_id=1, source_target_pairs={{0,8},{2,10},{4,12},{6,14},{8,0},{10,2},{12,4},{14,6},{16,24},{18,... | collective-permute-start | bytes 344072 | tf_op jit(solution)/shard_map/ppermute | solution.py:362
  31.7 6.5 %collective-permute-start.12 = (bf16[14,32,128]{2,1,0:T(8,128)(2,1)S(1)}, bf16[14,32,128]{2,1,0:T(8,128)(2,1)S(1)}, u32[]{:S(2)}, u32[]{:S(2)}) collective-permute-start(bf16[14,32,128]{2,1,0:T(8,128)(2,1)S(1)} %add_convert_fusion.1.refs_0_), channel_id=1, source_target_pairs={{0,4},{2,6},{4,0},{6,2},{8,12},{10,14},{12,8},{14,10},{16,20},{18,... | collective-permute-start | bytes 344072 | tf_op jit(solution)/shard_map/ppermute | solution.py:362
  33.7 8.0 %collective-permute-start.18 = (bf16[14,32,128]{2,1,0:T(8,128)(2,1)S(1)}, bf16[14,32,128]{2,1,0:T(8,128)(2,1)S(1)}, u32[]{:S(2)}, u32[]{:S(2)}) collective-permute-start(bf16[14,32,128]{2,1,0:T(8,128)(2,1)S(1)} %add_convert_fusion.refs_5_), channel_id=1, source_target_pairs={{0,12},{2,14},{4,8},{6,10},{8,4},{10,6},{12,0},{14,2},{16,28},{18,... | collective-permute-start | bytes 344072 | tf_op jit(solution)/shard_map/ppermute | solution.py:362
  35.2 7.0 %collective-permute-start.17 = (bf16[14,32,128]{2,1,0:T(8,128)(2,1)S(1)}, bf16[14,32,128]{2,1,0:T(8,128)(2,1)S(1)}, u32[]{:S(2)}, u32[]{:S(2)}) collective-permute-start(bf16[14,32,128]{2,1,0:T(8,128)(2,1)S(1)} %add_convert_fusion.refs_5_), channel_id=1, source_target_pairs={{0,8},{2,10},{4,12},{6,14},{8,0},{10,2},{12,4},{14,6},{16,24},{18,... | collective-permute-start | bytes 344072 | tf_op jit(solution)/shard_map/ppermute | solution.py:362
  36.8 5.5 %collective-permute-start.16 = (bf16[14,32,128]{2,1,0:T(8,128)(2,1)S(1)}, bf16[14,32,128]{2,1,0:T(8,128)(2,1)S(1)}, u32[]{:S(2)}, u32[]{:S(2)}) collective-permute-start(bf16[14,32,128]{2,1,0:T(8,128)(2,1)S(1)} %add_convert_fusion.refs_5_), channel_id=1, source_target_pairs={{0,4},{2,6},{4,0},{6,2},{8,12},{10,14},{12,8},{14,10},{16,20},{18,... | collective-permute-start | bytes 344072 | tf_op jit(solution)/shard_map/ppermute | solution.py:362
  38.3 4.1 %collective-permute-start.15 = (bf16[56,32,128]{2,1,0:T(8,128)(2,1)S(1)}, bf16[56,32,128]{2,1,0:T(8,128)(2,1)S(1)}, u32[]{:S(2)}, u32[]{:S(2)}) collective-permute-start(bf16[56,32,128]{2,1,0:T(8,128)(2,1)S(1)} %pad_maximum_fusion), channel_id=1, source_target_pairs={{0,2},{2,0},{4,6},{6,4},{8,10},{10,8},{12,14},{14,12},{16,18},{18,... | collective-permute-start | bytes 1376264 | tf_op jit(solution)/shard_map/ppermute | solution.py:362
  42.3 1.9 %collective-permute-start.19 = (bf16[56,32,128]{2,1,0:T(8,128)(2,1)S(1)}, bf16[56,32,128]{2,1,0:T(8,128)(2,1)S(1)}, u32[]{:S(2)}, u32[]{:S(2)}) collective-permute-start(bf16[56,32,128]{2,1,0:T(8,128)(2,1)S(1)} %pad_maximum_fusion.1), channel_id=1, source_target_pairs={{0,2},{2,0},{4,6},{6,4},{8,10},{10,8},{12,14},{14,12},{16,18},{18,... | collective-permute-start | bytes 1376264 | tf_op jit(solution)/shard_map/ppermute | solution.py:362

commit v4 on v2

--- a/solution.py
+++ b/solution.py
@@ -9,18 +9,9 @@
 
 LANES = 128
 PARTS = 8
-DELIVERY = (3, 1, 2, 0)
-GATHER = (6, 4, 2)
-SPLITS = (14, 14)
+DELIVERY = (1, 2, 3, 0)
+GATHER = (2, 4, 6)
 BLOCK = 7
-ORDER = (0, 1)
-SWAP = 2
-SAMPLE = 1
-STAGGER = True
-BACK = 4
-FINISH = 1
-DELAY = 0
-PLACE = 0
 VMEM_BYTES = 48 * 1024 * 1024
 BF16 = jnp.bfloat16
 F32 = jnp.float32
@@ -113,68 +104,61 @@
         ref[start + side * cells : start + (side + 1) * cells, :] = cots[:, side * LANES : (side + 1) * LANES]
 
 
-def sort_kernel(edge, x_hbm, cot_hbm, send_ref, own_ref, rows_ref, x_ref, cot_ref, sems):
-    half = edge // 2
-    cells = half**3
+def sort_kernel(edge, x_ref, keep_ref, send_ref):
+    cells = (edge // 2) ** 3
     here = lax.axis_index("shard")
-    copies = [
-        pltpu.make_async_copy(x_hbm, x_ref, sems.at[0]),
-        pltpu.make_async_copy(cot_hbm, cot_ref, sems.at[1]),
-    ]
-    for copy in copies:
-        copy.start()
-    for copy in copies:
-        copy.wait()
     for index, value in enumerate(sorted_cells(edge, x_ref)):
         low, high = value[:, :LANES], value[:, LANES:]
-        own_ref[index * cells : (index + 1) * cells, :] = jnp.where(here == 0, low, high)
+        keep_ref[index * cells : (index + 1) * cells, :] = jnp.where(here == 0, low, high)
         send_ref[index * cells : (index + 1) * cells, :] = jnp.where(here == 0, high, low)
-    cots = rows_in(rows_ref, cot_ref, half)
-    put_cots(own_ref, 8 * cells, cots)
-    put_cots(send_ref, 8 * cells, cots)
-
-
-def pack_kernel(edge, groups, own_ref, send_ref, x2_ref, cot2_ref, *refs):
-    piece_refs, rows_ref = refs[:groups], refs[groups]
+
+
+def crossing(core, distance):
+    return core ^ (bin(distance).count("1") % 2)
+
+
+def pack_kernel(edge, groups, keep_ref, give_ref, cot_ref, x2_ref, cot2_ref, *refs):
+    piece_refs, (own_ref, send_ref, rows_ref) = refs[:groups], refs[groups:]
     half = edge // 2
     cells = half**3
     width = LANES // groups
     place = lax.axis_index("dp")
     core, group = lax.rem(place, 2), lax.rem(place // 2, groups)
-    target = lax.axis_index("shard") ^ core
-    samples = [
-        [
-            jnp.where(core == 0, own_ref[rows, :], send_ref[rows, :])
-            for rows in (slice(index * cells, (index + 1) * cells) for index in range(8))
-        ],
-        [
-            jnp.where(target == 0, value[:, :LANES], value[:, LANES:])
-            for value in sorted_cells(edge, x2_ref)
-        ],
-    ]
+    here = lax.axis_index("shard")
+    second = sorted_cells(edge, x2_ref)
     size = 4 * LANES
     row = lax.broadcasted_iota(jnp.int32, (size, size), 0)
     col = lax.broadcasted_iota(jnp.int32, (size, size), 1)
     source = ((col // width) % 4) * LANES + (col // LANES) * width + col % width
     lane_order = (row == source).astype(BF16)
-    wide = jnp.concatenate(
-        [
-            jnp.concatenate(classes[4 * first : 4 * first + 4], axis=1)
-            for classes in samples
-            for first in range(2)
-        ],
-        axis=0,
-    )
-    packed = dot(wide, lane_order).astype(BF16)
-    cots = rows_in(rows_ref, cot2_ref, half)
+    packed = []
+    for ref, owner in ((keep_ref, here), (give_ref, 1 - here)):
+        samples = [
+            [ref[index * cells : (index + 1) * cells, :] for index in range(8)],
+            [jnp.where(owner == 0, value[:, :LANES], value[:, LANES:]) for value in second],
+        ]
+        wide = jnp.concatenate(
+            [
+                jnp.concatenate(classes[4 * first : 4 * first + 4], axis=1)
+                for classes in samples
+                for first in range(2)
+            ],
+            axis=0,
+        )
+        packed.append(dot(wide, lane_order).astype(BF16))
+    cots = [rows_in(rows_ref, ref, half) for ref in (cot_ref, cot2_ref)]
     for distance, ref in enumerate(piece_refs):
         owner = group ^ distance
-        value = packed[:, (groups - 1) * LANES :]
+        chosen = jnp.where(crossing(core, distance) == 0, packed[0], packed[1])
+        value = chosen[:, (groups - 1) * LANES :]
         for index in range(groups - 1):
-            value = jnp.where(owner == index, packed[:, index * LANES : (index + 1) * LANES], value)
+            value = jnp.where(owner == index, chosen[:, index * LANES : (index + 1) * LANES], value)
         ref[0 : 4 * cells, :] = value
-        ref[4 * cells : 6 * cells, :] = own_ref[8 * cells : 10 * cells, :]
-        put_cots(ref, 6 * cells, cots)
+        put_cots(ref, 4 * cells, cots[0])
+        put_cots(ref, 6 * cells, cots[1])
+    for ref, half_ref in ((own_ref, keep_ref), (send_ref, give_ref)):
+        ref[0 : 8 * cells, :] = half_ref[...]
+        put_cots(ref, 8 * cells, cots[0])
 
 
 def weight_kernel(half, groups, start, count, *refs):
@@ -296,7 +280,7 @@
         ).astype(BF16)
 
 
-def place_kernel(parts, width, step, runs, has_base, *refs):
+def place_kernel(parts, width, runs, has_base, *refs):
     out_ref, buffer, sem = refs[-3:]
     refs = refs[has_base:-3]
     place = lax.axis_index("dp")
@@ -323,7 +307,7 @@
         copy.wait()
 
 
-def vmem_call(body, outs, flops=0, scratch=(), **kwargs):
+def vmem_call(body, outs, scratch=()):
     space = pl.BlockSpec(memory_space=pltpu.VMEM)
     return pl.pallas_call(
         body,
@@ -331,8 +315,7 @@
         out_specs=jax.tree.map(lambda _: space, outs),
         scratch_shapes=scratch,
         compiler_params=pltpu.CompilerParams(vmem_limit_bytes=VMEM_BYTES),
-        cost_estimate=pl.CostEstimate(flops=flops, bytes_accessed=1 << 20, transcendentals=0),
-        **kwargs,
+        cost_estimate=pl.CostEstimate(flops=0, bytes_accessed=1 << 20, transcendentals=0),
     )
 
 
@@ -366,100 +349,59 @@
         pairs = []
         for i in range(groups_of):
             for j in range(shards_of):
-                pairs.append((i * shards_of + j, (i ^ (2 * distance)) * shards_of + (j ^ (i % 2))))
+                there = i ^ (2 * distance)
+                pairs.append((i * shards_of + j, there * shards_of + (j ^ crossing(i % 2, distance))))
         return lax.ppermute(value, ("dp", "shard"), pairs)
 
     values2, rows2 = across(values, 1), across(rows, 1)
-    send, own = vmem_call(
-        functools.partial(sort_kernel, edge),
-        (shape((10 * cells, LANES)),) * 2,
-        scratch=row_buffer
-        + [
-            pltpu.VMEM(values.shape, BF16),
-            pltpu.VMEM(rows.shape, BF16),
-            pltpu.SemaphoreType.DMA((2,)),
-        ],
-        in_specs=[pl.BlockSpec(memory_space=pl.ANY)] * 2,
-    )(values, rows)
-    pieces = vmem_call(
+    keep, give = vmem_call(functools.partial(sort_kernel, edge), (shape((8 * cells, LANES)),) * 2)(values)
+    *pieces, own, send = vmem_call(
         functools.partial(pack_kernel, edge, groups),
-        (shape((8 * cells, LANES)),) * groups,
+        (shape((8 * cells, LANES)),) * groups + (shape((10 * cells, LANES)),) * 2,
         scratch=row_buffer,
-    )(own, send, values2, rows2)
-    splits = SPLITS
+    )(keep, give, rows, values2, rows2)
     got = [deliver(pieces[distance], distance) for distance in DELIVERY]
-    if SWAP == 1:
-        send = after(send, *pieces)
-    elif SWAP == 2:
-        send = after(send, *got)
-    other = swap(send)
-
+    other = swap(after(send, *got))
     part, grad = vmem_call(
         functools.partial(sample_kernel, half, False),
         (shape((cells, chans), F32), shape((8 * cells, LANES))),
     )(own, weights)
-    if SAMPLE == 0:
-        other, part, grad = lax.optimization_barrier((other, part, grad))
-    (back,) = vmem_call(
-        functools.partial(sample_kernel, half, True), (shape((10 * cells, LANES)),)
-    )(other, weights)
-    if SAMPLE == 0:
-        *got, back = lax.optimization_barrier((*got, back))
-    elif SAMPLE == 1:
-        *got, part, grad = lax.optimization_barrier((*got, part, grad))
-    totals, sums = {}, []
-    for turn, index in enumerate(ORDER):
-        n, start = splits[index], sum(splits[:index])
-        operands = got
-        if turn == 1 and STAGGER:
-            operands = lax.optimization_barrier((*got, totals[ORDER[0]]))[:-1]
+    *got, part, grad = lax.optimization_barrier((*got, part, grad))
+    (back,) = vmem_call(functools.partial(sample_kernel, half, True), (shape((10 * cells, LANES)),))(other, weights)
+
+    splits = (count // 2, count - count // 2)
+    totals = []
+    for index, taps in enumerate(splits):
         keep, give = vmem_call(
-            functools.partial(weight_kernel, half, groups, start, n),
-            (shape((n, width, LANES), F32), shape((n, width, LANES))),
-        )(*operands)
-        sums.append(give)
-        if turn == 0 and BACK == 3:
-            back = after(back, give)
-        totals[index] = (keep + across(give, 1).astype(F32)).astype(BF16)
-        if turn == 0 and BACK == 4:
-            back = after(back, totals[index])
-    if BACK == 1:
-        back = after(back, *totals.values())
-    elif BACK == 2:
-        back = after(back, *sums)
-    returned = swap(back)
+            functools.partial(weight_kernel, half, groups, sum(splits[:index]), taps),
+            (shape((taps, width, LANES), F32), shape((taps, width, LANES))),
+        )(*got)
+        totals.append((keep + across(give, 1).astype(F32)).astype(BF16))
+        if index == 0:
+            *got, _ = lax.optimization_barrier((*got, totals[0]))
+    returned = swap(after(back, totals[0]))
     outputs, input_grad = vmem_call(
         functools.partial(finish_kernel, edge),
         (shape(rows.shape), shape((edge**3, chans))),
         scratch=row_buffer,
     )(part, grad, returned)
 
-    held = []
-    for turn, index in enumerate(ORDER):
-        total = totals[index]
-        if turn == 1 and DELAY == 1:
-            total = after(total, other)
-        if turn == 1 and DELAY == 2:
-            total = after(total, back)
+    direct = []
+    for index, total in enumerate(totals):
         distance = parts
         while distance < groups_of:
             arrived = across(total, distance)
-            if turn == FINISH:
+            if index == 1:
                 arrived, outputs, input_grad = lax.optimization_barrier((arrived, outputs, input_grad))
             total = (total.astype(F32) + arrived.astype(F32)).astype(BF16)
             distance *= 2
-        held.append(total)
-    direct, crossed = [None] * len(splits), [None] * len(splits)
-    for index, total in zip(ORDER, held):
-        direct[index] = [total] + [across(total, distance) for distance in GATHER]
-    for index in ORDER:
-        crossed[index] = across(jnp.concatenate(direct[index], axis=0), 1)
-    base = None
+        direct.append([total] + [across(total, distance) for distance in GATHER])
+    crossed = [across(jnp.concatenate(values, axis=0), 1) for values in direct]
 
     def put(base, operands, runs):
         have = [] if base is None else [base]
         return pl.pallas_call(
-            functools.partial(place_kernel, parts, width, BLOCK, runs, len(have)),
+            functools.partial(place_kernel, parts, width, runs, len(have)),
             in_specs=[pl.BlockSpec(memory_space=pl.ANY)] * len(have)
             + [pl.BlockSpec(memory_space=pltpu.VMEM)] * len(operands),
             out_specs=pl.BlockSpec(memory_space=pl.ANY),
@@ -472,36 +414,22 @@
             compiler_params=pltpu.CompilerParams(vmem_limit_bytes=VMEM_BYTES),
         )(*have, *operands)
 
-    def runs_of(indices, sets):
+    def runs_of(parts_of):
         runs, at = [], 0
-        for index, kinds in zip(indices, sets):
-            n, first = splits[index], sum(splits[:index])
-            for kind in kinds:
-                for low in range(0, n, BLOCK):
-                    size = min(BLOCK, n - low)
-                    pieces = []
-                    for order, distance in enumerate((0,) + GATHER):
-                        if kind == 0:
-                            pieces.append((at + order, low, distance, size))
-                        else:
-                            pieces.append((at, order * n + low, distance, size))
-                    runs.append((first + low, kind, pieces))
-                at += 1 if kind else 1 + len(GATHER)
+        for index, flip in parts_of:
+            for low in range(0, splits[index], BLOCK):
+                size = min(BLOCK, splits[index] - low)
+                pieces = []
+                for order, distance in enumerate((0,) + GATHER):
+                    place = (at, order * splits[index] + low) if flip else (at + order, low)
+                    pieces.append((*place, distance, size))
+                runs.append((sum(splits[:index]) + low, flip, pieces))
+            at += 1 if flip else 1 + len(GATHER)
         return runs
 
-    if PLACE == 0:
-        base = put(None, sum(direct, []), runs_of(range(len(splits)), [(0,)] * len(splits)))
-        base = put(base, crossed, runs_of(range(len(splits)), [(1,)] * len(splits)))
-    else:
-        early, late = ORDER[0], ORDER[1]
-        base = put(None, direct[early] + [crossed[early]], runs_of([early], [(0, 1)]))
-        if PLACE == 2:
-            *there, base = lax.optimization_barrier((*direct[late], base))
-            direct[late] = list(there)
-            crossed[late] = across(jnp.concatenate(there, axis=0), 1)
-        base = put(base, direct[late], runs_of([late], [(0,)]))
-        base = put(base, [crossed[late]], runs_of([late], [(1,)]))
-    return outputs.reshape(cotangent.shape), input_grad.reshape(inputs.shape), base
+    early = put(None, [*direct[0], crossed[0], *direct[1]], runs_of([(0, 0), (0, 1), (1, 0)]))
+    weight_grad = put(early, [crossed[1]], runs_of([(1, 1)]))
+    return outputs.reshape(cotangent.shape), input_grad.reshape(inputs.shape), weight_grad
 
 
 def build_cols(values):

time: 46.8 us -> 45 us (0.962)
  waiting for transfers between devices: 11.4 us -> 10 us
  starting transfers between devices: 23.1 us -> 22.5 us
    ppermute x14, waiting for transfers between devices: 6.43 us -> 5.36 us  [across(): lax.ppermute(value, 'dp', [(i, i ^ distance) for i in range(groups_of)])]
    ppermute x2, starting transfers between devices: 3.03 us -> 2.04 us  [swap(): return lax.ppermute(value, 'shard', [(0, 1), (1, 0)])]
    ppermute x4, starting transfers between devices: 5.29 us -> 6.08 us  [deliver(): return lax.ppermute(value, ('dp', 'shard'), pairs)]
    ppermute x4, waiting for transfers between devices: 3.82 us -> 3.09 us  [deliver(): return lax.ppermute(value, ('dp', 'shard'), pairs)]
  transfers between devices with their start and end apart: 20 -> 20, of which waited for: 10 -> 10; matrix products, arithmetic and copies ran while one was open for 1% -> 1% of each run, Pallas kernels for 11% -> 12%
where the time goes in v4:
time: 45 us; the launch traced here: 44.8 us
  starting transfers between devices  22.5 us (50%)
  waiting for transfers between devices  10 us (22%)
  Pallas kernels  7.97 us (18%)
  local copies, waits for them, and re-layouts  3.21 us (7%)
  between operations  0.78 us (2%)
    ppermute x14, starting transfers between devices, across(): lax.ppermute(value, 'dp', [(i, i ^ distance) for i in range(groups_of)])  14.4 us
    ppermute x4, starting transfers between devices, deliver(): return lax.ppermute(value, ('dp', 'shard'), pairs)  6.08 us
    ppermute x14, waiting for transfers between devices, across(): lax.ppermute(value, 'dp', [(i, i ^ distance) for i in range(groups_of)])  5.36 us
    unnamed x8, local copies, waits for them, and re-layouts  3.21 us
    ppermute x4, waiting for transfers between devices, deliver(): return lax.ppermute(value, ('dp', 'shard'), pairs)  3.09 us
    pallas_call x2, Pallas kernels, put(): pl.pallas_call(functools.partial(place_kernel, parts, width, runs, len(ha...  2.62 us
    ppermute x2, starting transfers between devices, swap(): return lax.ppermute(value, 'shard', [(0, 1), (1, 0)])  2.04 us
    ppermute x2, waiting for transfers between devices, swap(): return lax.ppermute(value, 'shard', [(0, 1), (1, 0)])  1.57 us
  transfers between devices with their start and end apart: 20, of which 10 were waited for; matrix products, arithmetic and copies ran while one was open for 1% of the time, Pallas kernels for 12%

profile of v4, /device:TPU:0, one launch (start us, length us, event | category | flops | bytes accessed | tf_op | source)
XLA Modules:
  0.0 44.8 jit_solution(7939460848327906282)
XLA Ops:
  0.6 0.5 %collective-permute-start = (bf16[512,256]{1,0:T(8,128)(2,1)}, bf16[512,256]{1,0:T(8,128)(2,1)S(1)}, u32[]{:S(2)}, u32[]{:S(2)}) collective-permute-start(bf16[512,256]{1,0:T(8,128)(2,1)} %bitcast.4), channel_id=1, source_target_pairs={{0,2},{2,0},{4,6},{6,4},{8,10},{10,8},{12,14},{14,12},{16,18},{18,... | collective-permute-start | bytes 786440 | tf_op jit(solution)/shard_map/ppermute | solution.py:343
  1.1 0.1 collective-permute-start.1
  1.2 0.0 copy-start.2
  1.2 0.9 %copy-done.2 = bf16[1,8,8,8,256]{4,3,2,1,0:T(8,128)(2,1)S(1)} copy-done((bf16[1,8,8,8,256]{4,3,2,1,0:T(8,128)(2,1)S(1)}, bf16[1,8,8,8,256]{4,3,2,1,0:T(8,128)(2,1)}, u32[]{:S(2)}) %copy-start.2) | copy-done | bytes 262168
  2.2 0.3 shard_map.58
  2.5 0.1 collective-permute-done.1.cot2_ref
  2.6 0.0 collective-permute-done.x2_ref
  2.6 0.0 copy-start.3
  2.6 0.8 %copy-done.3 = bf16[1,4,4,4,256]{4,3,2,1,0:T(4,128)(2,1)S(1)} copy-done((bf16[1,4,4,4,256]{4,3,2,1,0:T(4,128)(2,1)S(1)}, bf16[1,4,4,4,256]{4,3,2,1,0:T(4,128)(2,1)}, u32[]{:S(2)}) %copy-start.3) | copy-done | bytes 32792
  3.3 0.7 %shard_map.59 = (bf16[512,128]{1,0:T(8,128)(2,1)S(1)}, bf16[512,128]{1,0:T(8,128)(2,1)S(1)}, bf16[512,128]{1,0:T(8,128)(2,1)S(1)}, bf16[512,128]{1,0:T(8,128)(2,...) custom-call(bf16[512,128]{1,0:T(8,128)(2,1)S(1)} %get-tuple-element.34.keep_ref, ...), custom_call_target="tpu_custom_call" | custom-call | bytes 1048576 | tf_op jit(solution)/shard_map/pallas_call | solution.py:358
  4.1 3.9 %collective-permute-start.2 = (bf16[512,128]{1,0:T(8,128)(2,1)S(1)}, bf16[512,128]{1,0:T(8,128)(2,1)S(1)}, u32[]{:S(2)}, u32[]{:S(2)}) collective-permute-start(bf16[512,128]{1,0:T(8,128)(2,1)S(1)} %get-tuple-element.36), channel_id=1, source_target_pairs={{0,5},{1,4},{2,6},{3,7},{4,1},{5,0},{6,2},{7,3},{8,13},{9,12},{10,... | collective-permute-start | bytes 393224 | tf_op jit(solution)/shard_map/ppermute | solution.py:354
  8.0 1.5 %collective-permute-start.3 = (bf16[512,128]{1,0:T(8,128)(2,1)S(1)}, bf16[512,128]{1,0:T(8,128)(2,1)S(1)}, u32[]{:S(2)}, u32[]{:S(2)}) collective-permute-start(bf16[512,128]{1,0:T(8,128)(2,1)S(1)} %get-tuple-element.37), channel_id=1, source_target_pairs={{0,9},{1,8},{2,10},{3,11},{4,13},{5,12},{6,14},{7,15},{8,1},{9,0},... | collective-permute-start | bytes 393224 | tf_op jit(solution)/shard_map/ppermute | solution.py:354
  9.5 0.0 collective-permute-start.4
  9.5 0.7 %collective-permute-start.5 = (bf16[512,128]{1,0:T(8,128)(2,1)S(1)}, bf16[512,128]{1,0:T(8,128)(2,1)S(1)}, u32[]{:S(2)}, u32[]{:S(2)}) collective-permute-start(bf16[512,128]{1,0:T(8,128)(2,1)S(1)} %get-tuple-element.39), channel_id=1, source_target_pairs={{0,0},{1,1},{2,3},{3,2},{4,4},{5,5},{6,7},{7,6},{8,8},{9,9},{10,11... | collective-permute-start | bytes 393224 | tf_op jit(solution)/shard_map/ppermute | solution.py:354
  10.2 0.0 copy-start
  10.2 1.5 %copy-done = bf16[28,128,256]{2,1,0:T(8,128)(2,1)S(1)} copy-done((bf16[28,128,256]{2,1,0:T(8,128)(2,1)S(1)}, bf16[28,128,256]{2,1,0:T(8,128)(2,1)}, u32[]{:S(2)}) %copy-start) | copy-done | bytes 1835032
  11.7 0.0 copy-start.1
  11.7 1.0 %shard_map.60 = (f32[64,256]{1,0:T(8,128)S(1)}, bf16[512,128]{1,0:T(8,128)(2,1)S(1)}) custom-call(bf16[640,128]{1,0:T(8,128)(2,1)S(1)} %get-tuple-element.40.own_ref, bf16[28,128,256]{2,1,0:T(8,128)(2,1)S(1)} %copy-done), custom_call_target="tpu_custom_call" | custom-call | bytes 1048576 | tf_op jit(solution)/shard_map/pallas_call | solution.py:365
  12.6 0.0 collective-permute-done.2.refs_0_
  12.6 2.4 %collective-permute-done.3.refs_1_ = bf16[512,128]{1,0:T(8,128)(2,1)S(1)} collective-permute-done((bf16[512,128]{1,0:T(8,128)(2,1)S(1)}, bf16[512,128]{1,0:T(8,128)(2,1)S(1)}, u32[]{:S(2)}, u32[]{:S(2)}) %collective-permute-start.3) | collective-permute-done | bytes 131104 | tf_op jit(solution)/shard_map/ppermute | solution.py:354
  15.1 0.7 %collective-permute-done.4.refs_2_ = bf16[512,128]{1,0:T(8,128)(2,1)S(1)} collective-permute-done((bf16[512,128]{1,0:T(8,128)(2,1)S(1)}, bf16[512,128]{1,0:T(8,128)(2,1)S(1)}, u32[]{:S(2)}, u32[]{:S(2)}) %collective-permute-start.4) | collective-permute-done | bytes 131104 | tf_op jit(solution)/shard_map/ppermute | solution.py:354
  15.7 0.0 collective-permute-done.5.refs_3_
  15.7 0.7 %shard_map.61 = (f32[14,32,128]{2,1,0:T(8,128)S(1)}, bf16[14,32,128]{2,1,0:T(8,128)(2,1)S(1)}) custom-call(bf16[512,128]{1,0:T(8,128)(2,1)S(1)} %collective-permute-done.2.refs_0_, bf16[512,128]{1,0:T(8,128)(2,1)S(1)} %collective-permute-done.3.refs_1_, bf16[512,128]{1,0:T(8,128)(2,1)S(1)} %collective-permute-done.4.refs_2_, ...), custom_call_target="tpu_custom_call" | custom-call | bytes 1048576 | tf_op jit(solution)/shard_map/pallas_call | solution.py:375
  16.5 0.9 %collective-permute-start.6 = (bf16[14,32,128]{2,1,0:T(8,128)(2,1)S(1)}, bf16[14,32,128]{2,1,0:T(8,128)(2,1)S(1)}, u32[]{:S(2)}, u32[]{:S(2)}) collective-permute-start(bf16[14,32,128]{2,1,0:T(8,128)(2,1)S(1)} %get-tuple-element.48), channel_id=1, source_target_pairs={{0,2},{2,0},{4,6},{6,4},{8,10},{10,8},{12,14},{14,12},{16,18},{18,... | collective-permute-start | bytes 344072 | tf_op jit(solution)/shard_map/ppermute | solution.py:343
  17.3 0.9 %collective-permute-start.9 = (bf16[640,128]{1,0:T(8,128)(2,1)S(1)}, bf16[640,128]{1,0:T(8,128)(2,1)S(1)}, u32[]{:S(2)}, u32[]{:S(2)}) collective-permute-start(bf16[640,128]{1,0:T(8,128)(2,1)S(1)} %get-tuple-element.58), channel_id=1, source_target_pairs={{0,1},{1,0},{2,3},{3,2},{4,5},{5,4},{6,7},{7,6},{8,9},{9,8},{10,11... | collective-permute-start | bytes 491528 | tf_op jit(solution)/shard_map/ppermute | solution.py:346
  18.2 0.0 collective-permute-done.6
  18.3 0.6 %shard_map.62 = (f32[14,32,128]{2,1,0:T(8,128)S(1)}, bf16[14,32,128]{2,1,0:T(8,128)(2,1)S(1)}) custom-call(bf16[512,128]{1,0:T(8,128)(2,1)S(1)} %collective-permute-done.2.refs_0_, bf16[512,128]{1,0:T(8,128)(2,1)S(1)} %collective-permute-done.3.refs_1_, bf16[512,128]{1,0:T(8,128)(2,1)S(1)} %collective-permute-done.4.refs_2_, ...), custom_call_target="tpu_custom_call" | custom-call | bytes 1048576 | tf_op jit(solution)/shard_map/pallas_call | solution.py:375
  18.9 0.4 collective-permute-start.7
  19.3 2.6 %collective-permute-start.11 = (bf16[14,32,128]{2,1,0:T(8,128)(2,1)S(1)}, bf16[14,32,128]{2,1,0:T(8,128)(2,1)S(1)}, u32[]{:S(2)}, u32[]{:S(2)}) collective-permute-start(bf16[14,32,128]{2,1,0:T(8,128)(2,1)S(1)} %add_convert_fusion.3), channel_id=1, source_target_pairs={{0,16},{2,18},{4,20},{6,22},{8,24},{10,26},{12,28},{14,30},{16,0},... | collective-permute-start | bytes 344072 | tf_op jit(solution)/shard_map/ppermute | solution.py:343
  21.9 1.6 %collective-permute-done.9.own_ref = bf16[640,128]{1,0:T(8,128)(2,1)S(1)} collective-permute-done((bf16[640,128]{1,0:T(8,128)(2,1)S(1)}, bf16[640,128]{1,0:T(8,128)(2,1)S(1)}, u32[]{:S(2)}, u32[]{:S(2)}) %collective-permute-start.9) | collective-permute-done | bytes 163872 | tf_op jit(solution)/shard_map/ppermute | solution.py:346
  23.5 0.0 copy-done.1
  23.5 1.0 %shard_map.63 = bf16[640,128]{1,0:T(8,128)(2,1)S(1)} custom-call(bf16[640,128]{1,0:T(8,128)(2,1)S(1)} %collective-permute-done.9.own_ref, bf16[28,128,256]{2,1,0:T(8,128)(2,1)S(1)} %copy-done.1), custom_call_target="tpu_custom_call" | custom-call | bytes 1048576 | tf_op jit(solution)/shard_map/pallas_call | solution.py:370
  24.5 1.1 %collective-permute-start.10 = (bf16[640,128]{1,0:T(8,128)(2,1)S(1)}, bf16[640,128]{1,0:T(8,128)(2,1)S(1)}, u32[]{:S(2)}, u32[]{:S(2)}) collective-permute-start(bf16[640,128]{1,0:T(8,128)(2,1)S(1)} %shard_map.63), channel_id=1, source_target_pairs={{0,1},{1,0},{2,3},{3,2},{4,5},{5,4},{6,7},{7,6},{8,9},{9,8},{10,11... | collective-permute-start | bytes 491528 | tf_op jit(solution)/shard_map/ppermute | solution.py:346
  25.6 0.0 collective-permute-done.7
  25.6 2.7 %collective-permute-start.8 = (bf16[14,32,128]{2,1,0:T(8,128)(2,1)S(1)}, bf16[14,32,128]{2,1,0:T(8,128)(2,1)S(1)}, u32[]{:S(2)}, u32[]{:S(2)}) collective-permute-start(bf16[14,32,128]{2,1,0:T(8,128)(2,1)S(1)} %add_convert_fusion.2), channel_id=1, source_target_pairs={{0,16},{2,18},{4,20},{6,22},{8,24},{10,26},{12,28},{14,30},{16,0},... | collective-permute-start | bytes 344072 | tf_op jit(solution)/shard_map/ppermute | solution.py:343
  28.3 0.0 collective-permute-done.11
  28.3 2.0 %collective-permute-start.14 = (bf16[14,32,128]{2,1,0:T(8,128)(2,1)S(1)}, bf16[14,32,128]{2,1,0:T(8,128)(2,1)S(1)}, u32[]{:S(2)}, u32[]{:S(2)}) collective-permute-start(bf16[14,32,128]{2,1,0:T(8,128)(2,1)S(1)} %add_convert_fusion.1.refs_0_), channel_id=1, source_target_pairs={{0,12},{2,14},{4,8},{6,10},{8,4},{10,6},{12,0},{14,2},{16,28},{18,... | collective-permute-start | bytes 344072 | tf_op jit(solution)/shard_map/ppermute | solution.py:343
  30.3 0.4 %collective-permute-start.13 = (bf16[14,32,128]{2,1,0:T(8,128)(2,1)S(1)}, bf16[14,32,128]{2,1,0:T(8,128)(2,1)S(1)}, u32[]{:S(2)}, u32[]{:S(2)}) collective-permute-start(bf16[14,32,128]{2,1,0:T(8,128)(2,1)S(1)} %add_convert_fusion.1.refs_0_), channel_id=1, source_target_pairs={{0,8},{2,10},{4,12},{6,14},{8,0},{10,2},{12,4},{14,6},{16,24},{18,... | collective-permute-start | bytes 344072 | tf_op jit(solution)/shard_map/ppermute | solution.py:343
  30.7 1.1 %collective-permute-start.12 = (bf16[14,32,128]{2,1,0:T(8,128)(2,1)S(1)}, bf16[14,32,128]{2,1,0:T(8,128)(2,1)S(1)}, u32[]{:S(2)}, u32[]{:S(2)}) collective-permute-start(bf16[14,32,128]{2,1,0:T(8,128)(2,1)S(1)} %add_convert_fusion.1.refs_0_), channel_id=1, source_target_pairs={{0,4},{2,6},{4,0},{6,2},{8,12},{10,14},{12,8},{14,10},{16,20},{18,... | collective-permute-start | bytes 344072 | tf_op jit(solution)/shard_map/ppermute | solution.py:343
  31.9 0.0 collective-permute-done.10.got_ref
  31.9 1.1 %shard_map.64 = (bf16[4,4,4,256]{3,2,1,0:T(4,128)(2,1)}, bf16[512,256]{1,0:T(8,128)(2,1)}) custom-call(f32[64,256]{1,0:T(8,128)S(1)} %get-tuple-element.55.part_ref, bf16[512,128]{1,0:T(8,128)(2,1)S(1)} %get-tuple-element.56.grad_ref, bf16[640,128]{1,0:T(8,128)(2,1)S(1)} %collective-permute-done.10.got_ref), custom_call_target="tpu_custom_call" | custom-call | bytes 1048576 | tf_op jit(solution)/shard_map/pallas_call | solution.py:383
  33.0 0.3 collective-permute-done.8
  33.4 1.6 %collective-permute-start.18 = (bf16[14,32,128]{2,1,0:T(8,128)(2,1)S(1)}, bf16[14,32,128]{2,1,0:T(8,128)(2,1)S(1)}, u32[]{:S(2)}, u32[]{:S(2)}) collective-permute-start(bf16[14,32,128]{2,1,0:T(8,128)(2,1)S(1)} %add_convert_fusion.refs_5_), channel_id=1, source_target_pairs={{0,12},{2,14},{4,8},{6,10},{8,4},{10,6},{12,0},{14,2},{16,28},{18,... | collective-permute-start | bytes 344072 | tf_op jit(solution)/shard_map/ppermute | solution.py:343
  35.0 0.7 %collective-permute-start.17 = (bf16[14,32,128]{2,1,0:T(8,128)(2,1)S(1)}, bf16[14,32,128]{2,1,0:T(8,128)(2,1)S(1)}, u32[]{:S(2)}, u32[]{:S(2)}) collective-permute-start(bf16[14,32,128]{2,1,0:T(8,128)(2,1)S(1)} %add_convert_fusion.refs_5_), channel_id=1, source_target_pairs={{0,8},{2,10},{4,12},{6,14},{8,0},{10,2},{12,4},{14,6},{16,24},{18,... | collective-permute-start | bytes 344072 | tf_op jit(solution)/shard_map/ppermute | solution.py:343
  35.7 0.3 collective-permute-done.14.refs_3_
  36.0 1.3 %collective-permute-start.16 = (bf16[14,32,128]{2,1,0:T(8,128)(2,1)S(1)}, bf16[14,32,128]{2,1,0:T(8,128)(2,1)S(1)}, u32[]{:S(2)}, u32[]{:S(2)}) collective-permute-start(bf16[14,32,128]{2,1,0:T(8,128)(2,1)S(1)} %add_convert_fusion.refs_5_), channel_id=1, source_target_pairs={{0,4},{2,6},{4,0},{6,2},{8,12},{10,14},{12,8},{14,10},{16,20},{18,... | collective-permute-start | bytes 344072 | tf_op jit(solution)/shard_map/ppermute | solution.py:343
  37.3 0.9 %collective-permute-done.13.refs_2_ = bf16[14,32,128]{2,1,0:T(8,128)(2,1)S(1)} collective-permute-done((bf16[14,32,128]{2,1,0:T(8,128)(2,1)S(1)}, bf16[14,32,128]{2,1,0:T(8,128)(2,1)S(1)}, u32[]{:S(2)}, u32[]{:S(2)}) %collective-permute-start.13) | collective-permute-done | bytes 114720 | tf_op jit(solution)/shard_map/ppermute | solution.py:343
  38.2 0.0 collective-permute-done.12.refs_1_
  38.2 0.1 pad_maximum_fusion
  38.2 0.1 collective-permute-start.15
  38.3 2.2 %collective-permute-done.18.refs_8_ = bf16[14,32,128]{2,1,0:T(8,128)(2,1)S(1)} collective-permute-done((bf16[14,32,128]{2,1,0:T(8,128)(2,1)S(1)}, bf16[14,32,128]{2,1,0:T(8,128)(2,1)S(1)}, u32[]{:S(2)}, u32[]{:S(2)}) %collective-permute-start.18) | collective-permute-done | bytes 114720 | tf_op jit(solution)/shard_map/ppermute | solution.py:343
  40.5 1.3 %collective-permute-done.17.refs_7_ = bf16[14,32,128]{2,1,0:T(8,128)(2,1)S(1)} collective-permute-done((bf16[14,32,128]{2,1,0:T(8,128)(2,1)S(1)}, bf16[14,32,128]{2,1,0:T(8,128)(2,1)S(1)}, u32[]{:S(2)}, u32[]{:S(2)}) %collective-permute-start.17) | collective-permute-done | bytes 114720 | tf_op jit(solution)/shard_map/ppermute | solution.py:343
  41.8 0.0 collective-permute-done.16.refs_6_
  41.8 0.1 pad_maximum_fusion.1
  41.9 0.1 collective-permute-start.19
  42.0 0.0 collective-permute-done.15.refs_4_
  42.0 1.6 %shard_map.65.refs_0_ = f32[28,128,256]{2,1,0:T(8,128)} custom-call(bf16[14,32,128]{2,1,0:T(8,128)(2,1)S(1)} %add_convert_fusion.1.refs_0_, bf16[14,32,128]{2,1,0:T(8,128)(2,1)S(1)} %collective-permute-done.12.refs_1_, bf16[14,32,128]{2,1,0:T(8,128)(2,1)S(1)} %collective-permute-done.13.refs_2_, bf16[14,32,128]{2,1,0:T(8,128)(2,1)S(1)} %collective-permute-done.14.refs_3_, ...), custom_call_target="tpu_custom_call" | custom-call | tf_op jit(solution)/shard_map/pallas_call | solution.py:403
  43.6 0.2 collective-permute-done.19.refs_1_
  43.8 1.0 %shard_map.66 = f32[28,128,256]{2,1,0:T(8,128)} custom-call(f32[28,128,256]{2,1,0:T(8,128)} %shard_map.65.refs_0_, bf16[56,32,128]{2,1,0:T(8,128)(2,1)S(1)} %collective-permute-done.19.refs_1_), custom_call_target="tpu_custom_call", output_to_operand_aliasing={{}: (0, {})} | custom-call | tf_op jit(solution)/shard_map/pallas_call | solution.py:403
  (4 shorter events, 0.1 us)
Async XLA Ops:
  0.6 1.9 %collective-permute-start = (bf16[512,256]{1,0:T(8,128)(2,1)}, bf16[512,256]{1,0:T(8,128)(2,1)S(1)}, u32[]{:S(2)}, u32[]{:S(2)}) collective-permute-start(bf16[512,256]{1,0:T(8,128)(2,1)} %bitcast.4), channel_id=1, source_target_pairs={{0,2},{2,0},{4,6},{6,4},{8,10},{10,8},{12,14},{14,12},{16,18},{18,... | collective-permute-start | bytes 786440 | tf_op jit(solution)/shard_map/ppermute | solution.py:343
  1.1 1.4 %collective-permute-start.1 = (bf16[4,4,4,256]{3,2,1,0:T(4,128)(2,1)}, bf16[4,4,4,256]{3,2,1,0:T(4,128)(2,1)S(1)}, u32[]{:S(2)}, u32[]{:S(2)}) collective-permute-start(bf16[4,4,4,256]{3,2,1,0:T(4,128)(2,1)} %bitcast.6), channel_id=1, source_target_pairs={{0,2},{2,0},{4,6},{6,4},{8,10},{10,8},{12,14},{14,12},{16,18},{18,... | collective-permute-start | bytes 98312 | tf_op jit(solution)/shard_map/ppermute | solution.py:343
  1.2 0.9 %copy-start.2 = (bf16[1,8,8,8,256]{4,3,2,1,0:T(8,128)(2,1)S(1)}, bf16[1,8,8,8,256]{4,3,2,1,0:T(8,128)(2,1)}, u32[]{:S(2)}) copy-start(bf16[1,8,8,8,256]{4,3,2,1,0:T(8,128)(2,1)} %param.3) | copy-start | bytes 786436
  2.6 0.8 %copy-start.3 = (bf16[1,4,4,4,256]{4,3,2,1,0:T(4,128)(2,1)S(1)}, bf16[1,4,4,4,256]{4,3,2,1,0:T(4,128)(2,1)}, u32[]{:S(2)}) copy-start(bf16[1,4,4,4,256]{4,3,2,1,0:T(4,128)(2,1)} %param.4) | copy-start | bytes 98308
  4.1 8.6 %collective-permute-start.2 = (bf16[512,128]{1,0:T(8,128)(2,1)S(1)}, bf16[512,128]{1,0:T(8,128)(2,1)S(1)}, u32[]{:S(2)}, u32[]{:S(2)}) collective-permute-start(bf16[512,128]{1,0:T(8,128)(2,1)S(1)} %get-tuple-element.36), channel_id=1, source_target_pairs={{0,5},{1,4},{2,6},{3,7},{4,1},{5,0},{6,2},{7,3},{8,13},{9,12},{10,... | collective-permute-start | bytes 393224 | tf_op jit(solution)/shard_map/ppermute | solution.py:354
  8.0 7.1 %collective-permute-start.3 = (bf16[512,128]{1,0:T(8,128)(2,1)S(1)}, bf16[512,128]{1,0:T(8,128)(2,1)S(1)}, u32[]{:S(2)}, u32[]{:S(2)}) collective-permute-start(bf16[512,128]{1,0:T(8,128)(2,1)S(1)} %get-tuple-element.37), channel_id=1, source_target_pairs={{0,9},{1,8},{2,10},{3,11},{4,13},{5,12},{6,14},{7,15},{8,1},{9,0},... | collective-permute-start | bytes 393224 | tf_op jit(solution)/shard_map/ppermute | solution.py:354
  9.5 6.3 %collective-permute-start.4 = (bf16[512,128]{1,0:T(8,128)(2,1)S(1)}, bf16[512,128]{1,0:T(8,128)(2,1)S(1)}, u32[]{:S(2)}, u32[]{:S(2)}) collective-permute-start(bf16[512,128]{1,0:T(8,128)(2,1)S(1)} %get-tuple-element.38), channel_id=1, source_target_pairs={{0,12},{1,13},{2,15},{3,14},{4,8},{5,9},{6,11},{7,10},{8,4},{9,5},... | collective-permute-start | bytes 393224 | tf_op jit(solution)/shard_map/ppermute | solution.py:354
  9.5 6.2 %collective-permute-start.5 = (bf16[512,128]{1,0:T(8,128)(2,1)S(1)}, bf16[512,128]{1,0:T(8,128)(2,1)S(1)}, u32[]{:S(2)}, u32[]{:S(2)}) collective-permute-start(bf16[512,128]{1,0:T(8,128)(2,1)S(1)} %get-tuple-element.39), channel_id=1, source_target_pairs={{0,0},{1,1},{2,3},{3,2},{4,4},{5,5},{6,7},{7,6},{8,8},{9,9},{10,11... | collective-permute-start | bytes 393224 | tf_op jit(solution)/shard_map/ppermute | solution.py:354
  10.2 1.5 %copy-start = (bf16[28,128,256]{2,1,0:T(8,128)(2,1)S(1)}, bf16[28,128,256]{2,1,0:T(8,128)(2,1)}, u32[]{:S(2)}) copy-start(bf16[28,128,256]{2,1,0:T(8,128)(2,1)} %w_ref.3) | copy-start | bytes 5505028
  11.7 11.8 %copy-start.1 = (bf16[28,128,256]{2,1,0:T(8,128)(2,1)S(1)}, bf16[28,128,256]{2,1,0:T(8,128)(2,1)}, u32[]{:S(2)}) copy-start(bf16[28,128,256]{2,1,0:T(8,128)(2,1)} %w_ref.3) | copy-start | bytes 5505028
  16.5 1.8 %collective-permute-start.6 = (bf16[14,32,128]{2,1,0:T(8,128)(2,1)S(1)}, bf16[14,32,128]{2,1,0:T(8,128)(2,1)S(1)}, u32[]{:S(2)}, u32[]{:S(2)}) collective-permute-start(bf16[14,32,128]{2,1,0:T(8,128)(2,1)S(1)} %get-tuple-element.48), channel_id=1, source_target_pairs={{0,2},{2,0},{4,6},{6,4},{8,10},{10,8},{12,14},{14,12},{16,18},{18,... | collective-permute-start | bytes 344072 | tf_op jit(solution)/shard_map/ppermute | solution.py:343
  17.3 6.2 %collective-permute-start.9 = (bf16[640,128]{1,0:T(8,128)(2,1)S(1)}, bf16[640,128]{1,0:T(8,128)(2,1)S(1)}, u32[]{:S(2)}, u32[]{:S(2)}) collective-permute-start(bf16[640,128]{1,0:T(8,128)(2,1)S(1)} %get-tuple-element.58), channel_id=1, source_target_pairs={{0,1},{1,0},{2,3},{3,2},{4,5},{5,4},{6,7},{7,6},{8,9},{9,8},{10,11... | collective-permute-start | bytes 491528 | tf_op jit(solution)/shard_map/ppermute | solution.py:346
  18.9 6.7 %collective-permute-start.7 = (bf16[14,32,128]{2,1,0:T(8,128)(2,1)S(1)}, bf16[14,32,128]{2,1,0:T(8,128)(2,1)S(1)}, u32[]{:S(2)}, u32[]{:S(2)}) collective-permute-start(bf16[14,32,128]{2,1,0:T(8,128)(2,1)S(1)} %get-tuple-element.54), channel_id=1, source_target_pairs={{0,2},{2,0},{4,6},{6,4},{8,10},{10,8},{12,14},{14,12},{16,18},{18,... | collective-permute-start | bytes 344072 | tf_op jit(solution)/shard_map/ppermute | solution.py:343
  19.3 8.9 %collective-permute-start.11 = (bf16[14,32,128]{2,1,0:T(8,128)(2,1)S(1)}, bf16[14,32,128]{2,1,0:T(8,128)(2,1)S(1)}, u32[]{:S(2)}, u32[]{:S(2)}) collective-permute-start(bf16[14,32,128]{2,1,0:T(8,128)(2,1)S(1)} %add_convert_fusion.3), channel_id=1, source_target_pairs={{0,16},{2,18},{4,20},{6,22},{8,24},{10,26},{12,28},{14,30},{16,0},... | collective-permute-start | bytes 344072 | tf_op jit(solution)/shard_map/ppermute | solution.py:343
  24.5 7.4 %collective-permute-start.10 = (bf16[640,128]{1,0:T(8,128)(2,1)S(1)}, bf16[640,128]{1,0:T(8,128)(2,1)S(1)}, u32[]{:S(2)}, u32[]{:S(2)}) collective-permute-start(bf16[640,128]{1,0:T(8,128)(2,1)S(1)} %shard_map.63), channel_id=1, source_target_pairs={{0,1},{1,0},{2,3},{3,2},{4,5},{5,4},{6,7},{7,6},{8,9},{9,8},{10,11... | collective-permute-start | bytes 491528 | tf_op jit(solution)/shard_map/ppermute | solution.py:346
  25.6 7.7 %collective-permute-start.8 = (bf16[14,32,128]{2,1,0:T(8,128)(2,1)S(1)}, bf16[14,32,128]{2,1,0:T(8,128)(2,1)S(1)}, u32[]{:S(2)}, u32[]{:S(2)}) collective-permute-start(bf16[14,32,128]{2,1,0:T(8,128)(2,1)S(1)} %add_convert_fusion.2), channel_id=1, source_target_pairs={{0,16},{2,18},{4,20},{6,22},{8,24},{10,26},{12,28},{14,30},{16,0},... | collective-permute-start | bytes 344072 | tf_op jit(solution)/shard_map/ppermute | solution.py:343
  28.3 7.7 %collective-permute-start.14 = (bf16[14,32,128]{2,1,0:T(8,128)(2,1)S(1)}, bf16[14,32,128]{2,1,0:T(8,128)(2,1)S(1)}, u32[]{:S(2)}, u32[]{:S(2)}) collective-permute-start(bf16[14,32,128]{2,1,0:T(8,128)(2,1)S(1)} %add_convert_fusion.1.refs_0_), channel_id=1, source_target_pairs={{0,12},{2,14},{4,8},{6,10},{8,4},{10,6},{12,0},{14,2},{16,28},{18,... | collective-permute-start | bytes 344072 | tf_op jit(solution)/shard_map/ppermute | solution.py:343
  30.3 7.9 %collective-permute-start.13 = (bf16[14,32,128]{2,1,0:T(8,128)(2,1)S(1)}, bf16[14,32,128]{2,1,0:T(8,128)(2,1)S(1)}, u32[]{:S(2)}, u32[]{:S(2)}) collective-permute-start(bf16[14,32,128]{2,1,0:T(8,128)(2,1)S(1)} %add_convert_fusion.1.refs_0_), channel_id=1, source_target_pairs={{0,8},{2,10},{4,12},{6,14},{8,0},{10,2},{12,4},{14,6},{16,24},{18,... | collective-permute-start | bytes 344072 | tf_op jit(solution)/shard_map/ppermute | solution.py:343
  30.7 7.4 %collective-permute-start.12 = (bf16[14,32,128]{2,1,0:T(8,128)(2,1)S(1)}, bf16[14,32,128]{2,1,0:T(8,128)(2,1)S(1)}, u32[]{:S(2)}, u32[]{:S(2)}) collective-permute-start(bf16[14,32,128]{2,1,0:T(8,128)(2,1)S(1)} %add_convert_fusion.1.refs_0_), channel_id=1, source_target_pairs={{0,4},{2,6},{4,0},{6,2},{8,12},{10,14},{12,8},{14,10},{16,20},{18,... | collective-permute-start | bytes 344072 | tf_op jit(solution)/shard_map/ppermute | solution.py:343
  33.4 7.1 %collective-permute-start.18 = (bf16[14,32,128]{2,1,0:T(8,128)(2,1)S(1)}, bf16[14,32,128]{2,1,0:T(8,128)(2,1)S(1)}, u32[]{:S(2)}, u32[]{:S(2)}) collective-permute-start(bf16[14,32,128]{2,1,0:T(8,128)(2,1)S(1)} %add_convert_fusion.refs_5_), channel_id=1, source_target_pairs={{0,12},{2,14},{4,8},{6,10},{8,4},{10,6},{12,0},{14,2},{16,28},{18,... | collective-permute-start | bytes 344072 | tf_op jit(solution)/shard_map/ppermute | solution.py:343
  35.0 6.8 %collective-permute-start.17 = (bf16[14,32,128]{2,1,0:T(8,128)(2,1)S(1)}, bf16[14,32,128]{2,1,0:T(8,128)(2,1)S(1)}, u32[]{:S(2)}, u32[]{:S(2)}) collective-permute-start(bf16[14,32,128]{2,1,0:T(8,128)(2,1)S(1)} %add_convert_fusion.refs_5_), channel_id=1, source_target_pairs={{0,8},{2,10},{4,12},{6,14},{8,0},{10,2},{12,4},{14,6},{16,24},{18,... | collective-permute-start | bytes 344072 | tf_op jit(solution)/shard_map/ppermute | solution.py:343
  36.0 5.8 %collective-permute-start.16 = (bf16[14,32,128]{2,1,0:T(8,128)(2,1)S(1)}, bf16[14,32,128]{2,1,0:T(8,128)(2,1)S(1)}, u32[]{:S(2)}, u32[]{:S(2)}) collective-permute-start(bf16[14,32,128]{2,1,0:T(8,128)(2,1)S(1)} %add_convert_fusion.refs_5_), channel_id=1, source_target_pairs={{0,4},{2,6},{4,0},{6,2},{8,12},{10,14},{12,8},{14,10},{16,20},{18,... | collective-permute-start | bytes 344072 | tf_op jit(solution)/shard_map/ppermute | solution.py:343
  38.2 3.7 %collective-permute-start.15 = (bf16[56,32,128]{2,1,0:T(8,128)(2,1)S(1)}, bf16[56,32,128]{2,1,0:T(8,128)(2,1)S(1)}, u32[]{:S(2)}, u32[]{:S(2)}) collective-permute-start(bf16[56,32,128]{2,1,0:T(8,128)(2,1)S(1)} %pad_maximum_fusion), channel_id=1, source_target_pairs={{0,2},{2,0},{4,6},{6,4},{8,10},{10,8},{12,14},{14,12},{16,18},{18,... | collective-permute-start | bytes 1376264 | tf_op jit(solution)/shard_map/ppermute | solution.py:343
  41.9 1.9 %collective-permute-start.19 = (bf16[56,32,128]{2,1,0:T(8,128)(2,1)S(1)}, bf16[56,32,128]{2,1,0:T(8,128)(2,1)S(1)}, u32[]{:S(2)}, u32[]{:S(2)}) collective-permute-start(bf16[56,32,128]{2,1,0:T(8,128)(2,1)S(1)} %pad_maximum_fusion.1), channel_id=1, source_target_pairs={{0,2},{2,0},{4,6},{6,4},{8,10},{10,8},{12,14},{14,12},{16,18},{18,... | collective-permute-start | bytes 1376264 | tf_op jit(solution)/shard_map/ppermute | solution.py:343

commit v5 on v4

--- a/solution.py
+++ b/solution.py
@@ -369,7 +369,7 @@
     *got, part, grad = lax.optimization_barrier((*got, part, grad))
     (back,) = vmem_call(functools.partial(sample_kernel, half, True), (shape((10 * cells, LANES)),))(other, weights)
 
-    splits = (count // 2, count - count // 2)
+    splits = (count // 2 + 1, count - count // 2 - 1)
     totals = []
     for index, taps in enumerate(splits):
         keep, give = vmem_call(

time: 45 us -> 44.7 us (level)
  transfers between devices with their start and end apart: 20 -> 20, of which waited for: 10 -> 11; matrix products, arithmetic and copies ran while one was open for 1% -> 1% of each run, Pallas kernels for 12% -> 13%
where the time goes in v5:
time: 44.7 us; the launch traced here: 44.4 us
  starting transfers between devices  22.6 us (51%)
  waiting for transfers between devices  9.59 us (21%)
  Pallas kernels  7.97 us (18%)
  local copies, waits for them, and re-layouts  3.21 us (7%)
  between operations  0.78 us (2%)
    ppermute x14, starting transfers between devices, across(): lax.ppermute(value, 'dp', [(i, i ^ distance) for i in range(groups_of)])  14.5 us
    ppermute x4, starting transfers between devices, deliver(): return lax.ppermute(value, ('dp', 'shard'), pairs)  6.08 us
    ppermute x14, waiting for transfers between devices, across(): lax.ppermute(value, 'dp', [(i, i ^ distance) for i in range(groups_of)])  4.95 us
    unnamed x8, local copies, waits for them, and re-layouts  3.21 us
    ppermute x4, waiting for transfers between devices, deliver(): return lax.ppermute(value, ('dp', 'shard'), pairs)  3.09 us
    pallas_call x2, Pallas kernels, put(): pl.pallas_call(functools.partial(place_kernel, parts, width, runs, len(ha...  2.64 us
    ppermute x2, starting transfers between devices, swap(): return lax.ppermute(value, 'shard', [(0, 1), (1, 0)])  2.05 us
    ppermute x2, waiting for transfers between devices, swap(): return lax.ppermute(value, 'shard', [(0, 1), (1, 0)])  1.55 us
  transfers between devices with their start and end apart: 20, of which 11 were waited for; matrix products, arithmetic and copies ran while one was open for 1% of the time, Pallas kernels for 13%

profile of v5, /device:TPU:0, one launch (start us, length us, event | category | flops | bytes accessed | tf_op | source)
XLA Modules:
  0.0 44.4 jit_solution(4040671379944972620)
XLA Ops:
  0.6 0.5 %collective-permute-start = (bf16[512,256]{1,0:T(8,128)(2,1)}, bf16[512,256]{1,0:T(8,128)(2,1)S(1)}, u32[]{:S(2)}, u32[]{:S(2)}) collective-permute-start(bf16[512,256]{1,0:T(8,128)(2,1)} %bitcast.4), channel_id=1, source_target_pairs={{0,2},{2,0},{4,6},{6,4},{8,10},{10,8},{12,14},{14,12},{16,18},{18,... | collective-permute-start | bytes 786440 | tf_op jit(solution)/shard_map/ppermute | solution.py:343
  1.1 0.1 collective-permute-start.1
  1.2 0.0 copy-start.2
  1.2 0.9 %copy-done.2 = bf16[1,8,8,8,256]{4,3,2,1,0:T(8,128)(2,1)S(1)} copy-done((bf16[1,8,8,8,256]{4,3,2,1,0:T(8,128)(2,1)S(1)}, bf16[1,8,8,8,256]{4,3,2,1,0:T(8,128)(2,1)}, u32[]{:S(2)}) %copy-start.2) | copy-done | bytes 262168
  2.2 0.3 shard_map.58
  2.5 0.1 collective-permute-done.1.cot2_ref
  2.6 0.0 collective-permute-done.x2_ref
  2.6 0.0 copy-start.3
  2.6 0.8 %copy-done.3 = bf16[1,4,4,4,256]{4,3,2,1,0:T(4,128)(2,1)S(1)} copy-done((bf16[1,4,4,4,256]{4,3,2,1,0:T(4,128)(2,1)S(1)}, bf16[1,4,4,4,256]{4,3,2,1,0:T(4,128)(2,1)}, u32[]{:S(2)}) %copy-start.3) | copy-done | bytes 32792
  3.3 0.7 %shard_map.59 = (bf16[512,128]{1,0:T(8,128)(2,1)S(1)}, bf16[512,128]{1,0:T(8,128)(2,1)S(1)}, bf16[512,128]{1,0:T(8,128)(2,1)S(1)}, bf16[512,128]{1,0:T(8,128)(2,...) custom-call(bf16[512,128]{1,0:T(8,128)(2,1)S(1)} %get-tuple-element.34.keep_ref, ...), custom_call_target="tpu_custom_call" | custom-call | bytes 1048576 | tf_op jit(solution)/shard_map/pallas_call | solution.py:358
  4.1 3.9 %collective-permute-start.2 = (bf16[512,128]{1,0:T(8,128)(2,1)S(1)}, bf16[512,128]{1,0:T(8,128)(2,1)S(1)}, u32[]{:S(2)}, u32[]{:S(2)}) collective-permute-start(bf16[512,128]{1,0:T(8,128)(2,1)S(1)} %get-tuple-element.36), channel_id=1, source_target_pairs={{0,5},{1,4},{2,6},{3,7},{4,1},{5,0},{6,2},{7,3},{8,13},{9,12},{10,... | collective-permute-start | bytes 393224 | tf_op jit(solution)/shard_map/ppermute | solution.py:354
  8.0 1.5 %collective-permute-start.3 = (bf16[512,128]{1,0:T(8,128)(2,1)S(1)}, bf16[512,128]{1,0:T(8,128)(2,1)S(1)}, u32[]{:S(2)}, u32[]{:S(2)}) collective-permute-start(bf16[512,128]{1,0:T(8,128)(2,1)S(1)} %get-tuple-element.37), channel_id=1, source_target_pairs={{0,9},{1,8},{2,10},{3,11},{4,13},{5,12},{6,14},{7,15},{8,1},{9,0},... | collective-permute-start | bytes 393224 | tf_op jit(solution)/shard_map/ppermute | solution.py:354
  9.5 0.0 collective-permute-start.4
  9.5 0.7 %collective-permute-start.5 = (bf16[512,128]{1,0:T(8,128)(2,1)S(1)}, bf16[512,128]{1,0:T(8,128)(2,1)S(1)}, u32[]{:S(2)}, u32[]{:S(2)}) collective-permute-start(bf16[512,128]{1,0:T(8,128)(2,1)S(1)} %get-tuple-element.39), channel_id=1, source_target_pairs={{0,0},{1,1},{2,3},{3,2},{4,4},{5,5},{6,7},{7,6},{8,8},{9,9},{10,11... | collective-permute-start | bytes 393224 | tf_op jit(solution)/shard_map/ppermute | solution.py:354
  10.2 0.0 copy-start
  10.2 1.5 %copy-done = bf16[28,128,256]{2,1,0:T(8,128)(2,1)S(1)} copy-done((bf16[28,128,256]{2,1,0:T(8,128)(2,1)S(1)}, bf16[28,128,256]{2,1,0:T(8,128)(2,1)}, u32[]{:S(2)}) %copy-start) | copy-done | bytes 1835032
  11.7 0.0 copy-start.1
  11.7 1.0 %shard_map.60 = (f32[64,256]{1,0:T(8,128)S(1)}, bf16[512,128]{1,0:T(8,128)(2,1)S(1)}) custom-call(bf16[640,128]{1,0:T(8,128)(2,1)S(1)} %get-tuple-element.40.own_ref, bf16[28,128,256]{2,1,0:T(8,128)(2,1)S(1)} %copy-done), custom_call_target="tpu_custom_call" | custom-call | bytes 1048576 | tf_op jit(solution)/shard_map/pallas_call | solution.py:365
  12.6 0.0 collective-permute-done.2.refs_0_
  12.6 2.4 %collective-permute-done.3.refs_1_ = bf16[512,128]{1,0:T(8,128)(2,1)S(1)} collective-permute-done((bf16[512,128]{1,0:T(8,128)(2,1)S(1)}, bf16[512,128]{1,0:T(8,128)(2,1)S(1)}, u32[]{:S(2)}, u32[]{:S(2)}) %collective-permute-start.3) | collective-permute-done | bytes 131104 | tf_op jit(solution)/shard_map/ppermute | solution.py:354
  15.1 0.7 %collective-permute-done.4.refs_2_ = bf16[512,128]{1,0:T(8,128)(2,1)S(1)} collective-permute-done((bf16[512,128]{1,0:T(8,128)(2,1)S(1)}, bf16[512,128]{1,0:T(8,128)(2,1)S(1)}, u32[]{:S(2)}, u32[]{:S(2)}) %collective-permute-start.4) | collective-permute-done | bytes 131104 | tf_op jit(solution)/shard_map/ppermute | solution.py:354
  15.7 0.0 collective-permute-done.5.refs_3_
  15.7 0.7 %shard_map.61 = (f32[15,32,128]{2,1,0:T(8,128)S(1)}, bf16[15,32,128]{2,1,0:T(8,128)(2,1)S(1)}) custom-call(bf16[512,128]{1,0:T(8,128)(2,1)S(1)} %collective-permute-done.2.refs_0_, bf16[512,128]{1,0:T(8,128)(2,1)S(1)} %collective-permute-done.3.refs_1_, bf16[512,128]{1,0:T(8,128)(2,1)S(1)} %collective-permute-done.4.refs_2_, ...), custom_call_target="tpu_custom_call" | custom-call | bytes 1048576 | tf_op jit(solution)/shard_map/pallas_call | solution.py:375
  16.4 0.9 %collective-permute-start.6 = (bf16[15,32,128]{2,1,0:T(8,128)(2,1)S(1)}, bf16[15,32,128]{2,1,0:T(8,128)(2,1)S(1)}, u32[]{:S(2)}, u32[]{:S(2)}) collective-permute-start(bf16[15,32,128]{2,1,0:T(8,128)(2,1)S(1)} %get-tuple-element.48), channel_id=1, source_target_pairs={{0,2},{2,0},{4,6},{6,4},{8,10},{10,8},{12,14},{14,12},{16,18},{18,... | collective-permute-start | bytes 368648 | tf_op jit(solution)/shard_map/ppermute | solution.py:343
  17.3 0.9 %collective-permute-start.9 = (bf16[640,128]{1,0:T(8,128)(2,1)S(1)}, bf16[640,128]{1,0:T(8,128)(2,1)S(1)}, u32[]{:S(2)}, u32[]{:S(2)}) collective-permute-start(bf16[640,128]{1,0:T(8,128)(2,1)S(1)} %get-tuple-element.58), channel_id=1, source_target_pairs={{0,1},{1,0},{2,3},{3,2},{4,5},{5,4},{6,7},{7,6},{8,9},{9,8},{10,11... | collective-permute-start | bytes 491528 | tf_op jit(solution)/shard_map/ppermute | solution.py:346
  18.2 0.1 collective-permute-done.6
  18.3 0.6 %shard_map.62 = (f32[13,32,128]{2,1,0:T(8,128)S(1)}, bf16[13,32,128]{2,1,0:T(8,128)(2,1)S(1)}) custom-call(bf16[512,128]{1,0:T(8,128)(2,1)S(1)} %collective-permute-done.2.refs_0_, bf16[512,128]{1,0:T(8,128)(2,1)S(1)} %collective-permute-done.3.refs_1_, bf16[512,128]{1,0:T(8,128)(2,1)S(1)} %collective-permute-done.4.refs_2_, ...), custom_call_target="tpu_custom_call" | custom-call | bytes 1048576 | tf_op jit(solution)/shard_map/pallas_call | solution.py:375
  18.9 0.4 collective-permute-start.7
  19.3 2.6 %collective-permute-start.11 = (bf16[15,32,128]{2,1,0:T(8,128)(2,1)S(1)}, bf16[15,32,128]{2,1,0:T(8,128)(2,1)S(1)}, u32[]{:S(2)}, u32[]{:S(2)}) collective-permute-start(bf16[15,32,128]{2,1,0:T(8,128)(2,1)S(1)} %add_convert_fusion.1), channel_id=1, source_target_pairs={{0,16},{2,18},{4,20},{6,22},{8,24},{10,26},{12,28},{14,30},{16,0},... | collective-permute-start | bytes 368648 | tf_op jit(solution)/shard_map/ppermute | solution.py:343
  21.9 1.6 %collective-permute-done.9.own_ref = bf16[640,128]{1,0:T(8,128)(2,1)S(1)} collective-permute-done((bf16[640,128]{1,0:T(8,128)(2,1)S(1)}, bf16[640,128]{1,0:T(8,128)(2,1)S(1)}, u32[]{:S(2)}, u32[]{:S(2)}) %collective-permute-start.9) | collective-permute-done | bytes 163872 | tf_op jit(solution)/shard_map/ppermute | solution.py:346
  23.5 0.0 copy-done.1
  23.5 1.0 %shard_map.63 = bf16[640,128]{1,0:T(8,128)(2,1)S(1)} custom-call(bf16[640,128]{1,0:T(8,128)(2,1)S(1)} %collective-permute-done.9.own_ref, bf16[28,128,256]{2,1,0:T(8,128)(2,1)S(1)} %copy-done.1), custom_call_target="tpu_custom_call" | custom-call | bytes 1048576 | tf_op jit(solution)/shard_map/pallas_call | solution.py:370
  24.5 1.1 %collective-permute-start.10 = (bf16[640,128]{1,0:T(8,128)(2,1)S(1)}, bf16[640,128]{1,0:T(8,128)(2,1)S(1)}, u32[]{:S(2)}, u32[]{:S(2)}) collective-permute-start(bf16[640,128]{1,0:T(8,128)(2,1)S(1)} %shard_map.63), channel_id=1, source_target_pairs={{0,1},{1,0},{2,3},{3,2},{4,5},{5,4},{6,7},{7,6},{8,9},{9,8},{10,11... | collective-permute-start | bytes 491528 | tf_op jit(solution)/shard_map/ppermute | solution.py:346
  25.6 0.0 collective-permute-done.7
  25.6 2.7 %collective-permute-start.8 = (bf16[13,32,128]{2,1,0:T(8,128)(2,1)S(1)}, bf16[13,32,128]{2,1,0:T(8,128)(2,1)S(1)}, u32[]{:S(2)}, u32[]{:S(2)}) collective-permute-start(bf16[13,32,128]{2,1,0:T(8,128)(2,1)S(1)} %add_convert_fusion.3), channel_id=1, source_target_pairs={{0,16},{2,18},{4,20},{6,22},{8,24},{10,26},{12,28},{14,30},{16,0},... | collective-permute-start | bytes 319496 | tf_op jit(solution)/shard_map/ppermute | solution.py:343
  28.3 0.0 collective-permute-done.11
  28.3 2.0 %collective-permute-start.14 = (bf16[15,32,128]{2,1,0:T(8,128)(2,1)S(1)}, bf16[15,32,128]{2,1,0:T(8,128)(2,1)S(1)}, u32[]{:S(2)}, u32[]{:S(2)}) collective-permute-start(bf16[15,32,128]{2,1,0:T(8,128)(2,1)S(1)} %add_convert_fusion.refs_0_), channel_id=1, source_target_pairs={{0,12},{2,14},{4,8},{6,10},{8,4},{10,6},{12,0},{14,2},{16,28},{18,... | collective-permute-start | bytes 368648 | tf_op jit(solution)/shard_map/ppermute | solution.py:343
  30.3 0.6 %collective-permute-start.13 = (bf16[15,32,128]{2,1,0:T(8,128)(2,1)S(1)}, bf16[15,32,128]{2,1,0:T(8,128)(2,1)S(1)}, u32[]{:S(2)}, u32[]{:S(2)}) collective-permute-start(bf16[15,32,128]{2,1,0:T(8,128)(2,1)S(1)} %add_convert_fusion.refs_0_), channel_id=1, source_target_pairs={{0,8},{2,10},{4,12},{6,14},{8,0},{10,2},{12,4},{14,6},{16,24},{18,... | collective-permute-start | bytes 368648 | tf_op jit(solution)/shard_map/ppermute | solution.py:343
  30.9 1.0 %collective-permute-start.12 = (bf16[15,32,128]{2,1,0:T(8,128)(2,1)S(1)}, bf16[15,32,128]{2,1,0:T(8,128)(2,1)S(1)}, u32[]{:S(2)}, u32[]{:S(2)}) collective-permute-start(bf16[15,32,128]{2,1,0:T(8,128)(2,1)S(1)} %add_convert_fusion.refs_0_), channel_id=1, source_target_pairs={{0,4},{2,6},{4,0},{6,2},{8,12},{10,14},{12,8},{14,10},{16,20},{18,... | collective-permute-start | bytes 368648 | tf_op jit(solution)/shard_map/ppermute | solution.py:343
  31.9 0.0 collective-permute-done.10.got_ref
  31.9 1.1 %shard_map.64 = (bf16[4,4,4,256]{3,2,1,0:T(4,128)(2,1)}, bf16[512,256]{1,0:T(8,128)(2,1)}) custom-call(f32[64,256]{1,0:T(8,128)S(1)} %get-tuple-element.55.part_ref, bf16[512,128]{1,0:T(8,128)(2,1)S(1)} %get-tuple-element.56.grad_ref, bf16[640,128]{1,0:T(8,128)(2,1)S(1)} %collective-permute-done.10.got_ref), custom_call_target="tpu_custom_call" | custom-call | bytes 1048576 | tf_op jit(solution)/shard_map/pallas_call | solution.py:383
  33.0 0.0 collective-permute-done.8
  33.0 2.0 %collective-permute-start.18 = (bf16[13,32,128]{2,1,0:T(8,128)(2,1)S(1)}, bf16[13,32,128]{2,1,0:T(8,128)(2,1)S(1)}, u32[]{:S(2)}, u32[]{:S(2)}) collective-permute-start(bf16[13,32,128]{2,1,0:T(8,128)(2,1)S(1)} %add_convert_fusion.2.refs_5_), channel_id=1, source_target_pairs={{0,12},{2,14},{4,8},{6,10},{8,4},{10,6},{12,0},{14,2},{16,28},{18,... | collective-permute-start | bytes 319496 | tf_op jit(solution)/shard_map/ppermute | solution.py:343
  35.0 0.6 %collective-permute-start.17 = (bf16[13,32,128]{2,1,0:T(8,128)(2,1)S(1)}, bf16[13,32,128]{2,1,0:T(8,128)(2,1)S(1)}, u32[]{:S(2)}, u32[]{:S(2)}) collective-permute-start(bf16[13,32,128]{2,1,0:T(8,128)(2,1)S(1)} %add_convert_fusion.2.refs_5_), channel_id=1, source_target_pairs={{0,8},{2,10},{4,12},{6,14},{8,0},{10,2},{12,4},{14,6},{16,24},{18,... | collective-permute-start | bytes 319496 | tf_op jit(solution)/shard_map/ppermute | solution.py:343
  35.6 0.4 collective-permute-done.14.refs_3_
  36.0 1.1 %collective-permute-start.16 = (bf16[13,32,128]{2,1,0:T(8,128)(2,1)S(1)}, bf16[13,32,128]{2,1,0:T(8,128)(2,1)S(1)}, u32[]{:S(2)}, u32[]{:S(2)}) collective-permute-start(bf16[13,32,128]{2,1,0:T(8,128)(2,1)S(1)} %add_convert_fusion.2.refs_5_), channel_id=1, source_target_pairs={{0,4},{2,6},{4,0},{6,2},{8,12},{10,14},{12,8},{14,10},{16,20},{18,... | collective-permute-start | bytes 319496 | tf_op jit(solution)/shard_map/ppermute | solution.py:343
  37.1 1.2 %collective-permute-done.13.refs_2_ = bf16[15,32,128]{2,1,0:T(8,128)(2,1)S(1)} collective-permute-done((bf16[15,32,128]{2,1,0:T(8,128)(2,1)S(1)}, bf16[15,32,128]{2,1,0:T(8,128)(2,1)S(1)}, u32[]{:S(2)}, u32[]{:S(2)}) %collective-permute-start.13) | collective-permute-done | bytes 122912 | tf_op jit(solution)/shard_map/ppermute | solution.py:343
  38.3 0.4 collective-permute-done.12.refs_1_
  38.7 0.1 pad_maximum_fusion
  38.7 0.1 collective-permute-start.15
  38.8 2.0 %collective-permute-done.18.refs_8_ = bf16[13,32,128]{2,1,0:T(8,128)(2,1)S(1)} collective-permute-done((bf16[13,32,128]{2,1,0:T(8,128)(2,1)S(1)}, bf16[13,32,128]{2,1,0:T(8,128)(2,1)S(1)}, u32[]{:S(2)}, u32[]{:S(2)}) %collective-permute-start.18) | collective-permute-done | bytes 106528 | tf_op jit(solution)/shard_map/ppermute | solution.py:343
  40.8 0.8 %collective-permute-done.17.refs_7_ = bf16[13,32,128]{2,1,0:T(8,128)(2,1)S(1)} collective-permute-done((bf16[13,32,128]{2,1,0:T(8,128)(2,1)S(1)}, bf16[13,32,128]{2,1,0:T(8,128)(2,1)S(1)}, u32[]{:S(2)}, u32[]{:S(2)}) %collective-permute-start.17) | collective-permute-done | bytes 106528 | tf_op jit(solution)/shard_map/ppermute | solution.py:343
  41.6 0.0 collective-permute-done.16.refs_6_
  41.6 0.1 pad_maximum_fusion.1
  41.6 0.1 collective-permute-start.19
  41.7 0.0 collective-permute-done.15.refs_4_
  41.7 1.7 %shard_map.65.refs_0_ = f32[28,128,256]{2,1,0:T(8,128)} custom-call(bf16[15,32,128]{2,1,0:T(8,128)(2,1)S(1)} %add_convert_fusion.refs_0_, bf16[15,32,128]{2,1,0:T(8,128)(2,1)S(1)} %collective-permute-done.12.refs_1_, bf16[15,32,128]{2,1,0:T(8,128)(2,1)S(1)} %collective-permute-done.13.refs_2_, bf16[15,32,128]{2,1,0:T(8,128)(2,1)S(1)} %collective-permute-done.14.refs_3_, ...), custom_call_target="tpu_custom_call" | custom-call | tf_op jit(solution)/shard_map/pallas_call | solution.py:403
  43.4 0.1 collective-permute-done.19.refs_1_
  43.5 1.0 %shard_map.66 = f32[28,128,256]{2,1,0:T(8,128)} custom-call(f32[28,128,256]{2,1,0:T(8,128)} %shard_map.65.refs_0_, bf16[52,32,128]{2,1,0:T(8,128)(2,1)S(1)} %collective-permute-done.19.refs_1_), custom_call_target="tpu_custom_call", output_to_operand_aliasing={{}: (0, {})} | custom-call | tf_op jit(solution)/shard_map/pallas_call | solution.py:403
  (4 shorter events, 0.1 us)
Async XLA Ops:
  0.6 1.9 %collective-permute-start = (bf16[512,256]{1,0:T(8,128)(2,1)}, bf16[512,256]{1,0:T(8,128)(2,1)S(1)}, u32[]{:S(2)}, u32[]{:S(2)}) collective-permute-start(bf16[512,256]{1,0:T(8,128)(2,1)} %bitcast.4), channel_id=1, source_target_pairs={{0,2},{2,0},{4,6},{6,4},{8,10},{10,8},{12,14},{14,12},{16,18},{18,... | collective-permute-start | bytes 786440 | tf_op jit(solution)/shard_map/ppermute | solution.py:343
  1.1 1.4 %collective-permute-start.1 = (bf16[4,4,4,256]{3,2,1,0:T(4,128)(2,1)}, bf16[4,4,4,256]{3,2,1,0:T(4,128)(2,1)S(1)}, u32[]{:S(2)}, u32[]{:S(2)}) collective-permute-start(bf16[4,4,4,256]{3,2,1,0:T(4,128)(2,1)} %bitcast.6), channel_id=1, source_target_pairs={{0,2},{2,0},{4,6},{6,4},{8,10},{10,8},{12,14},{14,12},{16,18},{18,... | collective-permute-start | bytes 98312 | tf_op jit(solution)/shard_map/ppermute | solution.py:343
  1.2 0.9 %copy-start.2 = (bf16[1,8,8,8,256]{4,3,2,1,0:T(8,128)(2,1)S(1)}, bf16[1,8,8,8,256]{4,3,2,1,0:T(8,128)(2,1)}, u32[]{:S(2)}) copy-start(bf16[1,8,8,8,256]{4,3,2,1,0:T(8,128)(2,1)} %param.3) | copy-start | bytes 786436
  2.6 0.8 %copy-start.3 = (bf16[1,4,4,4,256]{4,3,2,1,0:T(4,128)(2,1)S(1)}, bf16[1,4,4,4,256]{4,3,2,1,0:T(4,128)(2,1)}, u32[]{:S(2)}) copy-start(bf16[1,4,4,4,256]{4,3,2,1,0:T(4,128)(2,1)} %param.4) | copy-start | bytes 98308
  4.1 8.6 %collective-permute-start.2 = (bf16[512,128]{1,0:T(8,128)(2,1)S(1)}, bf16[512,128]{1,0:T(8,128)(2,1)S(1)}, u32[]{:S(2)}, u32[]{:S(2)}) collective-permute-start(bf16[512,128]{1,0:T(8,128)(2,1)S(1)} %get-tuple-element.36), channel_id=1, source_target_pairs={{0,5},{1,4},{2,6},{3,7},{4,1},{5,0},{6,2},{7,3},{8,13},{9,12},{10,... | collective-permute-start | bytes 393224 | tf_op jit(solution)/shard_map/ppermute | solution.py:354
  8.0 7.1 %collective-permute-start.3 = (bf16[512,128]{1,0:T(8,128)(2,1)S(1)}, bf16[512,128]{1,0:T(8,128)(2,1)S(1)}, u32[]{:S(2)}, u32[]{:S(2)}) collective-permute-start(bf16[512,128]{1,0:T(8,128)(2,1)S(1)} %get-tuple-element.37), channel_id=1, source_target_pairs={{0,9},{1,8},{2,10},{3,11},{4,13},{5,12},{6,14},{7,15},{8,1},{9,0},... | collective-permute-start | bytes 393224 | tf_op jit(solution)/shard_map/ppermute | solution.py:354
  9.5 6.3 %collective-permute-start.4 = (bf16[512,128]{1,0:T(8,128)(2,1)S(1)}, bf16[512,128]{1,0:T(8,128)(2,1)S(1)}, u32[]{:S(2)}, u32[]{:S(2)}) collective-permute-start(bf16[512,128]{1,0:T(8,128)(2,1)S(1)} %get-tuple-element.38), channel_id=1, source_target_pairs={{0,12},{1,13},{2,15},{3,14},{4,8},{5,9},{6,11},{7,10},{8,4},{9,5},... | collective-permute-start | bytes 393224 | tf_op jit(solution)/shard_map/ppermute | solution.py:354
  9.5 6.2 %collective-permute-start.5 = (bf16[512,128]{1,0:T(8,128)(2,1)S(1)}, bf16[512,128]{1,0:T(8,128)(2,1)S(1)}, u32[]{:S(2)}, u32[]{:S(2)}) collective-permute-start(bf16[512,128]{1,0:T(8,128)(2,1)S(1)} %get-tuple-element.39), channel_id=1, source_target_pairs={{0,0},{1,1},{2,3},{3,2},{4,4},{5,5},{6,7},{7,6},{8,8},{9,9},{10,11... | collective-permute-start | bytes 393224 | tf_op jit(solution)/shard_map/ppermute | solution.py:354
  10.2 1.5 %copy-start = (bf16[28,128,256]{2,1,0:T(8,128)(2,1)S(1)}, bf16[28,128,256]{2,1,0:T(8,128)(2,1)}, u32[]{:S(2)}) copy-start(bf16[28,128,256]{2,1,0:T(8,128)(2,1)} %w_ref.3) | copy-start | bytes 5505028
  11.7 11.8 %copy-start.1 = (bf16[28,128,256]{2,1,0:T(8,128)(2,1)S(1)}, bf16[28,128,256]{2,1,0:T(8,128)(2,1)}, u32[]{:S(2)}) copy-start(bf16[28,128,256]{2,1,0:T(8,128)(2,1)} %w_ref.3) | copy-start | bytes 5505028
  16.4 1.9 %collective-permute-start.6 = (bf16[15,32,128]{2,1,0:T(8,128)(2,1)S(1)}, bf16[15,32,128]{2,1,0:T(8,128)(2,1)S(1)}, u32[]{:S(2)}, u32[]{:S(2)}) collective-permute-start(bf16[15,32,128]{2,1,0:T(8,128)(2,1)S(1)} %get-tuple-element.48), channel_id=1, source_target_pairs={{0,2},{2,0},{4,6},{6,4},{8,10},{10,8},{12,14},{14,12},{16,18},{18,... | collective-permute-start | bytes 368648 | tf_op jit(solution)/shard_map/ppermute | solution.py:343
  17.3 6.2 %collective-permute-start.9 = (bf16[640,128]{1,0:T(8,128)(2,1)S(1)}, bf16[640,128]{1,0:T(8,128)(2,1)S(1)}, u32[]{:S(2)}, u32[]{:S(2)}) collective-permute-start(bf16[640,128]{1,0:T(8,128)(2,1)S(1)} %get-tuple-element.58), channel_id=1, source_target_pairs={{0,1},{1,0},{2,3},{3,2},{4,5},{5,4},{6,7},{7,6},{8,9},{9,8},{10,11... | collective-permute-start | bytes 491528 | tf_op jit(solution)/shard_map/ppermute | solution.py:346
  18.9 6.7 %collective-permute-start.7 = (bf16[13,32,128]{2,1,0:T(8,128)(2,1)S(1)}, bf16[13,32,128]{2,1,0:T(8,128)(2,1)S(1)}, u32[]{:S(2)}, u32[]{:S(2)}) collective-permute-start(bf16[13,32,128]{2,1,0:T(8,128)(2,1)S(1)} %get-tuple-element.54), channel_id=1, source_target_pairs={{0,2},{2,0},{4,6},{6,4},{8,10},{10,8},{12,14},{14,12},{16,18},{18,... | collective-permute-start | bytes 319496 | tf_op jit(solution)/shard_map/ppermute | solution.py:343
  19.3 8.9 %collective-permute-start.11 = (bf16[15,32,128]{2,1,0:T(8,128)(2,1)S(1)}, bf16[15,32,128]{2,1,0:T(8,128)(2,1)S(1)}, u32[]{:S(2)}, u32[]{:S(2)}) collective-permute-start(bf16[15,32,128]{2,1,0:T(8,128)(2,1)S(1)} %add_convert_fusion.1), channel_id=1, source_target_pairs={{0,16},{2,18},{4,20},{6,22},{8,24},{10,26},{12,28},{14,30},{16,0},... | collective-permute-start | bytes 368648 | tf_op jit(solution)/shard_map/ppermute | solution.py:343
  24.5 7.4 %collective-permute-start.10 = (bf16[640,128]{1,0:T(8,128)(2,1)S(1)}, bf16[640,128]{1,0:T(8,128)(2,1)S(1)}, u32[]{:S(2)}, u32[]{:S(2)}) collective-permute-start(bf16[640,128]{1,0:T(8,128)(2,1)S(1)} %shard_map.63), channel_id=1, source_target_pairs={{0,1},{1,0},{2,3},{3,2},{4,5},{5,4},{6,7},{7,6},{8,9},{9,8},{10,11... | collective-permute-start | bytes 491528 | tf_op jit(solution)/shard_map/ppermute | solution.py:346
  25.6 7.4 %collective-permute-start.8 = (bf16[13,32,128]{2,1,0:T(8,128)(2,1)S(1)}, bf16[13,32,128]{2,1,0:T(8,128)(2,1)S(1)}, u32[]{:S(2)}, u32[]{:S(2)}) collective-permute-start(bf16[13,32,128]{2,1,0:T(8,128)(2,1)S(1)} %add_convert_fusion.3), channel_id=1, source_target_pairs={{0,16},{2,18},{4,20},{6,22},{8,24},{10,26},{12,28},{14,30},{16,0},... | collective-permute-start | bytes 319496 | tf_op jit(solution)/shard_map/ppermute | solution.py:343
  28.3 7.7 %collective-permute-start.14 = (bf16[15,32,128]{2,1,0:T(8,128)(2,1)S(1)}, bf16[15,32,128]{2,1,0:T(8,128)(2,1)S(1)}, u32[]{:S(2)}, u32[]{:S(2)}) collective-permute-start(bf16[15,32,128]{2,1,0:T(8,128)(2,1)S(1)} %add_convert_fusion.refs_0_), channel_id=1, source_target_pairs={{0,12},{2,14},{4,8},{6,10},{8,4},{10,6},{12,0},{14,2},{16,28},{18,... | collective-permute-start | bytes 368648 | tf_op jit(solution)/shard_map/ppermute | solution.py:343
  30.3 8.0 %collective-permute-start.13 = (bf16[15,32,128]{2,1,0:T(8,128)(2,1)S(1)}, bf16[15,32,128]{2,1,0:T(8,128)(2,1)S(1)}, u32[]{:S(2)}, u32[]{:S(2)}) collective-permute-start(bf16[15,32,128]{2,1,0:T(8,128)(2,1)S(1)} %add_convert_fusion.refs_0_), channel_id=1, source_target_pairs={{0,8},{2,10},{4,12},{6,14},{8,0},{10,2},{12,4},{14,6},{16,24},{18,... | collective-permute-start | bytes 368648 | tf_op jit(solution)/shard_map/ppermute | solution.py:343
  30.9 7.8 %collective-permute-start.12 = (bf16[15,32,128]{2,1,0:T(8,128)(2,1)S(1)}, bf16[15,32,128]{2,1,0:T(8,128)(2,1)S(1)}, u32[]{:S(2)}, u32[]{:S(2)}) collective-permute-start(bf16[15,32,128]{2,1,0:T(8,128)(2,1)S(1)} %add_convert_fusion.refs_0_), channel_id=1, source_target_pairs={{0,4},{2,6},{4,0},{6,2},{8,12},{10,14},{12,8},{14,10},{16,20},{18,... | collective-permute-start | bytes 368648 | tf_op jit(solution)/shard_map/ppermute | solution.py:343
  33.0 7.8 %collective-permute-start.18 = (bf16[13,32,128]{2,1,0:T(8,128)(2,1)S(1)}, bf16[13,32,128]{2,1,0:T(8,128)(2,1)S(1)}, u32[]{:S(2)}, u32[]{:S(2)}) collective-permute-start(bf16[13,32,128]{2,1,0:T(8,128)(2,1)S(1)} %add_convert_fusion.2.refs_5_), channel_id=1, source_target_pairs={{0,12},{2,14},{4,8},{6,10},{8,4},{10,6},{12,0},{14,2},{16,28},{18,... | collective-permute-start | bytes 319496 | tf_op jit(solution)/shard_map/ppermute | solution.py:343
  35.0 6.6 %collective-permute-start.17 = (bf16[13,32,128]{2,1,0:T(8,128)(2,1)S(1)}, bf16[13,32,128]{2,1,0:T(8,128)(2,1)S(1)}, u32[]{:S(2)}, u32[]{:S(2)}) collective-permute-start(bf16[13,32,128]{2,1,0:T(8,128)(2,1)S(1)} %add_convert_fusion.2.refs_5_), channel_id=1, source_target_pairs={{0,8},{2,10},{4,12},{6,14},{8,0},{10,2},{12,4},{14,6},{16,24},{18,... | collective-permute-start | bytes 319496 | tf_op jit(solution)/shard_map/ppermute | solution.py:343
  36.0 5.5 %collective-permute-start.16 = (bf16[13,32,128]{2,1,0:T(8,128)(2,1)S(1)}, bf16[13,32,128]{2,1,0:T(8,128)(2,1)S(1)}, u32[]{:S(2)}, u32[]{:S(2)}) collective-permute-start(bf16[13,32,128]{2,1,0:T(8,128)(2,1)S(1)} %add_convert_fusion.2.refs_5_), channel_id=1, source_target_pairs={{0,4},{2,6},{4,0},{6,2},{8,12},{10,14},{12,8},{14,10},{16,20},{18,... | collective-permute-start | bytes 319496 | tf_op jit(solution)/shard_map/ppermute | solution.py:343
  38.7 3.0 %collective-permute-start.15 = (bf16[60,32,128]{2,1,0:T(8,128)(2,1)S(1)}, bf16[60,32,128]{2,1,0:T(8,128)(2,1)S(1)}, u32[]{:S(2)}, u32[]{:S(2)}) collective-permute-start(bf16[60,32,128]{2,1,0:T(8,128)(2,1)S(1)} %pad_maximum_fusion), channel_id=1, source_target_pairs={{0,2},{2,0},{4,6},{6,4},{8,10},{10,8},{12,14},{14,12},{16,18},{18,... | collective-permute-start | bytes 1474568 | tf_op jit(solution)/shard_map/ppermute | solution.py:343
  41.6 1.8 %collective-permute-start.19 = (bf16[52,32,128]{2,1,0:T(8,128)(2,1)S(1)}, bf16[52,32,128]{2,1,0:T(8,128)(2,1)S(1)}, u32[]{:S(2)}, u32[]{:S(2)}) collective-permute-start(bf16[52,32,128]{2,1,0:T(8,128)(2,1)S(1)} %pad_maximum_fusion.1), channel_id=1, source_target_pairs={{0,2},{2,0},{4,6},{6,4},{8,10},{10,8},{12,14},{14,12},{16,18},{18,... | collective-permute-start | bytes 1277960 | tf_op jit(solution)/shard_map/ppermute | solution.py:343

commit v6 on v5

--- a/solution.py
+++ b/solution.py
@@ -10,7 +10,7 @@
 LANES = 128
 PARTS = 8
 DELIVERY = (1, 2, 3, 0)
-GATHER = (2, 4, 6)
+GATHER = (4, 2, 6)
 BLOCK = 7
 VMEM_BYTES = 48 * 1024 * 1024
 BF16 = jnp.bfloat16

time: 44.7 us -> 44.7 us (level)
  no operation moved by 1% of the time
where the time goes in v6:
time: 44.7 us; the launch traced here: 44.4 us
  starting transfers between devices  22.8 us (51%)
  waiting for transfers between devices  9.45 us (21%)
  Pallas kernels  7.97 us (18%)
  local copies, waits for them, and re-layouts  3.21 us (7%)
  between operations  0.78 us (2%)
    ppermute x14, starting transfers between devices, across(): lax.ppermute(value, 'dp', [(i, i ^ distance) for i in range(groups_of)])  14.6 us
    ppermute x4, starting transfers between devices, deliver(): return lax.ppermute(value, ('dp', 'shard'), pairs)  6.08 us
    ppermute x14, waiting for transfers between devices, across(): lax.ppermute(value, 'dp', [(i, i ^ distance) for i in range(groups_of)])  4.81 us
    unnamed x8, local copies, waits for them, and re-layouts  3.21 us
    ppermute x4, waiting for transfers between devices, deliver(): return lax.ppermute(value, ('dp', 'shard'), pairs)  3.09 us
    pallas_call x2, Pallas kernels, put(): pl.pallas_call(functools.partial(place_kernel, parts, width, runs, len(ha...  2.64 us
    ppermute x2, starting transfers between devices, swap(): return lax.ppermute(value, 'shard', [(0, 1), (1, 0)])  2.05 us
    ppermute x2, waiting for transfers between devices, swap(): return lax.ppermute(value, 'shard', [(0, 1), (1, 0)])  1.55 us
  transfers between devices with their start and end apart: 20, of which 11 were waited for; matrix products, arithmetic and copies ran while one was open for 1% of the time, Pallas kernels for 13%

profile of v6, /device:TPU:0, one launch (start us, length us, event | category | flops | bytes accessed | tf_op | source)
XLA Modules:
  0.0 44.4 jit_solution(9244277361069140946)
XLA Ops:
  0.6 0.5 %collective-permute-start = (bf16[512,256]{1,0:T(8,128)(2,1)}, bf16[512,256]{1,0:T(8,128)(2,1)S(1)}, u32[]{:S(2)}, u32[]{:S(2)}) collective-permute-start(bf16[512,256]{1,0:T(8,128)(2,1)} %bitcast.4), channel_id=1, source_target_pairs={{0,2},{2,0},{4,6},{6,4},{8,10},{10,8},{12,14},{14,12},{16,18},{18,... | collective-permute-start | bytes 786440 | tf_op jit(solution)/shard_map/ppermute | solution.py:343
  1.1 0.1 collective-permute-start.1
  1.2 0.0 copy-start.2
  1.2 0.9 %copy-done.2 = bf16[1,8,8,8,256]{4,3,2,1,0:T(8,128)(2,1)S(1)} copy-done((bf16[1,8,8,8,256]{4,3,2,1,0:T(8,128)(2,1)S(1)}, bf16[1,8,8,8,256]{4,3,2,1,0:T(8,128)(2,1)}, u32[]{:S(2)}) %copy-start.2) | copy-done | bytes 262168
  2.2 0.3 shard_map.58
  2.5 0.1 collective-permute-done.1.cot2_ref
  2.6 0.0 collective-permute-done.x2_ref
  2.6 0.0 copy-start.3
  2.6 0.8 %copy-done.3 = bf16[1,4,4,4,256]{4,3,2,1,0:T(4,128)(2,1)S(1)} copy-done((bf16[1,4,4,4,256]{4,3,2,1,0:T(4,128)(2,1)S(1)}, bf16[1,4,4,4,256]{4,3,2,1,0:T(4,128)(2,1)}, u32[]{:S(2)}) %copy-start.3) | copy-done | bytes 32792
  3.3 0.7 %shard_map.59 = (bf16[512,128]{1,0:T(8,128)(2,1)S(1)}, bf16[512,128]{1,0:T(8,128)(2,1)S(1)}, bf16[512,128]{1,0:T(8,128)(2,1)S(1)}, bf16[512,128]{1,0:T(8,128)(2,...) custom-call(bf16[512,128]{1,0:T(8,128)(2,1)S(1)} %get-tuple-element.34.keep_ref, ...), custom_call_target="tpu_custom_call" | custom-call | bytes 1048576 | tf_op jit(solution)/shard_map/pallas_call | solution.py:358
  4.1 3.9 %collective-permute-start.2 = (bf16[512,128]{1,0:T(8,128)(2,1)S(1)}, bf16[512,128]{1,0:T(8,128)(2,1)S(1)}, u32[]{:S(2)}, u32[]{:S(2)}) collective-permute-start(bf16[512,128]{1,0:T(8,128)(2,1)S(1)} %get-tuple-element.36), channel_id=1, source_target_pairs={{0,5},{1,4},{2,6},{3,7},{4,1},{5,0},{6,2},{7,3},{8,13},{9,12},{10,... | collective-permute-start | bytes 393224 | tf_op jit(solution)/shard_map/ppermute | solution.py:354
  8.0 1.5 %collective-permute-start.3 = (bf16[512,128]{1,0:T(8,128)(2,1)S(1)}, bf16[512,128]{1,0:T(8,128)(2,1)S(1)}, u32[]{:S(2)}, u32[]{:S(2)}) collective-permute-start(bf16[512,128]{1,0:T(8,128)(2,1)S(1)} %get-tuple-element.37), channel_id=1, source_target_pairs={{0,9},{1,8},{2,10},{3,11},{4,13},{5,12},{6,14},{7,15},{8,1},{9,0},... | collective-permute-start | bytes 393224 | tf_op jit(solution)/shard_map/ppermute | solution.py:354
  9.5 0.0 collective-permute-start.4
  9.5 0.7 %collective-permute-start.5 = (bf16[512,128]{1,0:T(8,128)(2,1)S(1)}, bf16[512,128]{1,0:T(8,128)(2,1)S(1)}, u32[]{:S(2)}, u32[]{:S(2)}) collective-permute-start(bf16[512,128]{1,0:T(8,128)(2,1)S(1)} %get-tuple-element.39), channel_id=1, source_target_pairs={{0,0},{1,1},{2,3},{3,2},{4,4},{5,5},{6,7},{7,6},{8,8},{9,9},{10,11... | collective-permute-start | bytes 393224 | tf_op jit(solution)/shard_map/ppermute | solution.py:354
  10.2 0.0 copy-start
  10.2 1.5 %copy-done = bf16[28,128,256]{2,1,0:T(8,128)(2,1)S(1)} copy-done((bf16[28,128,256]{2,1,0:T(8,128)(2,1)S(1)}, bf16[28,128,256]{2,1,0:T(8,128)(2,1)}, u32[]{:S(2)}) %copy-start) | copy-done | bytes 1835032
  11.7 0.0 copy-start.1
  11.7 1.0 %shard_map.60 = (f32[64,256]{1,0:T(8,128)S(1)}, bf16[512,128]{1,0:T(8,128)(2,1)S(1)}) custom-call(bf16[640,128]{1,0:T(8,128)(2,1)S(1)} %get-tuple-element.40.own_ref, bf16[28,128,256]{2,1,0:T(8,128)(2,1)S(1)} %copy-done), custom_call_target="tpu_custom_call" | custom-call | bytes 1048576 | tf_op jit(solution)/shard_map/pallas_call | solution.py:365
  12.6 0.0 collective-permute-done.2.refs_0_
  12.6 2.4 %collective-permute-done.3.refs_1_ = bf16[512,128]{1,0:T(8,128)(2,1)S(1)} collective-permute-done((bf16[512,128]{1,0:T(8,128)(2,1)S(1)}, bf16[512,128]{1,0:T(8,128)(2,1)S(1)}, u32[]{:S(2)}, u32[]{:S(2)}) %collective-permute-start.3) | collective-permute-done | bytes 131104 | tf_op jit(solution)/shard_map/ppermute | solution.py:354
  15.1 0.7 %collective-permute-done.4.refs_2_ = bf16[512,128]{1,0:T(8,128)(2,1)S(1)} collective-permute-done((bf16[512,128]{1,0:T(8,128)(2,1)S(1)}, bf16[512,128]{1,0:T(8,128)(2,1)S(1)}, u32[]{:S(2)}, u32[]{:S(2)}) %collective-permute-start.4) | collective-permute-done | bytes 131104 | tf_op jit(solution)/shard_map/ppermute | solution.py:354
  15.7 0.0 collective-permute-done.5.refs_3_
  15.7 0.7 %shard_map.61 = (f32[15,32,128]{2,1,0:T(8,128)S(1)}, bf16[15,32,128]{2,1,0:T(8,128)(2,1)S(1)}) custom-call(bf16[512,128]{1,0:T(8,128)(2,1)S(1)} %collective-permute-done.2.refs_0_, bf16[512,128]{1,0:T(8,128)(2,1)S(1)} %collective-permute-done.3.refs_1_, bf16[512,128]{1,0:T(8,128)(2,1)S(1)} %collective-permute-done.4.refs_2_, ...), custom_call_target="tpu_custom_call" | custom-call | bytes 1048576 | tf_op jit(solution)/shard_map/pallas_call | solution.py:375
  16.4 0.9 %collective-permute-start.6 = (bf16[15,32,128]{2,1,0:T(8,128)(2,1)S(1)}, bf16[15,32,128]{2,1,0:T(8,128)(2,1)S(1)}, u32[]{:S(2)}, u32[]{:S(2)}) collective-permute-start(bf16[15,32,128]{2,1,0:T(8,128)(2,1)S(1)} %get-tuple-element.48), channel_id=1, source_target_pairs={{0,2},{2,0},{4,6},{6,4},{8,10},{10,8},{12,14},{14,12},{16,18},{18,... | collective-permute-start | bytes 368648 | tf_op jit(solution)/shard_map/ppermute | solution.py:343
  17.3 0.9 %collective-permute-start.9 = (bf16[640,128]{1,0:T(8,128)(2,1)S(1)}, bf16[640,128]{1,0:T(8,128)(2,1)S(1)}, u32[]{:S(2)}, u32[]{:S(2)}) collective-permute-start(bf16[640,128]{1,0:T(8,128)(2,1)S(1)} %get-tuple-element.58), channel_id=1, source_target_pairs={{0,1},{1,0},{2,3},{3,2},{4,5},{5,4},{6,7},{7,6},{8,9},{9,8},{10,11... | collective-permute-start | bytes 491528 | tf_op jit(solution)/shard_map/ppermute | solution.py:346
  18.2 0.1 collective-permute-done.6
  18.3 0.6 %shard_map.62 = (f32[13,32,128]{2,1,0:T(8,128)S(1)}, bf16[13,32,128]{2,1,0:T(8,128)(2,1)S(1)}) custom-call(bf16[512,128]{1,0:T(8,128)(2,1)S(1)} %collective-permute-done.2.refs_0_, bf16[512,128]{1,0:T(8,128)(2,1)S(1)} %collective-permute-done.3.refs_1_, bf16[512,128]{1,0:T(8,128)(2,1)S(1)} %collective-permute-done.4.refs_2_, ...), custom_call_target="tpu_custom_call" | custom-call | bytes 1048576 | tf_op jit(solution)/shard_map/pallas_call | solution.py:375
  18.9 0.4 collective-permute-start.7
  19.3 2.6 %collective-permute-start.11 = (bf16[15,32,128]{2,1,0:T(8,128)(2,1)S(1)}, bf16[15,32,128]{2,1,0:T(8,128)(2,1)S(1)}, u32[]{:S(2)}, u32[]{:S(2)}) collective-permute-start(bf16[15,32,128]{2,1,0:T(8,128)(2,1)S(1)} %add_convert_fusion.1), channel_id=1, source_target_pairs={{0,16},{2,18},{4,20},{6,22},{8,24},{10,26},{12,28},{14,30},{16,0},... | collective-permute-start | bytes 368648 | tf_op jit(solution)/shard_map/ppermute | solution.py:343
  21.9 1.6 %collective-permute-done.9.own_ref = bf16[640,128]{1,0:T(8,128)(2,1)S(1)} collective-permute-done((bf16[640,128]{1,0:T(8,128)(2,1)S(1)}, bf16[640,128]{1,0:T(8,128)(2,1)S(1)}, u32[]{:S(2)}, u32[]{:S(2)}) %collective-permute-start.9) | collective-permute-done | bytes 163872 | tf_op jit(solution)/shard_map/ppermute | solution.py:346
  23.5 0.0 copy-done.1
  23.5 1.0 %shard_map.63 = bf16[640,128]{1,0:T(8,128)(2,1)S(1)} custom-call(bf16[640,128]{1,0:T(8,128)(2,1)S(1)} %collective-permute-done.9.own_ref, bf16[28,128,256]{2,1,0:T(8,128)(2,1)S(1)} %copy-done.1), custom_call_target="tpu_custom_call" | custom-call | bytes 1048576 | tf_op jit(solution)/shard_map/pallas_call | solution.py:370
  24.5 1.1 %collective-permute-start.10 = (bf16[640,128]{1,0:T(8,128)(2,1)S(1)}, bf16[640,128]{1,0:T(8,128)(2,1)S(1)}, u32[]{:S(2)}, u32[]{:S(2)}) collective-permute-start(bf16[640,128]{1,0:T(8,128)(2,1)S(1)} %shard_map.63), channel_id=1, source_target_pairs={{0,1},{1,0},{2,3},{3,2},{4,5},{5,4},{6,7},{7,6},{8,9},{9,8},{10,11... | collective-permute-start | bytes 491528 | tf_op jit(solution)/shard_map/ppermute | solution.py:346
  25.6 0.0 collective-permute-done.7
  25.6 2.7 %collective-permute-start.8 = (bf16[13,32,128]{2,1,0:T(8,128)(2,1)S(1)}, bf16[13,32,128]{2,1,0:T(8,128)(2,1)S(1)}, u32[]{:S(2)}, u32[]{:S(2)}) collective-permute-start(bf16[13,32,128]{2,1,0:T(8,128)(2,1)S(1)} %add_convert_fusion.3), channel_id=1, source_target_pairs={{0,16},{2,18},{4,20},{6,22},{8,24},{10,26},{12,28},{14,30},{16,0},... | collective-permute-start | bytes 319496 | tf_op jit(solution)/shard_map/ppermute | solution.py:343
  28.3 0.0 collective-permute-done.11
  28.3 2.0 %collective-permute-start.14 = (bf16[15,32,128]{2,1,0:T(8,128)(2,1)S(1)}, bf16[15,32,128]{2,1,0:T(8,128)(2,1)S(1)}, u32[]{:S(2)}, u32[]{:S(2)}) collective-permute-start(bf16[15,32,128]{2,1,0:T(8,128)(2,1)S(1)} %add_convert_fusion.refs_0_), channel_id=1, source_target_pairs={{0,12},{2,14},{4,8},{6,10},{8,4},{10,6},{12,0},{14,2},{16,28},{18,... | collective-permute-start | bytes 368648 | tf_op jit(solution)/shard_map/ppermute | solution.py:343
  30.3 0.7 %collective-permute-start.13 = (bf16[15,32,128]{2,1,0:T(8,128)(2,1)S(1)}, bf16[15,32,128]{2,1,0:T(8,128)(2,1)S(1)}, u32[]{:S(2)}, u32[]{:S(2)}) collective-permute-start(bf16[15,32,128]{2,1,0:T(8,128)(2,1)S(1)} %add_convert_fusion.refs_0_), channel_id=1, source_target_pairs={{0,4},{2,6},{4,0},{6,2},{8,12},{10,14},{12,8},{14,10},{16,20},{18,... | collective-permute-start | bytes 368648 | tf_op jit(solution)/shard_map/ppermute | solution.py:343
  31.0 0.9 %collective-permute-start.12 = (bf16[15,32,128]{2,1,0:T(8,128)(2,1)S(1)}, bf16[15,32,128]{2,1,0:T(8,128)(2,1)S(1)}, u32[]{:S(2)}, u32[]{:S(2)}) collective-permute-start(bf16[15,32,128]{2,1,0:T(8,128)(2,1)S(1)} %add_convert_fusion.refs_0_), channel_id=1, source_target_pairs={{0,8},{2,10},{4,12},{6,14},{8,0},{10,2},{12,4},{14,6},{16,24},{18,... | collective-permute-start | bytes 368648 | tf_op jit(solution)/shard_map/ppermute | solution.py:343
  31.9 0.0 collective-permute-done.10.got_ref
  31.9 1.1 %shard_map.64 = (bf16[4,4,4,256]{3,2,1,0:T(4,128)(2,1)}, bf16[512,256]{1,0:T(8,128)(2,1)}) custom-call(f32[64,256]{1,0:T(8,128)S(1)} %get-tuple-element.55.part_ref, bf16[512,128]{1,0:T(8,128)(2,1)S(1)} %get-tuple-element.56.grad_ref, bf16[640,128]{1,0:T(8,128)(2,1)S(1)} %collective-permute-done.10.got_ref), custom_call_target="tpu_custom_call" | custom-call | bytes 1048576 | tf_op jit(solution)/shard_map/pallas_call | solution.py:383
  33.0 0.0 collective-permute-done.8
  33.0 2.0 %collective-permute-start.18 = (bf16[13,32,128]{2,1,0:T(8,128)(2,1)S(1)}, bf16[13,32,128]{2,1,0:T(8,128)(2,1)S(1)}, u32[]{:S(2)}, u32[]{:S(2)}) collective-permute-start(bf16[13,32,128]{2,1,0:T(8,128)(2,1)S(1)} %add_convert_fusion.2.refs_5_), channel_id=1, source_target_pairs={{0,12},{2,14},{4,8},{6,10},{8,4},{10,6},{12,0},{14,2},{16,28},{18,... | collective-permute-start | bytes 319496 | tf_op jit(solution)/shard_map/ppermute | solution.py:343
  35.0 0.7 %collective-permute-start.17 = (bf16[13,32,128]{2,1,0:T(8,128)(2,1)S(1)}, bf16[13,32,128]{2,1,0:T(8,128)(2,1)S(1)}, u32[]{:S(2)}, u32[]{:S(2)}) collective-permute-start(bf16[13,32,128]{2,1,0:T(8,128)(2,1)S(1)} %add_convert_fusion.2.refs_5_), channel_id=1, source_target_pairs={{0,4},{2,6},{4,0},{6,2},{8,12},{10,14},{12,8},{14,10},{16,20},{18,... | collective-permute-start | bytes 319496 | tf_op jit(solution)/shard_map/ppermute | solution.py:343
  35.7 0.3 collective-permute-done.14.refs_3_
  36.0 1.1 %collective-permute-start.16 = (bf16[13,32,128]{2,1,0:T(8,128)(2,1)S(1)}, bf16[13,32,128]{2,1,0:T(8,128)(2,1)S(1)}, u32[]{:S(2)}, u32[]{:S(2)}) collective-permute-start(bf16[13,32,128]{2,1,0:T(8,128)(2,1)S(1)} %add_convert_fusion.2.refs_5_), channel_id=1, source_target_pairs={{0,8},{2,10},{4,12},{6,14},{8,0},{10,2},{12,4},{14,6},{16,24},{18,... | collective-permute-start | bytes 319496 | tf_op jit(solution)/shard_map/ppermute | solution.py:343
  37.2 1.7 %collective-permute-done.13.refs_2_ = bf16[15,32,128]{2,1,0:T(8,128)(2,1)S(1)} collective-permute-done((bf16[15,32,128]{2,1,0:T(8,128)(2,1)S(1)}, bf16[15,32,128]{2,1,0:T(8,128)(2,1)S(1)}, u32[]{:S(2)}, u32[]{:S(2)}) %collective-permute-start.13) | collective-permute-done | bytes 122912 | tf_op jit(solution)/shard_map/ppermute | solution.py:343
  38.9 0.0 collective-permute-done.12.refs_1_
  38.9 0.1 pad_maximum_fusion
  39.0 0.1 collective-permute-start.15
  39.0 1.8 %collective-permute-done.18.refs_8_ = bf16[13,32,128]{2,1,0:T(8,128)(2,1)S(1)} collective-permute-done((bf16[13,32,128]{2,1,0:T(8,128)(2,1)S(1)}, bf16[13,32,128]{2,1,0:T(8,128)(2,1)S(1)}, u32[]{:S(2)}, u32[]{:S(2)}) %collective-permute-start.18) | collective-permute-done | bytes 106528 | tf_op jit(solution)/shard_map/ppermute | solution.py:343
  40.8 0.6 %collective-permute-done.17.refs_7_ = bf16[13,32,128]{2,1,0:T(8,128)(2,1)S(1)} collective-permute-done((bf16[13,32,128]{2,1,0:T(8,128)(2,1)S(1)}, bf16[13,32,128]{2,1,0:T(8,128)(2,1)S(1)}, u32[]{:S(2)}, u32[]{:S(2)}) %collective-permute-start.17) | collective-permute-done | bytes 106528 | tf_op jit(solution)/shard_map/ppermute | solution.py:343
  41.4 0.1 collective-permute-done.16.refs_6_
  41.6 0.1 pad_maximum_fusion.1
  41.6 0.1 collective-permute-start.19
  41.7 0.0 collective-permute-done.15.refs_4_
  41.7 1.7 %shard_map.65.refs_0_ = f32[28,128,256]{2,1,0:T(8,128)} custom-call(bf16[15,32,128]{2,1,0:T(8,128)(2,1)S(1)} %add_convert_fusion.refs_0_, bf16[15,32,128]{2,1,0:T(8,128)(2,1)S(1)} %collective-permute-done.12.refs_1_, bf16[15,32,128]{2,1,0:T(8,128)(2,1)S(1)} %collective-permute-done.13.refs_2_, bf16[15,32,128]{2,1,0:T(8,128)(2,1)S(1)} %collective-permute-done.14.refs_3_, ...), custom_call_target="tpu_custom_call" | custom-call | tf_op jit(solution)/shard_map/pallas_call | solution.py:403
  43.4 0.1 collective-permute-done.19.refs_1_
  43.5 1.0 %shard_map.66 = f32[28,128,256]{2,1,0:T(8,128)} custom-call(f32[28,128,256]{2,1,0:T(8,128)} %shard_map.65.refs_0_, bf16[52,32,128]{2,1,0:T(8,128)(2,1)S(1)} %collective-permute-done.19.refs_1_), custom_call_target="tpu_custom_call", output_to_operand_aliasing={{}: (0, {})} | custom-call | tf_op jit(solution)/shard_map/pallas_call | solution.py:403
  (4 shorter events, 0.1 us)
Async XLA Ops:
  0.6 1.9 %collective-permute-start = (bf16[512,256]{1,0:T(8,128)(2,1)}, bf16[512,256]{1,0:T(8,128)(2,1)S(1)}, u32[]{:S(2)}, u32[]{:S(2)}) collective-permute-start(bf16[512,256]{1,0:T(8,128)(2,1)} %bitcast.4), channel_id=1, source_target_pairs={{0,2},{2,0},{4,6},{6,4},{8,10},{10,8},{12,14},{14,12},{16,18},{18,... | collective-permute-start | bytes 786440 | tf_op jit(solution)/shard_map/ppermute | solution.py:343
  1.1 1.4 %collective-permute-start.1 = (bf16[4,4,4,256]{3,2,1,0:T(4,128)(2,1)}, bf16[4,4,4,256]{3,2,1,0:T(4,128)(2,1)S(1)}, u32[]{:S(2)}, u32[]{:S(2)}) collective-permute-start(bf16[4,4,4,256]{3,2,1,0:T(4,128)(2,1)} %bitcast.6), channel_id=1, source_target_pairs={{0,2},{2,0},{4,6},{6,4},{8,10},{10,8},{12,14},{14,12},{16,18},{18,... | collective-permute-start | bytes 98312 | tf_op jit(solution)/shard_map/ppermute | solution.py:343
  1.2 0.9 %copy-start.2 = (bf16[1,8,8,8,256]{4,3,2,1,0:T(8,128)(2,1)S(1)}, bf16[1,8,8,8,256]{4,3,2,1,0:T(8,128)(2,1)}, u32[]{:S(2)}) copy-start(bf16[1,8,8,8,256]{4,3,2,1,0:T(8,128)(2,1)} %param.3) | copy-start | bytes 786436
  2.6 0.8 %copy-start.3 = (bf16[1,4,4,4,256]{4,3,2,1,0:T(4,128)(2,1)S(1)}, bf16[1,4,4,4,256]{4,3,2,1,0:T(4,128)(2,1)}, u32[]{:S(2)}) copy-start(bf16[1,4,4,4,256]{4,3,2,1,0:T(4,128)(2,1)} %param.4) | copy-start | bytes 98308
  4.1 8.6 %collective-permute-start.2 = (bf16[512,128]{1,0:T(8,128)(2,1)S(1)}, bf16[512,128]{1,0:T(8,128)(2,1)S(1)}, u32[]{:S(2)}, u32[]{:S(2)}) collective-permute-start(bf16[512,128]{1,0:T(8,128)(2,1)S(1)} %get-tuple-element.36), channel_id=1, source_target_pairs={{0,5},{1,4},{2,6},{3,7},{4,1},{5,0},{6,2},{7,3},{8,13},{9,12},{10,... | collective-permute-start | bytes 393224 | tf_op jit(solution)/shard_map/ppermute | solution.py:354
  8.0 7.1 %collective-permute-start.3 = (bf16[512,128]{1,0:T(8,128)(2,1)S(1)}, bf16[512,128]{1,0:T(8,128)(2,1)S(1)}, u32[]{:S(2)}, u32[]{:S(2)}) collective-permute-start(bf16[512,128]{1,0:T(8,128)(2,1)S(1)} %get-tuple-element.37), channel_id=1, source_target_pairs={{0,9},{1,8},{2,10},{3,11},{4,13},{5,12},{6,14},{7,15},{8,1},{9,0},... | collective-permute-start | bytes 393224 | tf_op jit(solution)/shard_map/ppermute | solution.py:354
  9.5 6.3 %collective-permute-start.4 = (bf16[512,128]{1,0:T(8,128)(2,1)S(1)}, bf16[512,128]{1,0:T(8,128)(2,1)S(1)}, u32[]{:S(2)}, u32[]{:S(2)}) collective-permute-start(bf16[512,128]{1,0:T(8,128)(2,1)S(1)} %get-tuple-element.38), channel_id=1, source_target_pairs={{0,12},{1,13},{2,15},{3,14},{4,8},{5,9},{6,11},{7,10},{8,4},{9,5},... | collective-permute-start | bytes 393224 | tf_op jit(solution)/shard_map/ppermute | solution.py:354
  9.5 6.2 %collective-permute-start.5 = (bf16[512,128]{1,0:T(8,128)(2,1)S(1)}, bf16[512,128]{1,0:T(8,128)(2,1)S(1)}, u32[]{:S(2)}, u32[]{:S(2)}) collective-permute-start(bf16[512,128]{1,0:T(8,128)(2,1)S(1)} %get-tuple-element.39), channel_id=1, source_target_pairs={{0,0},{1,1},{2,3},{3,2},{4,4},{5,5},{6,7},{7,6},{8,8},{9,9},{10,11... | collective-permute-start | bytes 393224 | tf_op jit(solution)/shard_map/ppermute | solution.py:354
  10.2 1.5 %copy-start = (bf16[28,128,256]{2,1,0:T(8,128)(2,1)S(1)}, bf16[28,128,256]{2,1,0:T(8,128)(2,1)}, u32[]{:S(2)}) copy-start(bf16[28,128,256]{2,1,0:T(8,128)(2,1)} %w_ref.3) | copy-start | bytes 5505028
  11.7 11.8 %copy-start.1 = (bf16[28,128,256]{2,1,0:T(8,128)(2,1)S(1)}, bf16[28,128,256]{2,1,0:T(8,128)(2,1)}, u32[]{:S(2)}) copy-start(bf16[28,128,256]{2,1,0:T(8,128)(2,1)} %w_ref.3) | copy-start | bytes 5505028
  16.4 1.9 %collective-permute-start.6 = (bf16[15,32,128]{2,1,0:T(8,128)(2,1)S(1)}, bf16[15,32,128]{2,1,0:T(8,128)(2,1)S(1)}, u32[]{:S(2)}, u32[]{:S(2)}) collective-permute-start(bf16[15,32,128]{2,1,0:T(8,128)(2,1)S(1)} %get-tuple-element.48), channel_id=1, source_target_pairs={{0,2},{2,0},{4,6},{6,4},{8,10},{10,8},{12,14},{14,12},{16,18},{18,... | collective-permute-start | bytes 368648 | tf_op jit(solution)/shard_map/ppermute | solution.py:343
  17.3 6.2 %collective-permute-start.9 = (bf16[640,128]{1,0:T(8,128)(2,1)S(1)}, bf16[640,128]{1,0:T(8,128)(2,1)S(1)}, u32[]{:S(2)}, u32[]{:S(2)}) collective-permute-start(bf16[640,128]{1,0:T(8,128)(2,1)S(1)} %get-tuple-element.58), channel_id=1, source_target_pairs={{0,1},{1,0},{2,3},{3,2},{4,5},{5,4},{6,7},{7,6},{8,9},{9,8},{10,11... | collective-permute-start | bytes 491528 | tf_op jit(solution)/shard_map/ppermute | solution.py:346
  18.9 6.7 %collective-permute-start.7 = (bf16[13,32,128]{2,1,0:T(8,128)(2,1)S(1)}, bf16[13,32,128]{2,1,0:T(8,128)(2,1)S(1)}, u32[]{:S(2)}, u32[]{:S(2)}) collective-permute-start(bf16[13,32,128]{2,1,0:T(8,128)(2,1)S(1)} %get-tuple-element.54), channel_id=1, source_target_pairs={{0,2},{2,0},{4,6},{6,4},{8,10},{10,8},{12,14},{14,12},{16,18},{18,... | collective-permute-start | bytes 319496 | tf_op jit(solution)/shard_map/ppermute | solution.py:343
  19.3 8.9 %collective-permute-start.11 = (bf16[15,32,128]{2,1,0:T(8,128)(2,1)S(1)}, bf16[15,32,128]{2,1,0:T(8,128)(2,1)S(1)}, u32[]{:S(2)}, u32[]{:S(2)}) collective-permute-start(bf16[15,32,128]{2,1,0:T(8,128)(2,1)S(1)} %add_convert_fusion.1), channel_id=1, source_target_pairs={{0,16},{2,18},{4,20},{6,22},{8,24},{10,26},{12,28},{14,30},{16,0},... | collective-permute-start | bytes 368648 | tf_op jit(solution)/shard_map/ppermute | solution.py:343
  24.5 7.4 %collective-permute-start.10 = (bf16[640,128]{1,0:T(8,128)(2,1)S(1)}, bf16[640,128]{1,0:T(8,128)(2,1)S(1)}, u32[]{:S(2)}, u32[]{:S(2)}) collective-permute-start(bf16[640,128]{1,0:T(8,128)(2,1)S(1)} %shard_map.63), channel_id=1, source_target_pairs={{0,1},{1,0},{2,3},{3,2},{4,5},{5,4},{6,7},{7,6},{8,9},{9,8},{10,11... | collective-permute-start | bytes 491528 | tf_op jit(solution)/shard_map/ppermute | solution.py:346
  25.6 7.4 %collective-permute-start.8 = (bf16[13,32,128]{2,1,0:T(8,128)(2,1)S(1)}, bf16[13,32,128]{2,1,0:T(8,128)(2,1)S(1)}, u32[]{:S(2)}, u32[]{:S(2)}) collective-permute-start(bf16[13,32,128]{2,1,0:T(8,128)(2,1)S(1)} %add_convert_fusion.3), channel_id=1, source_target_pairs={{0,16},{2,18},{4,20},{6,22},{8,24},{10,26},{12,28},{14,30},{16,0},... | collective-permute-start | bytes 319496 | tf_op jit(solution)/shard_map/ppermute | solution.py:343
  28.3 7.7 %collective-permute-start.14 = (bf16[15,32,128]{2,1,0:T(8,128)(2,1)S(1)}, bf16[15,32,128]{2,1,0:T(8,128)(2,1)S(1)}, u32[]{:S(2)}, u32[]{:S(2)}) collective-permute-start(bf16[15,32,128]{2,1,0:T(8,128)(2,1)S(1)} %add_convert_fusion.refs_0_), channel_id=1, source_target_pairs={{0,12},{2,14},{4,8},{6,10},{8,4},{10,6},{12,0},{14,2},{16,28},{18,... | collective-permute-start | bytes 368648 | tf_op jit(solution)/shard_map/ppermute | solution.py:343
  30.3 8.6 %collective-permute-start.13 = (bf16[15,32,128]{2,1,0:T(8,128)(2,1)S(1)}, bf16[15,32,128]{2,1,0:T(8,128)(2,1)S(1)}, u32[]{:S(2)}, u32[]{:S(2)}) collective-permute-start(bf16[15,32,128]{2,1,0:T(8,128)(2,1)S(1)} %add_convert_fusion.refs_0_), channel_id=1, source_target_pairs={{0,4},{2,6},{4,0},{6,2},{8,12},{10,14},{12,8},{14,10},{16,20},{18,... | collective-permute-start | bytes 368648 | tf_op jit(solution)/shard_map/ppermute | solution.py:343
  31.0 7.9 %collective-permute-start.12 = (bf16[15,32,128]{2,1,0:T(8,128)(2,1)S(1)}, bf16[15,32,128]{2,1,0:T(8,128)(2,1)S(1)}, u32[]{:S(2)}, u32[]{:S(2)}) collective-permute-start(bf16[15,32,128]{2,1,0:T(8,128)(2,1)S(1)} %add_convert_fusion.refs_0_), channel_id=1, source_target_pairs={{0,8},{2,10},{4,12},{6,14},{8,0},{10,2},{12,4},{14,6},{16,24},{18,... | collective-permute-start | bytes 368648 | tf_op jit(solution)/shard_map/ppermute | solution.py:343
  33.0 7.8 %collective-permute-start.18 = (bf16[13,32,128]{2,1,0:T(8,128)(2,1)S(1)}, bf16[13,32,128]{2,1,0:T(8,128)(2,1)S(1)}, u32[]{:S(2)}, u32[]{:S(2)}) collective-permute-start(bf16[13,32,128]{2,1,0:T(8,128)(2,1)S(1)} %add_convert_fusion.2.refs_5_), channel_id=1, source_target_pairs={{0,12},{2,14},{4,8},{6,10},{8,4},{10,6},{12,0},{14,2},{16,28},{18,... | collective-permute-start | bytes 319496 | tf_op jit(solution)/shard_map/ppermute | solution.py:343
  35.0 6.4 %collective-permute-start.17 = (bf16[13,32,128]{2,1,0:T(8,128)(2,1)S(1)}, bf16[13,32,128]{2,1,0:T(8,128)(2,1)S(1)}, u32[]{:S(2)}, u32[]{:S(2)}) collective-permute-start(bf16[13,32,128]{2,1,0:T(8,128)(2,1)S(1)} %add_convert_fusion.2.refs_5_), channel_id=1, source_target_pairs={{0,4},{2,6},{4,0},{6,2},{8,12},{10,14},{12,8},{14,10},{16,20},{18,... | collective-permute-start | bytes 319496 | tf_op jit(solution)/shard_map/ppermute | solution.py:343
  36.0 5.5 %collective-permute-start.16 = (bf16[13,32,128]{2,1,0:T(8,128)(2,1)S(1)}, bf16[13,32,128]{2,1,0:T(8,128)(2,1)S(1)}, u32[]{:S(2)}, u32[]{:S(2)}) collective-permute-start(bf16[13,32,128]{2,1,0:T(8,128)(2,1)S(1)} %add_convert_fusion.2.refs_5_), channel_id=1, source_target_pairs={{0,8},{2,10},{4,12},{6,14},{8,0},{10,2},{12,4},{14,6},{16,24},{18,... | collective-permute-start | bytes 319496 | tf_op jit(solution)/shard_map/ppermute | solution.py:343
  39.0 2.7 %collective-permute-start.15 = (bf16[60,32,128]{2,1,0:T(8,128)(2,1)S(1)}, bf16[60,32,128]{2,1,0:T(8,128)(2,1)S(1)}, u32[]{:S(2)}, u32[]{:S(2)}) collective-permute-start(bf16[60,32,128]{2,1,0:T(8,128)(2,1)S(1)} %pad_maximum_fusion), channel_id=1, source_target_pairs={{0,2},{2,0},{4,6},{6,4},{8,10},{10,8},{12,14},{14,12},{16,18},{18,... | collective-permute-start | bytes 1474568 | tf_op jit(solution)/shard_map/ppermute | solution.py:343
  41.6 1.8 %collective-permute-start.19 = (bf16[52,32,128]{2,1,0:T(8,128)(2,1)S(1)}, bf16[52,32,128]{2,1,0:T(8,128)(2,1)S(1)}, u32[]{:S(2)}, u32[]{:S(2)}) collective-permute-start(bf16[52,32,128]{2,1,0:T(8,128)(2,1)S(1)} %pad_maximum_fusion.1), channel_id=1, source_target_pairs={{0,2},{2,0},{4,6},{6,4},{8,10},{10,8},{12,14},{14,12},{16,18},{18,... | collective-permute-start | bytes 1277960 | tf_op jit(solution)/shard_map/ppermute | solution.py:343
